TPU v7x, 32 devices: a whole 2x2x4 slice. The times are simulated.
32 devices in a mesh: dp: 16 (over z, y, x), tensor: 2 (over core).
Axes of the slice: x: 2, y: 2, z: 4, core: 2. Of those that a mesh axis runs over, the one named last changes fastest.
Arguments:
- tokens: bfloat16 [2, 2048, 1024], P(None, 'dp'), may hold values from -6 to 6
- cu_seqlens: int32 [2, 32], replicated, may hold values from 0 to 2048, as said below
- attn_gain: bfloat16 [2, 1024], P(None, 'dp'), may hold values from 0.5 to 1.5
- mlp_gain: bfloat16 [2, 1024], P(None, 'dp'), may hold values from 0.5 to 1.5
- w_qkv: bfloat16 [2, 3, 1024, 1024], P(None, None, 'dp', 'tensor'), may hold values from -0.1875 to 0.1875
- w_attn_out: bfloat16 [2, 1024, 1024], P(None, 'dp', 'tensor'), may hold values from -2 to 2
- w_ffn_in: bfloat16 [2, 2, 1024, 2624], P(None, None, 'dp', 'tensor'), may hold values from -0.1875 to 0.1875
- w_ffn_out: bfloat16 [2, 1024, 2624], P(None, 'dp', 'tensor'), may hold values from -0.125 to 0.125
- out_grad: bfloat16 [2, 2048, 1024], P(None, 'dp'), may hold values from -6 to 6
Outputs:
- hidden_out: bfloat16 [2, 2048, 1024], P(None, 'dp')
- input_grad: float32 [2, 2048, 1024], P(None, 'dp')
- attn_gain_grad: float32 [2, 1024], P(None, 'dp')
- mlp_gain_grad: float32 [2, 1024], P(None, 'dp')
- w_qkv_grad: float32 [2, 3, 1024, 1024], P(None, None, 'dp', 'tensor')
- w_attn_out_grad: float32 [2, 1024, 1024], P(None, 'dp', 'tensor')
- w_ffn_in_grad: float32 [2, 2, 1024, 2624], P(None, None, 'dp', 'tensor')
- w_ffn_out_grad: float32 [2, 1024, 2624], P(None, 'dp', 'tensor')
Inputs may be any that keep to these rules, and one draw needn't show every extreme that they name: `cu_seqlens`: in each micro-batch the 32 boundaries rise strictly from 0 to 2048; no document has more than 128 tokens and some document has exactly 128; no interior boundary is a multiple of 128, and every aligned block of 128 tokens holds one or two interior boundaries.
All inputs are finite; a program needn't handle non-finite values.
Results may differ from a plain program's by a relative error of at most 0.025.
Values may be sent and summed in bfloat16 or wider, within the bound.
No kernel may reach another device: no remote copies, remote signals or barrier semaphores. Data moves between devices by JAX's collectives and lax.ppermute only.
A program may use at most 256 MiB of HBM per device.

v0:
```python
import jax
import jax.numpy as jnp
from jax import lax
from jax.sharding import PartitionSpec as P

HD = 64
HALF = 64


MASKED_SCORE = -1e30


def passed_along(x, axis, by):
    devices = lax.axis_size(axis)
    pairs = [(i, i + by) for i in range(devices) if 0 <= i + by < devices]
    return lax.ppermute(x, axis, pairs)


def extended(block, sides, width):
    for axis, dim in sides:
        count = lax.axis_size(axis)
        forward = [(i, i + 1) for i in range(count - 1)]
        backward = [(target, source) for source, target in forward]
        low = lax.ppermute(
            lax.slice_in_dim(block, block.shape[dim] - width, None, axis=dim), axis, forward
        )
        high = lax.ppermute(lax.slice_in_dim(block, 0, width, axis=dim), axis, backward)
        block = jnp.concatenate([low, block, high], axis=dim)
    return block


def layer_norm(values, scale_row):
    row_mean = jnp.mean(values, axis=-1, keepdims=True)
    centered = values - row_mean
    variance = jnp.mean(centered * centered, axis=-1, keepdims=True)
    return centered * lax.rsqrt(variance + 1e-05) * scale_row


def rotate(values, offsets, rope_base):
    half_dim = values.shape[-1] // 2
    inv_freq = rope_base ** (-(jnp.arange(half_dim, dtype=jnp.float32) * 2.0 / values.shape[-1]))
    angles = offsets.astype(jnp.float32)[:, None] * inv_freq[None, :]
    cosine = jnp.cos(angles)[:, None, :]
    sine_part = jnp.sin(angles)[:, None, :]
    first = values[..., :half_dim]
    second = values[..., half_dim:]
    return jnp.concatenate(
        [first * cosine - second * sine_part, second * cosine + first * sine_part], axis=-1
    )


def doc_info(bounds, token_index):
    inside = (token_index >= 0) & (token_index < bounds[-1])
    doc_ids = jnp.sum((token_index[:, None] >= bounds[None, 1:-1]).astype(jnp.int32), axis=1)
    doc_start = jnp.max(
        jnp.where(token_index[:, None] >= bounds[None, :-1], bounds[None, :-1], 0), axis=1
    )
    return (jnp.where(inside, doc_ids, -1), token_index - doc_start)


def stacked(key_rows, k_docs, k_index):
    block_rows = key_rows.shape[0]
    blocks = key_rows.shape[0] // block_rows
    return (
        key_rows.reshape(blocks, block_rows, key_rows.shape[1]),
        k_docs.reshape(blocks, block_rows),
        k_index.reshape(blocks, block_rows),
    )


def split_kv(piece_kv, head_count):
    width = piece_kv.shape[1] // 2
    return (
        piece_kv[:, :width].reshape(-1, head_count, HD),
        piece_kv[:, width:].reshape(-1, head_count, HD),
    )


def make_allowed(q_docs, q_index, k_docs, k_index, windowed):
    allowed = q_docs[:, None] == k_docs[None, :]
    if windowed:
        allowed = allowed & (jnp.abs(q_index[:, None] - k_index[None, :]) <= HALF)
    return allowed


def scores(q_rows, key_part, allowed):
    raw_scores = jnp.einsum("qhd,khd->hqk", q_rows, key_part, preferred_element_type=jnp.float32)
    return jnp.where(allowed[None], 0.125 * raw_scores, MASKED_SCORE)


def attn_probs(score_rows, log_total, allowed):
    return jnp.where(allowed[None], jnp.exp(score_rows - log_total[:, :, None]), 0.0)


def softmax_stats(q_rows, q_docs, q_index, key_rows, k_docs, k_index, windowed):
    head_count = q_rows.shape[1]

    def softmax_advance(running, block_data):
        row_max, row_sum = running
        piece_kv, piece_docs, piece_index = block_data
        key_part, value_part = split_kv(piece_kv, head_count)
        allowed = make_allowed(q_docs, q_index, piece_docs, piece_index, windowed)
        score_rows = scores(q_rows, key_part, allowed)
        new_max = jnp.maximum(row_max, jnp.max(score_rows, axis=2))
        weighted = jnp.where(allowed[None], jnp.exp(score_rows - new_max[:, :, None]), 0.0)
        return ((new_max, row_sum * jnp.exp(row_max - new_max) + jnp.sum(weighted, axis=2)), None)

    start_state = (
        jnp.full((head_count, q_rows.shape[0]), MASKED_SCORE, jnp.float32),
        jnp.zeros((head_count, q_rows.shape[0]), jnp.float32),
    )
    (row_max, row_sum), _ = lax.scan(
        softmax_advance, start_state, stacked(key_rows, k_docs, k_index)
    )
    return row_max + jnp.log(row_sum)


def context_rows(q_rows, q_docs, q_index, key_rows, k_docs, k_index, log_total, windowed):
    head_count = q_rows.shape[1]

    def context_advance(running, block_data):
        piece_kv, piece_docs, piece_index = block_data
        key_part, value_part = split_kv(piece_kv, head_count)
        allowed = make_allowed(q_docs, q_index, piece_docs, piece_index, windowed)
        probs_b = attn_probs(scores(q_rows, key_part, allowed), log_total, allowed).astype(
            jnp.bfloat16
        )
        return (
            running
            + jnp.einsum("hqk,khd->qhd", probs_b, value_part, preferred_element_type=jnp.float32),
            None,
        )

    result, _ = lax.scan(
        context_advance, jnp.zeros(q_rows.shape, jnp.float32), stacked(key_rows, k_docs, k_index)
    )
    return result


def query_side(q_rows, dout_rows, q_docs, q_index, key_rows, k_docs, k_index, log_total, windowed):
    head_count = q_rows.shape[1]
    blocks_data = stacked(key_rows, k_docs, k_index)

    def dot_step(running, block_data):
        piece_kv, piece_docs, piece_index = block_data
        key_part, value_part = split_kv(piece_kv, head_count)
        allowed = make_allowed(q_docs, q_index, piece_docs, piece_index, windowed)
        probs_f = attn_probs(scores(q_rows, key_part, allowed), log_total, allowed)
        prob_grads = jnp.einsum(
            "qhd,khd->hqk", dout_rows, value_part, preferred_element_type=jnp.float32
        )
        return (running + jnp.sum(probs_f * prob_grads, axis=2), None)

    row_dots, _ = lax.scan(dot_step, jnp.zeros(log_total.shape, jnp.float32), blocks_data)

    def grad_step(running, block_data):
        piece_kv, piece_docs, piece_index = block_data
        key_part, value_part = split_kv(piece_kv, head_count)
        allowed = make_allowed(q_docs, q_index, piece_docs, piece_index, windowed)
        probs_f = attn_probs(scores(q_rows, key_part, allowed), log_total, allowed)
        prob_grads = jnp.einsum(
            "qhd,khd->hqk", dout_rows, value_part, preferred_element_type=jnp.float32
        )
        score_grads = (probs_f * (prob_grads - row_dots[:, :, None])).astype(jnp.bfloat16)
        return (
            running
            + 0.125
            * jnp.einsum("hqk,khd->qhd", score_grads, key_part, preferred_element_type=jnp.float32),
            None,
        )

    d_query, _ = lax.scan(grad_step, jnp.zeros(q_rows.shape, jnp.float32), blocks_data)
    return (row_dots, d_query)


def key_side(
    q_rows,
    dout_rows,
    log_total,
    row_dots,
    q_docs,
    q_index,
    key_part,
    value_part,
    k_docs,
    k_index,
    windowed,
):
    allowed = make_allowed(q_docs, q_index, k_docs, k_index, windowed)
    probs_f = attn_probs(scores(q_rows, key_part, allowed), log_total, allowed)
    prob_grads = jnp.einsum(
        "qhd,khd->hqk", dout_rows, value_part, preferred_element_type=jnp.float32
    )
    score_grads = (probs_f * (prob_grads - row_dots[:, :, None])).astype(jnp.bfloat16)
    d_key = 0.125 * jnp.einsum(
        "hqk,qhd->khd", score_grads, q_rows, preferred_element_type=jnp.float32
    )
    d_value = jnp.einsum(
        "hqk,qhd->khd", probs_f.astype(jnp.bfloat16), dout_rows, preferred_element_type=jnp.float32
    )
    key_count = key_part.shape[0]
    return jnp.concatenate([d_key.reshape(key_count, -1), d_value.reshape(key_count, -1)], axis=1)


def all_key_terms(
    q_rows, dout_rows, log_total, row_dots, q_docs, q_index, key_rows, k_docs, k_index, windowed
):
    head_count = q_rows.shape[1]

    def one_block(block_data):
        block_kv, block_docs, block_index = block_data
        key_part, value_part = split_kv(block_kv, head_count)
        return key_side(
            q_rows,
            dout_rows,
            log_total,
            row_dots,
            q_docs,
            q_index,
            key_part,
            value_part,
            block_docs,
            block_index,
            windowed,
        )

    return lax.map(one_block, stacked(key_rows, k_docs, k_index)).reshape(
        key_rows.shape[0], key_rows.shape[1]
    )


def heads_total(partial_rows):
    return lax.psum(partial_rows.astype(jnp.bfloat16), "tensor").astype(jnp.float32)


def send_rim(rim_rows, offset_by):
    return passed_along(rim_rows.astype(jnp.bfloat16), "dp", offset_by).astype(rim_rows.dtype)


def send_doc_rim(rim_rows, offset_by):
    return passed_along(rim_rows.astype(jnp.bfloat16), "dp", offset_by).astype(rim_rows.dtype)


def layer_forward(x_in, bounds, token_base, weights, windowed):
    gain_attn, gain_mlp, proj_qkv, proj_out, ffn_in, ffn_out = weights
    row_count = x_in.shape[0]
    head_count = proj_qkv.shape[2] // HD
    token_index = token_base + jnp.arange(row_count, dtype=jnp.int32)
    doc_ids, offsets = doc_info(bounds, token_index)
    rope_base = 10000.0 if windowed else 160000.0
    normed_b = layer_norm(x_in, gain_attn.astype(jnp.float32)).astype(jnp.bfloat16)
    qkv = jnp.einsum("td,sdc->stc", normed_b, proj_qkv, preferred_element_type=jnp.float32)
    q_rows = rotate(qkv[0].reshape(row_count, head_count, HD), offsets, rope_base).astype(
        jnp.bfloat16
    )
    key_own = rotate(qkv[1].reshape(row_count, head_count, HD), offsets, rope_base).astype(
        jnp.bfloat16
    )
    value_own = qkv[2].reshape(row_count, head_count, HD).astype(jnp.bfloat16)
    own_kv = jnp.concatenate(
        [key_own.reshape(row_count, -1), value_own.reshape(row_count, -1)], axis=1
    )
    if windowed:
        key_rows = extended(own_kv, (("dp", 0),), HALF)
    else:
        key_rows = extended(own_kv, (("dp", 0),), row_count)
    reach = (key_rows.shape[0] - row_count) // 2
    k_index = token_base - reach + jnp.arange(row_count + 2 * reach, dtype=jnp.int32)
    k_docs, _ = doc_info(bounds, k_index)
    log_total = softmax_stats(q_rows, doc_ids, token_index, key_rows, k_docs, k_index, windowed)
    context_b = (
        context_rows(q_rows, doc_ids, token_index, key_rows, k_docs, k_index, log_total, windowed)
        .reshape(row_count, -1)
        .astype(jnp.bfloat16)
    )
    x_mid = x_in + heads_total(
        jnp.einsum("tc,dc->td", context_b, proj_out, preferred_element_type=jnp.float32)
    )
    hidden_in_b = layer_norm(x_mid, gain_mlp.astype(jnp.float32)).astype(jnp.bfloat16)
    gate_up = jnp.einsum("td,sdf->stf", hidden_in_b, ffn_in, preferred_element_type=jnp.float32)
    hidden_b = (jax.nn.gelu(gate_up[0], approximate=False) * gate_up[1]).astype(jnp.bfloat16)
    x_out = x_mid + heads_total(
        jnp.einsum("tf,df->td", hidden_b, ffn_out, preferred_element_type=jnp.float32)
    )
    kept = (
        x_in,
        normed_b,
        qkv,
        q_rows,
        key_rows,
        k_docs,
        k_index,
        doc_ids,
        token_index,
        offsets,
        log_total,
        context_b,
        x_mid,
        hidden_in_b,
        gate_up,
        hidden_b,
    )
    return (x_out, kept)


def layer_backward(grad_rows, weights, kept, windowed):
    gain_attn, gain_mlp, proj_qkv, proj_out, ffn_in, ffn_out = weights
    (
        x_in,
        normed_b,
        qkv,
        q_rows,
        key_rows,
        k_docs,
        k_index,
        doc_ids,
        token_index,
        offsets,
        log_total,
        context_b,
        x_mid,
        hidden_in_b,
        gate_up,
        hidden_b,
    ) = kept
    row_count = x_in.shape[0]
    head_count = proj_qkv.shape[2] // HD
    rope_base = 10000.0 if windowed else 160000.0
    grad_b = grad_rows.astype(jnp.bfloat16)
    d_ffn_out = jnp.einsum("td,tf->df", grad_b, hidden_b, preferred_element_type=jnp.float32)
    d_hidden = jnp.einsum("td,df->tf", grad_b, ffn_out, preferred_element_type=jnp.float32)
    _, glu_back = jax.vjp(
        lambda gate_part, up_part: jax.nn.gelu(gate_part, approximate=False) * up_part,
        gate_up[0],
        gate_up[1],
    )
    d_gate, d_up = glu_back(d_hidden)
    d_gate_up = jnp.stack([d_gate, d_up]).astype(jnp.bfloat16)
    d_ffn_in = jnp.einsum("td,stf->sdf", hidden_in_b, d_gate_up, preferred_element_type=jnp.float32)
    d_hidden_in = heads_total(
        jnp.einsum("stf,sdf->td", d_gate_up, ffn_in, preferred_element_type=jnp.float32)
    )
    _, norm_back_mlp = jax.vjp(layer_norm, x_mid, gain_mlp.astype(jnp.float32))
    d_mid, d_gain_mlp = norm_back_mlp(d_hidden_in)
    d_mid = d_mid + grad_rows
    mid_b = d_mid.astype(jnp.bfloat16)
    d_proj_out = jnp.einsum("td,tc->dc", mid_b, context_b, preferred_element_type=jnp.float32)
    dout_b = jnp.einsum("td,dc->tc", mid_b, proj_out, preferred_element_type=jnp.float32).astype(
        jnp.bfloat16
    )
    dout_rows = dout_b.reshape(row_count, head_count, HD)
    row_dots, d_query = query_side(
        q_rows, dout_rows, doc_ids, token_index, key_rows, k_docs, k_index, log_total, windowed
    )
    width = key_rows.shape[1]
    reach = (key_rows.shape[0] - row_count) // 2
    rim_terms = all_key_terms(
        q_rows,
        dout_rows,
        log_total,
        row_dots,
        doc_ids,
        token_index,
        key_rows,
        k_docs,
        k_index,
        windowed,
    )
    if windowed:
        from_right = send_rim(rim_terms[:reach], -1)
        from_left = send_rim(rim_terms[row_count + reach :], 1)
    else:
        from_right = send_doc_rim(rim_terms[:reach], -1)
        from_left = send_doc_rim(rim_terms[row_count + reach :], 1)
    d_kv = rim_terms[reach : reach + row_count]
    d_kv = d_kv.at[:reach].add(from_left).at[row_count - reach :].add(from_right)
    d_key = d_kv[:, : width // 2].reshape(row_count, head_count, HD)
    d_value = d_kv[:, width // 2 :]
    _, rope_back = jax.vjp(
        lambda values: rotate(values, offsets, rope_base), qkv[0].reshape(row_count, head_count, HD)
    )
    d_query_pre = rope_back(d_query)[0]
    d_key_pre = rope_back(d_key)[0]
    d_qkv = jnp.stack(
        [d_query_pre.reshape(row_count, -1), d_key_pre.reshape(row_count, -1), d_value]
    ).astype(jnp.bfloat16)
    d_proj_qkv = jnp.einsum("td,stc->sdc", normed_b, d_qkv, preferred_element_type=jnp.float32)
    d_normed = heads_total(
        jnp.einsum("stc,sdc->td", d_qkv, proj_qkv, preferred_element_type=jnp.float32)
    )
    _, norm_back_attn = jax.vjp(layer_norm, x_in, gain_attn.astype(jnp.float32))
    d_input, d_gain_attn = norm_back_attn(d_normed)
    return (d_input + d_mid, (d_gain_attn, d_gain_mlp, d_proj_qkv, d_proj_out, d_ffn_in, d_ffn_out))


def shards(
    tokens, cu_seqlens, attn_gain, mlp_gain, w_qkv, w_attn_out, w_ffn_in, w_ffn_out, out_grad
):
    row_count = tokens.shape[1]
    micro_total = tokens.shape[0]
    token_base = lax.axis_index("dp") * row_count
    layer_total = w_qkv.shape[0]

    def fetch_layer(layer_idx):
        return (
            lax.all_gather(attn_gain[layer_idx], "dp", axis=0, tiled=True),
            lax.all_gather(mlp_gain[layer_idx], "dp", axis=0, tiled=True),
            lax.all_gather(w_qkv[layer_idx], "dp", axis=1, tiled=True),
            lax.all_gather(w_attn_out[layer_idx], "dp", axis=0, tiled=True),
            lax.all_gather(w_ffn_in[layer_idx], "dp", axis=1, tiled=True),
            lax.all_gather(w_ffn_out[layer_idx], "dp", axis=0, tiled=True),
        )

    def weights_for(layer_idx):
        return fetch_layer(layer_idx)

    outputs = []
    input_grads = []
    grad_sums = [None] * layer_total
    owned_layers = [None] * layer_total
    for micro_idx in range(micro_total):
        bounds = cu_seqlens[micro_idx]
        x_rows = tokens[micro_idx].astype(jnp.float32)
        kept_list = []
        for layer_idx in range(layer_total):
            x_rows, kept = layer_forward(
                x_rows, bounds, token_base, weights_for(layer_idx), layer_idx % 2 == 0
            )
            kept_list.append(kept)
        outputs.append(x_rows.astype(jnp.bfloat16))
        grad_rows = out_grad[micro_idx].astype(jnp.float32)
        for layer_idx in reversed(range(layer_total)):
            grad_rows, layer_grads = layer_backward(
                grad_rows, weights_for(layer_idx), kept_list[layer_idx], layer_idx % 2 == 0
            )
            if grad_sums[layer_idx] is None:
                grad_sums[layer_idx] = layer_grads
            else:
                grad_sums[layer_idx] = tuple(
                    (old + new for old, new in zip(grad_sums[layer_idx], layer_grads))
                )
            owned_layers[layer_idx] = None
        input_grads.append(grad_rows)
    joined = tuple(
        (
            jnp.stack([grad_sums[layer_idx][member] for layer_idx in range(layer_total)])
            for member in range(6)
        )
    )
    owned = (
        lax.psum_scatter(joined[0], "dp", scatter_dimension=1, tiled=True),
        lax.psum_scatter(joined[1], "dp", scatter_dimension=1, tiled=True),
        lax.psum_scatter(joined[2], "dp", scatter_dimension=2, tiled=True),
        lax.psum_scatter(joined[3], "dp", scatter_dimension=1, tiled=True),
        lax.psum_scatter(joined[4], "dp", scatter_dimension=2, tiled=True),
        lax.psum_scatter(joined[5], "dp", scatter_dimension=1, tiled=True),
    )
    return (
        jnp.stack(outputs),
        jnp.stack(input_grads),
        owned[0],
        owned[1],
        owned[2],
        owned[3],
        owned[4],
        owned[5],
    )


def solution(mesh):
    in_specs = (
        P(None, "dp", None),
        P(),
        P(None, "dp"),
        P(None, "dp"),
        P(None, None, "dp", "tensor"),
        P(None, "dp", "tensor"),
        P(None, None, "dp", "tensor"),
        P(None, "dp", "tensor"),
        P(None, "dp", None),
    )
    out_specs = (
        P(None, "dp", None),
        P(None, "dp", None),
        P(None, "dp"),
        P(None, "dp"),
        P(None, None, "dp", "tensor"),
        P(None, "dp", "tensor"),
        P(None, None, "dp", "tensor"),
        P(None, "dp", "tensor"),
    )
    return jax.shard_map(shards, mesh=mesh, in_specs=in_specs, out_specs=out_specs, check_vma=False)
```

profile of v0, /device:TPU:0, one launch (start us, length us, event | category | flops | bytes accessed | tf_op | source)
XLA Modules:
  0.0 2484.3 jit_solution(10317542562365840065)
XLA Ops:
  19.9 44.4 %all-reduce.24 = (bf16[1024]{0:T(1024)(128)(2,1)S(1)}, bf16[1024]{0:T(1024)(128)(2,1)S(1)}, bf16[1024]{0:T(1024)(128)(2,1)S(1)}, bf16[1024]{0:T(1024)(128)(2,1)S(1)}) all-reduce(bf16[1024]{0:T(1024)(128)(2,1)S(1)} %dynamic-update-slice.20, bf16[1024]{0:T(1024)(128)(2,1)S(1)} %dynamic-update-slice.21, ...), channel_id=2, replica_groups=mesh['dp'=16,'tensor'=2] {'dp'}, use_global_device_ids=true, to_apply=%add.16 | all-reduce | flops 4096 | bytes 16384
  67.3 14.8 all-gather.21.cloned.1.call-done
  98.2 41.6 %all-gather.23.cloned.1.call-done = bf16[1,1024,512]{2,1,0:T(8,128)(2,1)} async-done(((bf16[1,64,512]{2,1,0:T(8,128)(2,1)}), bf16[1,1024,512]{2,1,0:T(8,128)(2,1)}) %all-gather.23.cloned.1.call-update) | async-done | bytes 1048592 | tf_op jit(solution)/shard_map/all_gather | solution.py:409
  142.3 17.5 all-reduce.42.cloned.1.call-done
  182.7 16.1 all-reduce.44.cloned.1.call-done
  201.3 91.4 %all-gather.25.cloned.1.call-done = bf16[1,2,1024,1312]{3,1,0,2:T(2,128)(2,1)} async-done(((bf16[1,2,64,1312]{3,1,0,2:T(2,128)(2,1)}), bf16[1,2,1024,1312]{3,1,0,2:T(2,128)(2,1)}) %all-gather.25.cloned.1.call-update) | async-done | bytes 5373968 | tf_op jit(solution)/shard_map/all_gather | solution.py:410
  292.7 14.8 copy.201
  318.2 41.4 %all-gather.27.cloned.1.call-done = bf16[1,1024,1312]{2,1,0:T(8,128)(2,1)} async-done(((bf16[1,64,1312]{2,1,0:T(8,128)(2,1)}), bf16[1,1024,1312]{2,1,0:T(8,128)(2,1)}) %all-gather.27.cloned.1.call-update) | async-done | bytes 2686992 | tf_op jit(solution)/shard_map/all_gather | solution.py:411
  370.0 13.1 all-reduce.60.cloned.1.call-done
  384.7 70.9 %all-gather.29.cloned.1.call-done = bf16[1,3,1024,512]{3,2,1,0:T(8,128)(2,1)} async-done(((bf16[1,3,64,512]{3,2,1,0:T(8,128)(2,1)}), bf16[1,3,1024,512]{3,2,1,0:T(8,128)(2,1)}) %all-gather.29.cloned.1.call-update) | async-done | bytes 3145744 | tf_op jit(solution)/shard_map/all_gather | solution.py:408
  470.1 16.0 collective-permute-start.6
  490.2 26.7 %all-gather.31.cloned.1.call-done = bf16[1,1024,512]{2,1,0:T(8,128)(2,1)} async-done(((bf16[1,64,512]{2,1,0:T(8,128)(2,1)}), bf16[1,1024,512]{2,1,0:T(8,128)(2,1)}) %all-gather.31.cloned.1.call-update) | async-done | bytes 1048592 | tf_op jit(solution)/shard_map/all_gather | solution.py:409
  521.3 63.9 %all-gather.35.cloned.1.call-done = bf16[1,1024,1312]{2,1,0:T(8,128)(2,1)} async-done(((bf16[1,64,1312]{2,1,0:T(8,128)(2,1)}), bf16[1,1024,1312]{2,1,0:T(8,128)(2,1)}) %all-gather.35.cloned.1.call-update) | async-done | bytes 2686992 | tf_op jit(solution)/shard_map/all_gather | solution.py:411
  592.4 84.5 %all-gather.33.cloned.1.call-done = bf16[1,2,1024,1312]{3,1,0,2:T(2,128)(2,1)} async-done(((bf16[1,2,64,1312]{3,1,0,2:T(2,128)(2,1)}), bf16[1,2,1024,1312]{3,1,0,2:T(2,128)(2,1)}) %all-gather.33.cloned.1.call-update) | async-done | bytes 5373968 | tf_op jit(solution)/shard_map/all_gather | solution.py:410
  676.9 14.9 copy.208
  717.8 16.6 all-reduce.56.cloned.1.call-done
  791.0 7.8 collective-permute-done.9
  828.8 5.7 fusion.317
  834.5 10.1 all-reduce.54.cloned.1.call-done
  861.2 9.7 add_bitcast_fusion
  872.1 8.8 all-reduce.52.cloned.1.call-done
  954.2 12.1 all-reduce.50.cloned.1.call-done
  971.2 17.0 pad_maximum_fusion
  988.2 33.8 %copy.248 = f32[2,2,1024,1312]{3,1,0,2:T(2,128)} copy(f32[2,2,1024,1312]{2,3,1,0:T(8,128)} %pad_maximum_fusion) | data formatting | bytes 42991616 | tf_op jit(solution)/shard_map/stack | solution.py:446
  1038.0 6.3 pad_maximum_fusion.2
  1044.3 17.7 copy.249
  1066.9 11.9 pad_maximum_fusion.1
  1078.9 19.4 copy.247
  1110.5 11.4 reduce-scatter.10.cloned.1.call-done
  1123.3 614.0 %all-reduce.46.cloned.1.call-done = f32[2,2,1024,1312]{3,1,0,2:T(2,128)} async-done(((f32[2,2,1024,1312]{3,1,0,2:T(2,128)}), f32[2,2,1024,1312]{3,1,0,2:T(2,128)}) %all-reduce.46.cloned.1.call-update) | async-done | bytes 21495824
  1740.1 639.8 %all-reduce.48.cloned.1.call-done = (f32[2,3,1024,512]{3,0,1,2:T(2,128)}, f32[2,1024,1312]{2,0,1:T(2,128)}) async-done(((f32[2,3,1024,512]{3,0,1,2:T(2,128)}, f32[2,1024,1312]{2,0,1:T(2,128)}), (f32[2,3,1024,512]{3,0,1,2:T(2,128)}, f32[2,1024,1312]{2,0,1:T(2,128)})) %all-reduce.48.cloned.1.call-update) | async-done | bytes 23330832
  2384.4 92.7 %reduce-scatter.8.cloned.1.call-done = f32[2,64,512]{2,1,0:T(8,128)} async-done(((f32[2,1024,512]{2,1,0:T(8,128)}), f32[2,64,512]{2,1,0:T(8,128)}) %reduce-scatter.8.cloned.1.call-update) | async-done | bytes 262160 | tf_op jit(solution)/shard_map/reduce_scatter | solution.py:454
  (935 shorter events, 356.8 us)
Async XLA Ops:
  7.2 74.9 %all-gather.21.cloned.1.call-start = ((), (), s32[]{:S(2)}) async-start(), calls=%async_computation.6 | async-start | bytes 3342336 | tf_op jit(solution)/shard_map/all_gather | solution.py:408
  9.1 130.7 %all-gather.23.cloned.1.call-start = ((), (), s32[]{:S(2)}) async-start(), calls=%async_computation.7 | async-start | bytes 1114112 | tf_op jit(solution)/shard_map/all_gather | solution.py:409
  10.7 149.1 %all-reduce.42.cloned.1.call-start = ((), (), s32[]{:S(2)}) async-start(), calls=%async_computation.3 | async-start | bytes 524288 | tf_op jit(solution)/shard_map/psum | solution.py:233
  142.2 56.6 %all-reduce.44.cloned.1.call-start = ((), (), s32[]{:S(2)}) async-start(), calls=%async_computation.4 | async-start | bytes 524288 | tf_op jit(solution)/shard_map/psum | solution.py:233
  179.3 113.4 %all-gather.25.cloned.1.call-start = ((), (), s32[]{:S(2)}) async-start(), calls=%async_computation.8 | async-start | bytes 6127616 | tf_op jit(solution)/shard_map/all_gather | solution.py:410
  180.5 179.1 %all-gather.27.cloned.1.call-start = ((), (), s32[]{:S(2)}) async-start(), calls=%async_computation.9 | async-start | bytes 3063808 | tf_op jit(solution)/shard_map/all_gather | solution.py:411
  182.4 200.8 %all-reduce.60.cloned.1.call-start = ((), (), s32[]{:S(2)}) async-start(), calls=%async_computation.23 | async-start | bytes 1048576 | tf_op jit(solution)/shard_map/psum | solution.py:233
  365.2 90.5 %all-gather.29.cloned.1.call-start = ((), (), s32[]{:S(2)}) async-start(), calls=%async_computation.10 | async-start | bytes 3342336 | tf_op jit(solution)/shard_map/all_gather | solution.py:408
  365.9 151.0 %all-gather.31.cloned.1.call-start = ((), (), s32[]{:S(2)}) async-start(), calls=%async_computation.11 | async-start | bytes 1114112 | tf_op jit(solution)/shard_map/all_gather | solution.py:409
  366.7 218.6 %all-gather.35.cloned.1.call-start = ((), (), s32[]{:S(2)}) async-start(), calls=%async_computation.13 | async-start | bytes 3063808 | tf_op jit(solution)/shard_map/all_gather | solution.py:411
  367.2 309.6 %all-gather.33.cloned.1.call-start = ((), (), s32[]{:S(2)}) async-start(), calls=%async_computation.12 | async-start | bytes 6127616 | tf_op jit(solution)/shard_map/all_gather | solution.py:410
  368.4 328.6 %all-reduce.58.cloned.1.call-start = ((), (), s32[]{:S(2)}) async-start(), calls=%async_computation.22 | async-start | bytes 1048576 | tf_op jit(solution)/shard_map/psum | solution.py:233
  459.5 26.7 %collective-permute-start.3 = (bf16[128,1024]{1,0:T(8,128)(2,1)S(1)}, bf16[128,1024]{1,0:T(8,128)(2,1)S(1)}, u32[]{:S(2)}, u32[]{:S(2)}) collective-permute-start(bf16[128,1024]{1,0:T(8,128)(2,1)S(1)} %pad_maximum_fusion.30), channel_id=1, source_target_pairs={{2,0},{4,2},{6,4},{8,6},{10,8},{12,10},{14,12},{16,14},{18,16},{20... | collective-permute-start | bytes 786440 | tf_op jit(solution)/shard_map/ppermute | solution.py:27
  460.8 25.4 %collective-permute-start.2 = (bf16[128,1024]{1,0:T(8,128)(2,1)S(1)}, bf16[128,1024]{1,0:T(8,128)(2,1)S(1)}, u32[]{:S(2)}, u32[]{:S(2)}) collective-permute-start(bf16[128,1024]{1,0:T(8,128)(2,1)S(1)} %pad_maximum_fusion.30), channel_id=1, source_target_pairs={{0,2},{2,4},{4,6},{6,8},{8,10},{10,12},{12,14},{14,16},{16,18},{18... | collective-permute-start | bytes 786440 | tf_op jit(solution)/shard_map/ppermute | solution.py:24
  468.8 17.9 collective-permute-start.7
  470.1 16.6 collective-permute-start.6
  521.3 213.1 %all-reduce.56.cloned.1.call-start = ((), (), s32[]{:S(2)}) async-start(), calls=%async_computation.21 | async-start | bytes 1048576 | tf_op jit(solution)/shard_map/psum | solution.py:233
  714.2 130.5 %all-reduce.54.cloned.1.call-start = ((), (), s32[]{:S(2)}) async-start(), calls=%async_computation.20 | async-start | bytes 1048576 | tf_op jit(solution)/shard_map/psum | solution.py:233
  768.7 19.5 collective-permute-start.12
  773.2 15.0 collective-permute-start.13
  781.0 10.0 collective-permute-start.8
  785.6 13.2 collective-permute-start.9
  824.9 56.1 %all-reduce.52.cloned.1.call-start = ((), (), s32[]{:S(2)}) async-start(), calls=%async_computation.19 | async-start | bytes 1048576 | tf_op jit(solution)/shard_map/psum | solution.py:233
  860.9 105.4 %all-reduce.50.cloned.1.call-start = ((), (), s32[]{:S(2)}) async-start(), calls=%async_computation.18 | async-start | bytes 2097152 | tf_op jit(solution)/shard_map/psum | solution.py:233
  913.1 14.9 collective-permute-start.15
  914.4 12.6 collective-permute-start.14
  921.0 11.4 collective-permute-start.11
  944.4 161.2 %reduce-scatter.12.cloned.1.call-start = ((), (), s32[]{:S(2)}) async-start(), calls=%async_computation.15 | async-start | bytes 557056
  954.2 167.8 %reduce-scatter.10.cloned.1.call-start = ((), (), s32[]{:S(2)}) async-start(), calls=%async_computation.14 | async-start | bytes 557056
  971.1 766.2 %all-reduce.46.cloned.1.call-start = ((), (), s32[]{:S(2)}) async-start(), calls=%async_computation.16 | async-start | bytes 46137344
  1022.0 1357.9 %all-reduce.48.cloned.1.call-start = ((), (), s32[]{:S(2)}) async-start(), calls=%async_computation.17 | async-start | bytes 48234496
  1098.4 1378.7 %reduce-scatter.8.cloned.1.call-start = ((), (), s32[]{:S(2)}) async-start(), calls=%async_computation.5 | async-start | bytes 4456448 | tf_op jit(solution)/shard_map/reduce_scatter | solution.py:454
  (273 other events, 5044.7 us)
Sparse Core Ops, SparseCore 0:
  11.4 70.6 all-gather.20
  85.4 54.3 all-gather.22
  142.7 17.0 all-reduce.41
  179.4 19.4 all-reduce.43
  202.0 90.6 all-gather.24
  295.3 64.2 all-gather.26
  365.3 17.8 all-reduce.59
  386.9 68.7 all-gather.28
  458.8 58.1 all-gather.30
  520.5 64.6 all-gather.34
  588.3 88.5 all-gather.32
  679.8 17.2 all-reduce.57
  714.3 19.9 all-reduce.55
  825.0 19.6 all-reduce.53
  860.9 19.9 all-reduce.51
  944.5 21.8 all-reduce.49
  969.0 77.7 reduce-scatter.11
  1049.0 72.9 reduce-scatter.9
  1128.4 608.9 all-reduce.45
  1743.6 636.1 all-reduce.47
  2382.8 94.1 reduce-scatter.7
where the time goes:
time: 2500 us; the launch traced here: 2480 us
  waiting for transfers between devices  1920 us (77%)
  local copies, waits for them, and re-layouts  180 us (7%)
  matrix products  149 us (6%)
  other arithmetic  112 us (4%)
  starting transfers between devices  59 us (2%)
  blocking collectives  44.4 us (2%)
    unnamed x25, waiting for transfers between devices  1270 us
    all_gather x2, waiting for transfers between devices, fetch_layer(): lax.all_gather(w_ffn_in[layer_idx], 'dp', axis=1, tiled=True)  176 us
    all_gather x2, waiting for transfers between devices, fetch_layer(): lax.all_gather(w_ffn_out[layer_idx], 'dp', axis=0, tiled=True)  105 us
    psum x8, waiting for transfers between devices, heads_total(): lax.psum(partial_rows.astype(jnp.bfloat16), 'tensor').astype(jnp.float32)  99.7 us
    reduce_scatter x1, waiting for transfers between devices, shards(): lax.psum_scatter(joined[3], 'dp', scatter_dimension=1, tiled=True)  92.7 us
    all_gather x2, waiting for transfers between devices, fetch_layer(): lax.all_gather(w_qkv[layer_idx], 'dp', axis=1, tiled=True)  85.8 us
    another operation x3, local copies, waits for them, and re-layouts, shards(): jnp.stack([grad_sums[layer_idx][member] for layer_idx in range(layer_tota...  71 us
    all_gather x2, waiting for transfers between devices, fetch_layer(): lax.all_gather(w_attn_out[layer_idx], 'dp', axis=0, tiled=True)  68.4 us
  transfers between devices with their start and end apart: 37, of which 27 were waited for; matrix products, arithmetic and copies ran while one was open for 11% of the time, Pallas kernels for 0%

commit v1 on v0

v1 whole, which is shorter than its diff:
```python
import functools

import jax
import jax.numpy as jnp
from jax import lax
from jax.experimental import pallas as pl
from jax.experimental.pallas import tpu as pltpu
from jax.sharding import Mesh
from jax.sharding import PartitionSpec as P

HD = 64
HALF = 64
BLK = 128
TEAM = 4
MASKED = -1e30
BF = jnp.bfloat16
F32 = jnp.float32


def mm(a, b, ca, cb):
    return lax.dot_general(a, b, (((ca,), (cb,)), ((), ())), preferred_element_type=F32)


def hop_team(x, k):
    return lax.ppermute(x, ("y", "x"), [(i, i ^ k) for i in range(TEAM)])


def hop_core(x):
    return lax.ppermute(x, "c", [(0, 1), (1, 0)])


def hop_z(x, s):
    n = lax.axis_size("z")
    return lax.ppermute(x, "z", [(i, (i + s) % n) for i in range(n)])


def step_z(x, by):
    n = lax.axis_size("z")
    return lax.ppermute(x, "z", [(i, i + by) for i in range(n) if 0 <= i + by < n])


def gather_rows(own):
    parts = jnp.stack([own] + [hop_team(own, k) for k in range(1, TEAM)], axis=1)
    other = hop_core(parts)
    both = jnp.stack([parts, other], axis=2)
    n, rows, width = own.shape
    return both.reshape(n, TEAM * 2 * rows, width)


def sum_rows(partial):
    n, rows, width = partial.shape
    b = partial.reshape(n, TEAM, 2, rows // (2 * TEAM), width)
    h = b[:, :, 0].astype(F32) + hop_core(b[:, :, 1]).astype(F32)
    hb = h.astype(BF)
    total = h[:, 0]
    for k in range(1, TEAM):
        total = total + hop_team(hb[:, k], k).astype(F32)
    return total


def norm_parts(v):
    mean = jnp.mean(v, axis=-1, keepdims=True)
    cent = v - mean
    rstd = lax.rsqrt(jnp.mean(cent * cent, axis=-1, keepdims=True) + 1e-05)
    return cent * rstd, rstd


def norm_back(dout, v, gain):
    xhat, rstd = norm_parts(v)
    dgain = jnp.sum(dout * xhat, axis=(0, 1))
    dx = dout * gain
    m1 = jnp.mean(dx, axis=-1, keepdims=True)
    m2 = jnp.mean(dx * xhat, axis=-1, keepdims=True)
    return rstd * (dx - m1 - xhat * m2), dgain


def swap_halves(v):
    width = v.shape[-1]
    lane = lax.broadcasted_iota(jnp.int32, v.shape, v.ndim - 1) % HD
    up = jnp.roll(v, -(HD // 2), axis=-1)
    down = jnp.roll(v, HD // 2, axis=-1)
    del width
    return jnp.where(lane < HD // 2, up, down)


def band_from(m, qkv_ref, lo_ref, hi_ref, kb, vb, width, rows):
    kb[:BLK] = lo_ref[0, :, :width]
    vb[:BLK] = lo_ref[0, :, width:]
    kb[BLK + rows :] = hi_ref[0, :, :width]
    vb[BLK + rows :] = hi_ref[0, :, width:]
    sub = rows // 8
    for j in range(8):
        src = pl.ds(pl.multiple_of((m ^ j) * sub, sub), sub)
        kb[BLK + j * sub : BLK + (j + 1) * sub] = qkv_ref[0, src, width : 2 * width]
        vb[BLK + j * sub : BLK + (j + 1) * sub] = qkv_ref[0, src, 2 * width :]


def allowed_of(i, dcol_ref, drow_ref, windowed):
    qd = dcol_ref[0, BLK + i * BLK : 2 * BLK + i * BLK, :]
    kd = drow_ref[0, :, i * BLK : (i + 3) * BLK]
    ok = qd == kd
    if windowed:
        shape = (BLK, 3 * BLK)
        gap = lax.broadcasted_iota(jnp.int32, shape, 1) - lax.broadcasted_iota(jnp.int32, shape, 0) - BLK
        ok = ok & (gap <= HALF) & (gap >= -HALF)
    return ok


def take(ref, m, i, lanes, sub):
    per = BLK // sub
    return jnp.concatenate(
        [
            ref[0, pl.ds(pl.multiple_of((m ^ (per * i + e)) * sub, sub), sub), lanes]
            for e in range(per)
        ],
        axis=0,
    )


def put(ref, m, i, lanes, sub, value):
    per = BLK // sub
    for e in range(per):
        ref[0, pl.ds(pl.multiple_of((m ^ (per * i + e)) * sub, sub), sub), lanes] = value[
            e * sub : (e + 1) * sub
        ]


def attn_fwd_kernel(m_ref, qkv_ref, lo_ref, hi_ref, dcol_ref, drow_ref, ctx_ref, kb, vb, *, windowed):
    m = m_ref[0]
    rows = qkv_ref.shape[1]
    width = qkv_ref.shape[2] // 3
    sub = rows // 8
    band_from(m, qkv_ref, lo_ref, hi_ref, kb, vb, width, rows)
    head_of = lax.broadcasted_iota(jnp.int32, (BLK, width), 1) // HD
    for i in range(rows // BLK):
        ok = allowed_of(i, dcol_ref, drow_ref, windowed)
        q = take(qkv_ref, m, i, slice(0, width), sub)
        k = kb[i * BLK : (i + 3) * BLK]
        v = vb[i * BLK : (i + 3) * BLK]
        out = jnp.zeros((BLK, width), F32)
        for h in range(width // HD):
            qh = jnp.where(head_of == h, q, jnp.zeros_like(q))
            s = jnp.where(ok, 0.125 * mm(qh, k, 1, 1), MASKED)
            e = jnp.exp(s - jnp.max(s, axis=1, keepdims=True))
            p = (e / jnp.sum(e, axis=1, keepdims=True)).astype(BF)
            out = jnp.where(head_of == h, mm(p, v, 1, 0), out)
        put(ctx_ref, m, i, slice(0, width), sub, out.astype(BF))


def attn_bwd_kernel(
    m_ref, qkv_ref, lo_ref, hi_ref, dcol_ref, drow_ref, dctx_ref, dq_ref, dk_ref, dv_ref, kb, vb, *, windowed
):
    m = m_ref[0]
    rows = qkv_ref.shape[1]
    width = qkv_ref.shape[2] // 3
    sub = rows // 8
    band_from(m, qkv_ref, lo_ref, hi_ref, kb, vb, width, rows)
    head_of = lax.broadcasted_iota(jnp.int32, (BLK, width), 1) // HD
    dk_ref[...] = jnp.zeros(dk_ref.shape, F32)
    dv_ref[...] = jnp.zeros(dv_ref.shape, F32)
    for i in range(rows // BLK):
        ok = allowed_of(i, dcol_ref, drow_ref, windowed)
        q = take(qkv_ref, m, i, slice(0, width), sub)
        do = take(dctx_ref, m, i, slice(0, width), sub)
        band = slice(i * BLK, (i + 3) * BLK)
        k = kb[band]
        v = vb[band]
        dq = jnp.zeros((BLK, width), F32)
        dk = jnp.zeros((3 * BLK, width), F32)
        dv = jnp.zeros((3 * BLK, width), F32)
        for h in range(width // HD):
            mine = head_of == h
            qh = jnp.where(mine, q, jnp.zeros_like(q))
            doh = jnp.where(mine, do, jnp.zeros_like(do))
            s = jnp.where(ok, 0.125 * mm(qh, k, 1, 1), MASKED)
            e = jnp.exp(s - jnp.max(s, axis=1, keepdims=True))
            p = e / jnp.sum(e, axis=1, keepdims=True)
            dp = mm(doh, v, 1, 1)
            ds = (p * (dp - jnp.sum(p * dp, axis=1, keepdims=True))).astype(BF)
            dq = jnp.where(mine, mm(ds, k, 1, 0), dq)
            dk = dk + mm(ds, qh, 0, 0)
            dv = dv + mm(p.astype(BF), doh, 0, 0)
        put(dq_ref, m, i, slice(0, width), sub, 0.125 * dq)
        dk_ref[0, band] = dk_ref[0, band] + 0.125 * dk
        dv_ref[0, band] = dv_ref[0, band] + dv


def whole_block(shape):
    return pl.BlockSpec((1,) + shape[1:], lambda n, m: (n,) + (0,) * (len(shape) - 1))


def call_attention(kernel, m, ins, outs, windowed):
    n, rows, width = ins[0].shape[0], ins[0].shape[1], ins[0].shape[2] // 3
    pairs = n * rows * 3 * BLK * (width // HD)
    return pl.pallas_call(
        functools.partial(kernel, windowed=windowed),
        grid_spec=pltpu.PrefetchScalarGridSpec(
            num_scalar_prefetch=1,
            grid=(n,),
            in_specs=[whole_block(a.shape) for a in ins],
            out_specs=[whole_block(o.shape) for o in outs],
            scratch_shapes=[pltpu.VMEM((rows + 2 * BLK, width), BF)] * 2,
        ),
        out_shape=outs,
        compiler_params=pltpu.CompilerParams(vmem_limit_bytes=48 * 1024 * 1024),
        cost_estimate=pl.CostEstimate(
            flops=pairs * HD * 8, bytes_accessed=n * rows * width * 12, transcendentals=pairs
        ),
    )(m, *ins)


def pad_units(w, units):
    return jnp.pad(w, [(0, 0)] * (w.ndim - 1) + [(0, units - w.shape[-1])])


def spread(pack_of, t, z):
    own = pack_of(t)
    rows, width = own.shape
    nz = lax.axis_size("z")
    plane = jnp.zeros((TEAM * rows, width), own.dtype)
    for k in range(TEAM):
        part = own if k == 0 else hop_team(pack_of(t ^ k), k)
        plane = lax.dynamic_update_slice(plane, part, ((t ^ k) * rows, 0))
    full = jnp.zeros((nz * TEAM * rows, width), own.dtype)
    for s in range(nz):
        part = plane if s == 0 else hop_z(plane, s)
        full = lax.dynamic_update_slice(full, part, (((z - s) % nz) * TEAM * rows, 0))
    return full


def collect(grad, t, z, rows):
    nz = lax.axis_size("z")
    width = grad.shape[1]
    span = TEAM * rows
    low = grad.astype(BF)
    total = lax.dynamic_slice(low, (z * span, 0), (span, width)).astype(F32)
    for s in range(1, nz):
        piece = lax.dynamic_slice(low, (((z + s) % nz) * span, 0), (span, width))
        total = total + hop_z(piece, s).astype(F32)
    out = [lax.dynamic_slice(total, (t * rows, 0), (rows, width))]
    low = total.astype(BF)
    for k in range(1, TEAM):
        piece = lax.dynamic_slice(low, ((t ^ k) * rows, 0), (rows, width))
        out.append(hop_team(piece, k).astype(F32))
    return out


def columns(parts, t, lo, width):
    rows = parts[0].shape[0]
    full = jnp.zeros((rows, TEAM * width), F32)
    for k in range(TEAM):
        full = lax.dynamic_update_slice(full, parts[k][:, lo : lo + width], (0, (t ^ k) * width))
    return full


def gelu_parts(gate):
    cdf = 0.5 * (1.0 + lax.erf(gate * 0.7071067811865476))
    return gate * cdf, cdf + gate * jnp.exp(-0.5 * gate * gate) * 0.3989422804014327


def shards(tokens, cu_seqlens, attn_gain, mlp_gain, w_qkv, w_attn_out, w_ffn_in, w_ffn_out, out_grad):
    z = lax.axis_index("z")
    t = lax.axis_index("y") * 2 + lax.axis_index("x")
    c = lax.axis_index("c")
    m = 2 * t + c
    micro, chip_rows, feat = tokens.shape
    layers = w_qkv.shape[0]
    d_rows = w_qkv.shape[2]
    head_cols = w_qkv.shape[3] // TEAM
    own_rows = chip_rows // 2
    team_rows = TEAM * chip_rows
    unit_real = w_ffn_in.shape[3]
    units = -(-unit_real // (TEAM * 128)) * 128

    ffn_in_pad = pad_units(w_ffn_in, TEAM * units)
    ffn_out_pad = pad_units(w_ffn_out, TEAM * units)
    gains_cols = jnp.pad(
        jnp.concatenate([attn_gain, mlp_gain], axis=0).T, ((0, 0), (0, 128 - 2 * layers))
    )

    def attn_pack(layer):
        def of(member):
            q3 = lax.dynamic_slice_in_dim(w_qkv[layer], member * head_cols, head_cols, axis=2)
            o = lax.dynamic_slice_in_dim(w_attn_out[layer], member * head_cols, head_cols, axis=1)
            items = [q3[0], q3[1], q3[2], o]
            if layer == 0:
                items.append(gains_cols)
            return jnp.concatenate(items, axis=1)

        return of

    def ffn_pack(layer):
        def of(member):
            gu = lax.dynamic_slice_in_dim(ffn_in_pad[layer], member * units, units, axis=2)
            dn = lax.dynamic_slice_in_dim(ffn_out_pad[layer], member * units, units, axis=1)
            return jnp.concatenate([gu[0], gu[1], dn], axis=1)

        return of

    def own_half(x):
        return lax.dynamic_slice_in_dim(x, c * own_rows, own_rows, axis=1)

    tok_own = own_half(tokens)
    grad_own = own_half(out_grad)
    tok_all = gather_rows(tok_own)

    packs = []
    for layer in range(layers):
        packs.append([spread(attn_pack(layer), t, z), None])
        packs[layer][1] = spread(ffn_pack(layer), t, z)
    gains = packs[0][0][:, 4 * head_cols : 4 * head_cols + 2 * layers].T.astype(F32)
    grad_all = gather_rows(grad_own)

    band_index = z * team_rows - BLK + jnp.arange(team_rows + 2 * BLK, dtype=jnp.int32)
    inside = (band_index >= 0) & (band_index < cu_seqlens[0, -1])
    band_docs = jnp.sum(
        (band_index[None, :, None] >= cu_seqlens[:, None, 1:-1]).astype(jnp.int32), axis=2
    )
    band_docs = jnp.where(inside[None], band_docs, -1)
    docs_col = band_docs[:, :, None]
    docs_row = band_docs[:, None, :]
    blocks = jnp.arange(2 * TEAM, dtype=jnp.int32) ^ m
    local_index = (
        z * team_rows + blocks[:, None] * own_rows + jnp.arange(own_rows, dtype=jnp.int32)[None]
    ).reshape(-1)
    start = jnp.max(
        jnp.where(
            local_index[None, :, None] >= cu_seqlens[:, None, :-1], cu_seqlens[:, None, :-1], 0
        ),
        axis=2,
    )
    offsets = (local_index[None] - start).astype(F32)
    tables = []
    for layer in range(layers):
        base = 10000.0 if layer % 2 == 0 else 160000.0
        inv = base ** (-(jnp.arange(HD // 2, dtype=F32) * 2.0 / HD))
        ang = offsets[:, :, None] * inv
        cos, sin = jnp.cos(ang), jnp.sin(ang)
        heads = head_cols // HD
        tables.append(
            (
                jnp.concatenate([cos, cos] * heads, axis=-1),
                jnp.concatenate([-sin, sin] * heads, axis=-1),
            )
        )
    m_arr = jnp.reshape(m, (1,)).astype(jnp.int32)

    def flat(x):
        return x.reshape(-1, x.shape[-1])

    def edge(kv, first):
        b = kv.reshape(micro, 2 * TEAM, own_rows, kv.shape[-1])
        picks = [0, 1] if first else [2 * TEAM - 2, 2 * TEAM - 1]
        return jnp.concatenate(
            [lax.dynamic_index_in_dim(b, m ^ j, axis=1, keepdims=False) for j in picks], axis=1
        )

    x_own = tok_own.astype(F32)
    saved = []
    for layer in range(layers):
        windowed = layer % 2 == 0
        wa, wf = packs[layer]
        w3 = wa[:, : 3 * head_cols]
        wo = wa[:, 3 * head_cols : 4 * head_cols]
        g_attn, g_mlp = gains[layer], gains[layers + layer]
        if layer == 0:
            a = (norm_parts(tok_all.astype(F32))[0] * g_attn).astype(BF)
        else:
            a = gather_rows((norm_parts(x_own)[0] * g_attn).astype(BF))
        qkv = mm(flat(a), w3, 1, 0).reshape(micro, team_rows, -1)
        cos, sin = tables[layer]
        q, k, v = (qkv[:, :, i * head_cols : (i + 1) * head_cols] for i in range(3))
        kv_b = jnp.concatenate([k * cos + swap_halves(k) * sin, v], axis=-1).astype(BF)
        lo = step_z(edge(kv_b, False), 1)
        hi = step_z(edge(kv_b, True), -1)
        qkv_b = jnp.concatenate([(q * cos + swap_halves(q) * sin).astype(BF), kv_b], axis=-1)
        ctx = call_attention(
            attn_fwd_kernel,
            m_arr,
            [qkv_b, lo, hi, docs_col, docs_row],
            [jax.ShapeDtypeStruct((micro, team_rows, head_cols), BF)],
            windowed,
        )[0]
        part = mm(flat(ctx), wo, 1, 1).astype(BF).reshape(micro, team_rows, feat)
        mid_own = x_own + sum_rows(part)
        b = gather_rows((norm_parts(mid_own)[0] * g_mlp).astype(BF))
        gu = mm(flat(b), wf[:, : 2 * units], 1, 0)
        gate, up = gu[:, :units], gu[:, units:]
        hid = (gelu_parts(gate)[0] * up).astype(BF)
        part = mm(hid, wf[:, 2 * units :], 1, 1).astype(BF).reshape(micro, team_rows, feat)
        saved.append((x_own, a, qkv_b, lo, hi, ctx, mid_own, b, gate, up, hid))
        x_own = mid_own + sum_rows(part)

    def join_core(own):
        other = hop_core(own)
        first = jnp.where(c == 0, own, other)
        second = jnp.where(c == 0, other, own)
        return jnp.concatenate([first, second], axis=1)

    hidden_out = join_core(x_own.astype(BF))

    dy_own = grad_own.astype(F32)
    dyb = grad_all
    reduced = [None] * layers
    for layer in reversed(range(layers)):
        windowed = layer % 2 == 0
        wa, wf = packs[layer]
        w3 = wa[:, : 3 * head_cols]
        wo = wa[:, 3 * head_cols : 4 * head_cols]
        g_attn, g_mlp = gains[layer], gains[layers + layer]
        x_in, a, qkv_b, lo, hi, ctx, mid_own, b, gate, up, hid = saved[layer]
        dyb2 = flat(dyb)
        dhid = mm(dyb2, wf[:, 2 * units :], 1, 0)
        act, slope = gelu_parts(gate)
        dgu = jnp.concatenate([dhid * up * slope, dhid * act], axis=1).astype(BF)
        part = mm(dgu, wf[:, : 2 * units], 1, 1).astype(BF).reshape(micro, team_rows, feat)
        db = sum_rows(part)
        d_ffn = jnp.concatenate(
            [mm(flat(b), dgu, 0, 0).astype(BF), mm(dyb2, hid, 0, 0).astype(BF)], axis=1
        )
        ffn_parts = collect(d_ffn, t, z, d_rows)
        back, dg_mlp = norm_back(db, mid_own, g_mlp)
        dmid_own = dy_own + back
        dmb = gather_rows(dmid_own.astype(BF))
        dmb2 = flat(dmb)
        dctx = mm(dmb2, wo, 1, 0).astype(BF).reshape(micro, team_rows, head_cols)
        band = team_rows + 2 * BLK
        dq, dk, dv = call_attention(
            attn_bwd_kernel,
            m_arr,
            [qkv_b, lo, hi, docs_col, docs_row, dctx],
            [
                jax.ShapeDtypeStruct((micro, team_rows, head_cols), F32),
                jax.ShapeDtypeStruct((micro, band, head_cols), F32),
                jax.ShapeDtypeStruct((micro, band, head_cols), F32),
            ],
            windowed,
        )
        dkv = jnp.concatenate([dk, dv], axis=-1)
        from_next = step_z(dkv[:, BLK + team_rows :].astype(BF), 1).astype(F32)
        from_prev = step_z(dkv[:, :BLK].astype(BF), -1).astype(F32)
        dkv = dkv[:, BLK : BLK + team_rows]
        dkv = dkv.at[:, :BLK].add(from_next).at[:, team_rows - BLK :].add(from_prev)
        true_blocks = dkv.reshape(micro, 2 * TEAM, own_rows, 2 * head_cols)
        dkv = jnp.concatenate(
            [lax.dynamic_index_in_dim(true_blocks, m ^ j, 1, False) for j in range(2 * TEAM)], axis=1
        )
        cos, sin = tables[layer]
        dk, dv = dkv[:, :, :head_cols], dkv[:, :, head_cols:]
        dqkv = jnp.concatenate(
            [dq * cos + swap_halves(dq * sin), dk * cos + swap_halves(dk * sin), dv], axis=-1
        ).astype(BF)
        dqkv2 = flat(dqkv)
        part = mm(dqkv2, w3, 1, 1).astype(BF).reshape(micro, team_rows, feat)
        da = sum_rows(part)
        back, dg_attn = norm_back(da, x_in, g_attn)
        dy_own = dmid_own + back
        if layer > 0:
            dyb = gather_rows(dy_own.astype(BF))
        d_gain = jnp.pad(jnp.stack([dg_attn, dg_mlp], axis=1), ((0, 0), (0, 126))).astype(BF)
        d_attn = jnp.concatenate(
            [mm(flat(a), dqkv2, 0, 0).astype(BF), mm(dmb2, flat(ctx), 0, 0).astype(BF), d_gain],
            axis=1,
        )
        reduced[layer] = (collect(d_attn, t, z, d_rows), ffn_parts)

    input_grad = join_core(dy_own)

    g_attn_out, g_mlp_out, g_qkv, g_out, g_in, g_down = [], [], [], [], [], []
    for layer in range(layers):
        attn_parts, ffn_parts = reduced[layer]
        g_qkv.append(jnp.stack([columns(attn_parts, t, i * head_cols, head_cols) for i in range(3)]))
        g_out.append(columns(attn_parts, t, 3 * head_cols, head_cols))
        gain_sum = sum(p[:, 4 * head_cols : 4 * head_cols + 2] for p in attn_parts)
        gain_sum = gain_sum + hop_core(gain_sum)
        g_attn_out.append(gain_sum[:, 0])
        g_mlp_out.append(gain_sum[:, 1])
        g_in.append(jnp.stack([columns(ffn_parts, t, i * units, units)[:, :unit_real] for i in range(2)]))
        g_down.append(columns(ffn_parts, t, 2 * units, units)[:, :unit_real])
    return (
        hidden_out,
        input_grad,
        jnp.stack(g_attn_out),
        jnp.stack(g_mlp_out),
        jnp.stack(g_qkv),
        jnp.stack(g_out),
        jnp.stack(g_in),
        jnp.stack(g_down),
    )


def solution(mesh):
    dp, tensor = mesh.devices.shape
    fine = Mesh(mesh.devices.reshape(dp // TEAM, 2, 2, tensor), ("z", "y", "x", "c"))
    rows = ("z", "y", "x")
    in_specs = (
        P(None, rows, None),
        P(),
        P(None, rows),
        P(None, rows),
        P(None, None, rows, "c"),
        P(None, rows, "c"),
        P(None, None, rows, "c"),
        P(None, rows, "c"),
        P(None, rows, None),
    )
    out_specs = (
        P(None, rows, None),
        P(None, rows, None),
        P(None, rows),
        P(None, rows),
        P(None, None, rows, "c"),
        P(None, rows, "c"),
        P(None, None, rows, "c"),
        P(None, rows, "c"),
    )
    return jax.shard_map(shards, mesh=fine, in_specs=in_specs, out_specs=out_specs, check_vma=False)
```

time: 2500 us -> 892 us (0.36)
  waiting for transfers between devices: 1920 us -> 347 us
  matrix products: 149 us -> 30.1 us
  starting transfers between devices: 59 us -> 159 us
  blocking collectives: 44.4 us -> 0 us
  local copies, waits for them, and re-layouts: 180 us -> 215 us
  Pallas kernels: 0 us -> 28.8 us
    unnamed x25 -> x0, waiting for transfers between devices: 1270 us -> none
    all_gather x8 -> x0, waiting for transfers between devices: 435 us -> none  [the longest x2 176 us: fetch_layer(): lax.all_gather(w_ffn_in[layer_idx], 'dp', axis=1, tiled=True)]
    ppermute x16 -> x124, waiting for transfers between devices: 24.1 us -> 347 us  [the longest x24 222 us: hop_z(): return lax.ppermute(x, 'z', [(i, (i + s) % n) for i in range(n)])]
    dot_general x72 -> x24, matrix products: 149 us -> 30.1 us  [mm(): lax.dot_general(a, b, (((ca,), (cb,)), ((), ())), preferred_element_type=...]
    ppermute x16 -> x124, starting transfers between devices: 56.9 us -> 159 us  [the longest x72 84.9 us: hop_team(): return lax.ppermute(x, ('y', 'x'), [(i, i ^ k) for i in range(TEAM)])]
    psum x8 -> x0, waiting for transfers between devices: 99.7 us -> none  [heads_total(): lax.psum(partial_rows.astype(jnp.bfloat16), 'tensor').astype(jnp.float32)]
    reduce_scatter x1 -> x0, waiting for transfers between devices: 92.7 us -> none  [shards(): lax.psum_scatter(joined[3], 'dp', scatter_dimension=1, tiled=True)]
    dynamic_update_slice x0 -> x79, local copies, waits for them, and re-layouts: none -> 60.1 us  [the longest x49 31.5 us: columns(): lax.dynamic_update_slice(full, parts[k][:, lo:lo + width], (0, (t ^ k) *...]
  transfers between devices with their start and end apart: 37 -> 124, of which waited for: 27 -> 53; matrix products, arithmetic and copies ran while one was open for 11% -> 30% of each run, Pallas kernels for 0% -> 2%
where the time goes in v1:
time: 892 us; the launch traced here: 879 us
  waiting for transfers between devices  347 us (39%)
  local copies, waits for them, and re-layouts  215 us (24%)
  starting transfers between devices  159 us (18%)
  other arithmetic  92.8 us (10%)
  matrix products  30.1 us (3%)
  Pallas kernels  28.8 us (3%)
    ppermute x24, waiting for transfers between devices, hop_z(): return lax.ppermute(x, 'z', [(i, (i + s) % n) for i in range(n)])  222 us
    ppermute x72, waiting for transfers between devices, hop_team(): return lax.ppermute(x, ('y', 'x'), [(i, i ^ k) for i in range(TEAM)])  99.7 us
    ppermute x72, starting transfers between devices, hop_team(): return lax.ppermute(x, ('y', 'x'), [(i, i ^ k) for i in range(TEAM)])  84.9 us
    ppermute x24, starting transfers between devices, hop_z(): return lax.ppermute(x, 'z', [(i, (i + s) % n) for i in range(n)])  45.9 us
    slice x32, local copies, waits for them, and re-layouts, columns(): parts[k][:, lo:lo + width]  43.8 us
    unnamed x370, local copies, waits for them, and re-layouts  36.2 us
    dynamic_update_slice x49, local copies, waits for them, and re-layouts, columns(): lax.dynamic_update_slice(full, parts[k][:, lo:lo + width], (0, (t ^ k) *...  31.5 us
    dot_general x24, matrix products, mm(): lax.dot_general(a, b, (((ca,), (cb,)), ((), ())), preferred_element_type=...  30.1 us
  transfers between devices with their start and end apart: 124, of which 53 were waited for; matrix products, arithmetic and copies ran while one was open for 30% of the time, Pallas kernels for 2%

profile of v1, /device:TPU:0, one launch (start us, length us, event | category | flops | bytes accessed | tf_op | source)
XLA Modules:
  0.0 878.6 jit_solution(9221004053447037319)
XLA Ops:
  25.1 6.1 fusion.129
  57.4 12.9 %collective-permute-done.8 = bf16[256,640]{0,1:T(8,128)(2,1)S(1)} collective-permute-done((bf16[256,640]{0,1:T(8,128)(2,1)}, bf16[256,640]{0,1:T(8,128)(2,1)S(1)}, u32[]{:S(2)}, u32[]{:S(2)}) %collective-permute-start.8) | collective-permute-done | bytes 327712 | tf_op jit(solution)/shard_map/ppermute | solution.py:34
  87.3 9.3 %collective-permute-start.10 = (bf16[2,128,256]{2,1,0:T(8,128)(2,1)S(1)}, bf16[2,128,256]{2,1,0:T(8,128)(2,1)S(1)}, u32[]{:S(2)}, u32[]{:S(2)}) collective-permute-start(bf16[2,128,256]{2,1,0:T(8,128)(2,1)S(1)} %pad_maximum_fusion.44), channel_id=1, source_target_pairs={{0,8},{8,16},{16,24},{1,9},{9,17},{17,25},{2,10},{10,18},{18,26},{... | collective-permute-start | bytes 393224 | tf_op jit(solution)/shard_map/ppermute | solution.py:39
  103.8 5.8 shard_map.152
  120.1 7.8 collective-permute-done.21
  140.1 4.9 collective-permute-done.18
  150.4 6.2 collective-permute-done.23
  156.6 23.3 %collective-permute-done.24 = bf16[256,1152]{1,0:T(8,128)(2,1)S(1)} collective-permute-done((bf16[256,1152]{1,0:T(8,128)(2,1)S(1)}, bf16[256,1152]{1,0:T(8,128)(2,1)S(1)}, u32[]{:S(2)}, u32[]{:S(2)}) %collective-permute-start.24) | collective-permute-done | bytes 589856 | tf_op jit(solution)/shard_map/ppermute | solution.py:34
  236.1 12.1 %collective-permute-start.37 = (bf16[256,512]{0,1:T(8,128)(2,1)}, bf16[256,512]{0,1:T(8,128)(2,1)S(1)}, u32[]{:S(2)}, u32[]{:S(2)}) collective-permute-start(bf16[256,512]{0,1:T(8,128)(2,1)} %dynamic_update_slice.315), channel_id=1, source_target_pairs={{0,8},{8,16},{16,24},{24,0},{1,9},{9,17},{17,25},{25,1},{2,10},{10... | collective-permute-start | bytes 786440 | tf_op jit(solution)/shard_map/ppermute | solution.py:34
  256.6 11.0 %collective-permute-done.38 = bf16[256,512]{0,1:T(8,128)(2,1)S(1)} collective-permute-done((bf16[256,512]{0,1:T(8,128)(2,1)}, bf16[256,512]{0,1:T(8,128)(2,1)S(1)}, u32[]{:S(2)}, u32[]{:S(2)}) %collective-permute-start.38) | collective-permute-done | bytes 262176 | tf_op jit(solution)/shard_map/ppermute | solution.py:34
  275.9 8.0 collective-permute-start.40
  291.0 5.8 shard_map.153
  314.9 6.9 collective-permute-done.51
  337.2 4.7 collective-permute-done.48
  347.2 22.1 %collective-permute-done.54 = bf16[256,1152]{1,0:T(8,128)(2,1)S(1)} collective-permute-done((bf16[256,1152]{1,0:T(8,128)(2,1)}, bf16[256,1152]{1,0:T(8,128)(2,1)S(1)}, u32[]{:S(2)}, u32[]{:S(2)}) %collective-permute-start.54) | collective-permute-done | bytes 589856 | tf_op jit(solution)/shard_map/ppermute | solution.py:34
  386.1 9.2 %collective-permute-start.120 = (bf16[256,1152]{0,1:T(8,128)(2,1)S(1)}, bf16[256,1152]{0,1:T(8,128)(2,1)S(1)}, u32[]{:S(2)}, u32[]{:S(2)}) collective-permute-start(bf16[256,1152]{0,1:T(8,128)(2,1)S(1)} %get-tuple-element.118), channel_id=1, source_target_pairs={{0,24},{8,0},{16,8},{24,16},{1,25},{9,1},{17,9},{25,17},{2,26},{10... | collective-permute-start | bytes 1769480 | tf_op jit(solution)/shard_map/ppermute | solution.py:34
  400.8 8.5 collective-permute-done.120
  409.3 39.1 %collective-permute-done.119 = bf16[256,1152]{0,1:T(8,128)(2,1)S(1)} collective-permute-done((bf16[256,1152]{0,1:T(8,128)(2,1)S(1)}, bf16[256,1152]{0,1:T(8,128)(2,1)S(1)}, u32[]{:S(2)}, u32[]{:S(2)}) %collective-permute-start.119) | collective-permute-done | bytes 589856 | tf_op jit(solution)/shard_map/ppermute | solution.py:34
  514.6 8.6 shard_map.154
  528.1 5.2 collective-permute-done.74
  556.5 5.4 collective-permute-done.78
  562.8 9.6 %collective-permute-done.77 = bf16[2,64,1024]{2,1,0:T(8,128)(2,1)S(1)} collective-permute-done((bf16[2,64,1024]{2,1,0:T(8,128)(2,1)S(1)}, bf16[2,64,1024]{2,1,0:T(8,128)(2,1)S(1)}, u32[]{:S(2)}, u32[]{:S(2)}) %collective-permute-start.77) | collective-permute-done | bytes 262176 | tf_op jit(solution)/shard_map/ppermute | solution.py:25
  578.3 6.0 collective-permute-done.81
  592.6 17.7 %collective-permute-done.106 = bf16[256,640]{0,1:T(8,128)(2,1)S(1)} collective-permute-done((bf16[256,640]{0,1:T(8,128)(2,1)S(1)}, bf16[256,640]{0,1:T(8,128)(2,1)S(1)}, u32[]{:S(2)}, u32[]{:S(2)}) %collective-permute-start.106) | collective-permute-done | bytes 327712 | tf_op jit(solution)/shard_map/ppermute | solution.py:34
  663.1 11.5 %collective-permute-done.114 = bf16[256,1152]{0,1:T(8,128)(2,1)S(1)} collective-permute-done((bf16[256,1152]{0,1:T(8,128)(2,1)S(1)}, bf16[256,1152]{0,1:T(8,128)(2,1)S(1)}, u32[]{:S(2)}, u32[]{:S(2)}) %collective-permute-start.114) | collective-permute-done | bytes 589856 | tf_op jit(solution)/shard_map/ppermute | solution.py:34
  674.6 35.1 %collective-permute-done.113 = bf16[256,1152]{0,1:T(8,128)(2,1)S(1)} collective-permute-done((bf16[256,1152]{0,1:T(8,128)(2,1)S(1)}, bf16[256,1152]{0,1:T(8,128)(2,1)S(1)}, u32[]{:S(2)}, u32[]{:S(2)}) %collective-permute-start.113) | collective-permute-done | bytes 589856 | tf_op jit(solution)/shard_map/ppermute | solution.py:34
  773.2 8.6 shard_map.155
  788.6 6.1 collective-permute-done.92
  807.8 5.4 collective-permute-done.96
  813.2 5.2 collective-permute-done.95
  823.0 5.8 collective-permute-done.100
  828.8 22.2 %collective-permute-done.99 = bf16[256,640]{0,1:T(8,128)(2,1)S(1)} collective-permute-done((bf16[256,640]{0,1:T(8,128)(2,1)S(1)}, bf16[256,640]{0,1:T(8,128)(2,1)S(1)}, u32[]{:S(2)}, u32[]{:S(2)}) %collective-permute-start.99) | collective-permute-done | bytes 327712 | tf_op jit(solution)/shard_map/ppermute | solution.py:34
  (1036 shorter events, 517.6 us)
Async XLA Ops:
  2.4 45.6 %collective-permute-start.2 = (bf16[2,64,1024]{2,1,0:T(8,128)(2,1)S(1)}, bf16[2,64,1024]{2,1,0:T(8,128)(2,1)S(1)}, u32[]{:S(2)}, u32[]{:S(2)}) collective-permute-start(bf16[2,64,1024]{2,1,0:T(8,128)(2,1)S(1)} %get-tuple-element.90), channel_id=1, source_target_pairs={{0,6},{2,4},{4,2},{6,0},{1,7},{3,5},{5,3},{7,1},{8,14},{10,12},{12... | collective-permute-start | bytes 786440 | tf_op jit(solution)/shard_map/ppermute | solution.py:25
  6.3 41.7 %collective-permute-start.1 = (bf16[2,64,1024]{2,1,0:T(8,128)(2,1)S(1)}, bf16[2,64,1024]{2,1,0:T(8,128)(2,1)}, u32[]{:S(2)}, u32[]{:S(2)}) collective-permute-start(bf16[2,64,1024]{2,1,0:T(8,128)(2,1)S(1)} %get-tuple-element.90), channel_id=1, source_target_pairs={{0,4},{2,6},{4,0},{6,2},{1,5},{3,7},{5,1},{7,3},{8,12},{10,14},{12... | collective-permute-start | bytes 786440 | tf_op jit(solution)/shard_map/ppermute | solution.py:25
  6.8 41.2 %collective-permute-start = (bf16[2,64,1024]{2,1,0:T(8,128)(2,1)S(1)}, bf16[2,64,1024]{2,1,0:T(8,128)(2,1)}, u32[]{:S(2)}, u32[]{:S(2)}) collective-permute-start(bf16[2,64,1024]{2,1,0:T(8,128)(2,1)S(1)} %get-tuple-element.90), channel_id=1, source_target_pairs={{0,2},{2,0},{4,6},{6,4},{1,3},{3,1},{5,7},{7,5},{8,10},{10,8},{12,... | collective-permute-start | bytes 786440 | tf_op jit(solution)/shard_map/ppermute | solution.py:25
  114.9 23.4 %collective-permute-start.22 = (bf16[64,1152]{1,0:T(8,128)(2,1)S(1)}, bf16[64,1152]{1,0:T(8,128)(2,1)S(1)}, u32[]{:S(2)}, u32[]{:S(2)}) collective-permute-start(bf16[64,1152]{1,0:T(8,128)(2,1)S(1)} %pad_maximum_fusion.40), channel_id=1, source_target_pairs={{0,6},{2,4},{4,2},{6,0},{1,7},{3,5},{5,3},{7,1},{8,14},{10,12},{12... | collective-permute-start | bytes 442376 | tf_op jit(solution)/shard_map/ppermute | solution.py:25
  138.7 41.2 %collective-permute-start.24 = (bf16[256,1152]{1,0:T(8,128)(2,1)S(1)}, bf16[256,1152]{1,0:T(8,128)(2,1)S(1)}, u32[]{:S(2)}, u32[]{:S(2)}) collective-permute-start(bf16[256,1152]{1,0:T(8,128)(2,1)S(1)} %constant_dynamic-update-slice_fusion.95), channel_id=1, source_target_pairs={{0,16},{8,24},{16,0},{24,8},{1,17},{9,25},{17,1},{25,9},{2,18},{10... | collective-permute-start | bytes 1769480 | tf_op jit(solution)/shard_map/ppermute | solution.py:34
  149.5 30.6 %collective-permute-start.19 = (bf16[2,4,64,1024]{3,2,0,1:T(8,128)(2,1)S(1)}, bf16[2,4,64,1024]{3,2,0,1:T(8,128)(2,1)S(1)}, u32[]{:S(2)}, u32[]{:S(2)}) collective-permute-start(bf16[2,4,64,1024]{3,2,0,1:T(8,128)(2,1)S(1)} %get-tuple-element.215), channel_id=1, source_target_pairs={{0,1},{1,0},{2,3},{3,2},{4,5},{5,4},{6,7},{7,6},{8,9},{9,8},{10,11... | collective-permute-start | bytes 3145736 | tf_op jit(solution)/shard_map/ppermute | solution.py:29
  149.6 30.4 %collective-permute-start.25 = (bf16[256,1152]{1,0:T(8,128)(2,1)S(1)}, bf16[256,1152]{1,0:T(8,128)(2,1)S(1)}, u32[]{:S(2)}, u32[]{:S(2)}) collective-permute-start(bf16[256,1152]{1,0:T(8,128)(2,1)S(1)} %constant_dynamic-update-slice_fusion.95), channel_id=1, source_target_pairs={{0,24},{8,0},{16,8},{24,16},{1,25},{9,1},{17,9},{25,17},{2,26},{10... | collective-permute-start | bytes 1769480 | tf_op jit(solution)/shard_map/ppermute | solution.py:34
  196.1 34.0 %collective-permute-start.34 = (bf16[64,512]{0,1:T(8,128)(2,1)}, bf16[64,512]{0,1:T(8,128)(2,1)}, u32[]{:S(2)}, u32[]{:S(2)}) collective-permute-start(bf16[64,512]{0,1:T(8,128)(2,1)} %pad_maximum_fusion.47), channel_id=1, source_target_pairs={{0,2},{2,0},{4,6},{6,4},{1,3},{3,1},{5,7},{7,5},{8,10},{10,8},{12,... | collective-permute-start | bytes 196616 | tf_op jit(solution)/shard_map/ppermute | solution.py:25
  201.1 31.3 %collective-permute-start.35 = (bf16[64,512]{0,1:T(8,128)(2,1)}, bf16[64,512]{0,1:T(8,128)(2,1)}, u32[]{:S(2)}, u32[]{:S(2)}) collective-permute-start(bf16[64,512]{0,1:T(8,128)(2,1)} %pad_maximum_fusion.48), channel_id=1, source_target_pairs={{0,4},{2,6},{4,0},{6,2},{1,5},{3,7},{5,1},{7,3},{8,12},{10,14},{12... | collective-permute-start | bytes 196616 | tf_op jit(solution)/shard_map/ppermute | solution.py:25
  227.2 40.5 %collective-permute-start.33 = (bf16[2,4,64,1024]{3,2,0,1:T(8,128)(2,1)}, bf16[2,4,64,1024]{3,2,0,1:T(8,128)(2,1)}, u32[]{:S(2)}, u32[]{:S(2)}) collective-permute-start(bf16[2,4,64,1024]{3,2,0,1:T(8,128)(2,1)} %get-tuple-element.210), channel_id=1, source_target_pairs={{0,1},{1,0},{2,3},{3,2},{4,5},{5,4},{6,7},{7,6},{8,9},{9,8},{10,11... | collective-permute-start | bytes 3145736 | tf_op jit(solution)/shard_map/ppermute | solution.py:29
  251.2 57.0 %collective-permute-start.50 = (bf16[64,1152]{1,0:T(8,128)(2,1)}, bf16[64,1152]{1,0:T(8,128)(2,1)}, u32[]{:S(2)}, u32[]{:S(2)}) collective-permute-start(bf16[64,1152]{1,0:T(8,128)(2,1)} %pad_maximum_fusion.41), channel_id=1, source_target_pairs={{0,2},{2,0},{4,6},{6,4},{1,3},{3,1},{5,7},{7,5},{8,10},{10,8},{12,... | collective-permute-start | bytes 442376 | tf_op jit(solution)/shard_map/ppermute | solution.py:25
  304.0 30.2 %collective-permute-start.63 = (bf16[2,64,1024]{2,1,0:T(8,128)(2,1)}, bf16[2,64,1024]{2,1,0:T(8,128)(2,1)S(1)}, u32[]{:S(2)}, u32[]{:S(2)}) collective-permute-start(bf16[2,64,1024]{2,1,0:T(8,128)(2,1)} %constant_dynamic-slice_fusion.39), channel_id=1, source_target_pairs={{0,6},{2,4},{4,2},{6,0},{1,7},{3,5},{5,3},{7,1},{8,14},{10,12},{12... | collective-permute-start | bytes 786440 | tf_op jit(solution)/shard_map/ppermute | solution.py:25
  334.2 35.1 %collective-permute-start.54 = (bf16[256,1152]{1,0:T(8,128)(2,1)}, bf16[256,1152]{1,0:T(8,128)(2,1)S(1)}, u32[]{:S(2)}, u32[]{:S(2)}) collective-permute-start(bf16[256,1152]{1,0:T(8,128)(2,1)} %constant_dynamic-update-slice_fusion.84), channel_id=1, source_target_pairs={{0,16},{8,24},{16,0},{24,8},{1,17},{9,25},{17,1},{25,9},{2,18},{10... | collective-permute-start | bytes 1769480 | tf_op jit(solution)/shard_map/ppermute | solution.py:34
  341.9 31.4 %collective-permute-start.64 = (bf16[2,4,64,1024]{3,2,0,1:T(8,128)(2,1)S(1)}, bf16[2,4,64,1024]{3,2,0,1:T(8,128)(2,1)S(1)}, u32[]{:S(2)}, u32[]{:S(2)}) collective-permute-start(bf16[2,4,64,1024]{3,2,0,1:T(8,128)(2,1)S(1)} %get-tuple-element.200), channel_id=1, source_target_pairs={{0,1},{1,0},{2,3},{3,2},{4,5},{5,4},{6,7},{7,6},{8,9},{9,8},{10,11... | collective-permute-start | bytes 3145736 | tf_op jit(solution)/shard_map/ppermute | solution.py:29
  345.7 27.5 %collective-permute-start.55 = (bf16[256,1152]{1,0:T(8,128)(2,1)}, bf16[256,1152]{1,0:T(8,128)(2,1)S(1)}, u32[]{:S(2)}, u32[]{:S(2)}) collective-permute-start(bf16[256,1152]{1,0:T(8,128)(2,1)} %constant_dynamic-update-slice_fusion.84), channel_id=1, source_target_pairs={{0,24},{8,0},{16,8},{24,16},{1,25},{9,1},{17,9},{25,17},{2,26},{10... | collective-permute-start | bytes 1769480 | tf_op jit(solution)/shard_map/ppermute | solution.py:34
  347.0 27.7 %collective-permute-start.49 = (bf16[2,4,64,1024]{3,2,0,1:T(8,128)(2,1)S(1)}, bf16[2,4,64,1024]{3,2,0,1:T(8,128)(2,1)S(1)}, u32[]{:S(2)}, u32[]{:S(2)}) collective-permute-start(bf16[2,4,64,1024]{3,2,0,1:T(8,128)(2,1)S(1)} %get-tuple-element.205), channel_id=1, source_target_pairs={{0,1},{1,0},{2,3},{3,2},{4,5},{5,4},{6,7},{7,6},{8,9},{9,8},{10,11... | collective-permute-start | bytes 3145736 | tf_op jit(solution)/shard_map/ppermute | solution.py:29
  384.8 86.8 %collective-permute-start.65 = (bf16[2,4,64,1024]{3,2,0,1:T(8,128)(2,1)}, bf16[2,4,64,1024]{3,2,0,1:T(8,128)(2,1)}, u32[]{:S(2)}, u32[]{:S(2)}) collective-permute-start(bf16[2,4,64,1024]{3,2,0,1:T(8,128)(2,1)} %bitcast.629), channel_id=1, source_target_pairs={{0,1},{1,0},{2,3},{3,2},{4,5},{5,4},{6,7},{7,6},{8,9},{9,8},{10,11... | collective-permute-start | bytes 3145736 | tf_op jit(solution)/shard_map/ppermute | solution.py:29
  386.1 23.3 %collective-permute-start.120 = (bf16[256,1152]{0,1:T(8,128)(2,1)S(1)}, bf16[256,1152]{0,1:T(8,128)(2,1)S(1)}, u32[]{:S(2)}, u32[]{:S(2)}) collective-permute-start(bf16[256,1152]{0,1:T(8,128)(2,1)S(1)} %get-tuple-element.118), channel_id=1, source_target_pairs={{0,24},{8,0},{16,8},{24,16},{1,25},{9,1},{17,9},{25,17},{2,26},{10... | collective-permute-start | bytes 1769480 | tf_op jit(solution)/shard_map/ppermute | solution.py:34
  395.3 53.1 %collective-permute-start.119 = (bf16[256,1152]{0,1:T(8,128)(2,1)S(1)}, bf16[256,1152]{0,1:T(8,128)(2,1)S(1)}, u32[]{:S(2)}, u32[]{:S(2)}) collective-permute-start(bf16[256,1152]{0,1:T(8,128)(2,1)S(1)} %get-tuple-element.117), channel_id=1, source_target_pairs={{0,16},{8,24},{16,0},{24,8},{1,17},{9,25},{17,1},{25,9},{2,18},{10... | collective-permute-start | bytes 1769480 | tf_op jit(solution)/shard_map/ppermute | solution.py:34
  396.8 51.6 %collective-permute-start.118 = (bf16[256,1152]{0,1:T(8,128)(2,1)S(1)}, bf16[256,1152]{0,1:T(8,128)(2,1)S(1)}, u32[]{:S(2)}, u32[]{:S(2)}) collective-permute-start(bf16[256,1152]{0,1:T(8,128)(2,1)S(1)} %get-tuple-element.116), channel_id=1, source_target_pairs={{0,8},{8,16},{16,24},{24,0},{1,9},{9,17},{17,25},{25,1},{2,10},{10... | collective-permute-start | bytes 1769480 | tf_op jit(solution)/shard_map/ppermute | solution.py:34
  400.8 143.1 %collective-permute-start.56 = (bf16[2,4,64,1024]{3,2,0,1:T(8,128)(2,1)}, bf16[2,4,64,1024]{3,2,0,1:T(8,128)(2,1)}, u32[]{:S(2)}, u32[]{:S(2)}) collective-permute-start(bf16[2,4,64,1024]{3,2,0,1:T(8,128)(2,1)} %bitcast.630), channel_id=1, source_target_pairs={{0,1},{1,0},{2,3},{3,2},{4,5},{5,4},{6,7},{7,6},{8,9},{9,8},{10,11... | collective-permute-start | bytes 3145736 | tf_op jit(solution)/shard_map/ppermute | solution.py:29
  456.0 25.2 %collective-permute-start.123 = (bf16[64,1152]{0,1:T(8,128)(2,1)}, bf16[64,1152]{0,1:T(8,128)(2,1)}, u32[]{:S(2)}, u32[]{:S(2)}) collective-permute-start(bf16[64,1152]{0,1:T(8,128)(2,1)} %get-tuple-element.238), channel_id=1, source_target_pairs={{0,6},{2,4},{4,2},{6,0},{1,7},{3,5},{5,3},{7,1},{8,14},{10,12},{12... | collective-permute-start | bytes 442376 | tf_op jit(solution)/shard_map/ppermute | solution.py:25
  545.9 26.9 %collective-permute-start.59 = (bf16[2,64,1024]{2,1,0:T(8,128)(2,1)S(1)}, bf16[2,64,1024]{2,1,0:T(8,128)(2,1)S(1)}, u32[]{:S(2)}, u32[]{:S(2)}) collective-permute-start(bf16[2,64,1024]{2,1,0:T(8,128)(2,1)S(1)} %get-tuple-element.202), channel_id=1, source_target_pairs={{0,6},{2,4},{4,2},{6,0},{1,7},{3,5},{5,3},{7,1},{8,14},{10,12},{12... | collective-permute-start | bytes 786440 | tf_op jit(solution)/shard_map/ppermute | solution.py:25
  547.7 25.1 %collective-permute-start.58 = (bf16[2,64,1024]{2,1,0:T(8,128)(2,1)S(1)}, bf16[2,64,1024]{2,1,0:T(8,128)(2,1)S(1)}, u32[]{:S(2)}, u32[]{:S(2)}) collective-permute-start(bf16[2,64,1024]{2,1,0:T(8,128)(2,1)S(1)} %get-tuple-element.203), channel_id=1, source_target_pairs={{0,4},{2,6},{4,0},{6,2},{1,5},{3,7},{5,1},{7,3},{8,12},{10,14},{12... | collective-permute-start | bytes 786440 | tf_op jit(solution)/shard_map/ppermute | solution.py:25
  584.3 25.9 %collective-permute-start.106 = (bf16[256,640]{0,1:T(8,128)(2,1)S(1)}, bf16[256,640]{0,1:T(8,128)(2,1)S(1)}, u32[]{:S(2)}, u32[]{:S(2)}) collective-permute-start(bf16[256,640]{0,1:T(8,128)(2,1)S(1)} %get-tuple-element.172), channel_id=1, source_target_pairs={{0,16},{8,24},{16,0},{24,8},{1,17},{9,25},{17,1},{25,9},{2,18},{10... | collective-permute-start | bytes 983048 | tf_op jit(solution)/shard_map/ppermute | solution.py:34
  591.7 56.9 %collective-permute-start.82 = (bf16[2,4,64,1024]{3,2,0,1:T(8,128)(2,1)}, bf16[2,4,64,1024]{3,2,0,1:T(8,128)(2,1)}, u32[]{:S(2)}, u32[]{:S(2)}) collective-permute-start(bf16[2,4,64,1024]{3,2,0,1:T(8,128)(2,1)} %get-tuple-element.190), channel_id=1, source_target_pairs={{0,1},{1,0},{2,3},{3,2},{4,5},{5,4},{6,7},{7,6},{8,9},{9,8},{10,11... | collective-permute-start | bytes 3145736 | tf_op jit(solution)/shard_map/ppermute | solution.py:29
  657.6 52.1 %collective-permute-start.113 = (bf16[256,1152]{0,1:T(8,128)(2,1)S(1)}, bf16[256,1152]{0,1:T(8,128)(2,1)S(1)}, u32[]{:S(2)}, u32[]{:S(2)}) collective-permute-start(bf16[256,1152]{0,1:T(8,128)(2,1)S(1)} %get-tuple-element.114), channel_id=1, source_target_pairs={{0,16},{8,24},{16,0},{24,8},{1,17},{9,25},{17,1},{25,9},{2,18},{10... | collective-permute-start | bytes 1769480 | tf_op jit(solution)/shard_map/ppermute | solution.py:34
  657.9 51.8 %collective-permute-start.112 = (bf16[256,1152]{0,1:T(8,128)(2,1)S(1)}, bf16[256,1152]{0,1:T(8,128)(2,1)S(1)}, u32[]{:S(2)}, u32[]{:S(2)}) collective-permute-start(bf16[256,1152]{0,1:T(8,128)(2,1)S(1)} %get-tuple-element.113), channel_id=1, source_target_pairs={{0,8},{8,16},{16,24},{24,0},{1,9},{9,17},{17,25},{25,1},{2,10},{10... | collective-permute-start | bytes 1769480 | tf_op jit(solution)/shard_map/ppermute | solution.py:34
  663.1 76.0 %collective-permute-start.83 = (bf16[2,4,64,1024]{3,2,0,1:T(8,128)(2,1)}, bf16[2,4,64,1024]{3,2,0,1:T(8,128)(2,1)}, u32[]{:S(2)}, u32[]{:S(2)}) collective-permute-start(bf16[2,4,64,1024]{3,2,0,1:T(8,128)(2,1)} %bitcast.627), channel_id=1, source_target_pairs={{0,1},{1,0},{2,3},{3,2},{4,5},{5,4},{6,7},{7,6},{8,9},{9,8},{10,11... | collective-permute-start | bytes 3145736 | tf_op jit(solution)/shard_map/ppermute | solution.py:29
  819.6 31.5 %collective-permute-start.99 = (bf16[256,640]{0,1:T(8,128)(2,1)S(1)}, bf16[256,640]{0,1:T(8,128)(2,1)S(1)}, u32[]{:S(2)}, u32[]{:S(2)}) collective-permute-start(bf16[256,640]{0,1:T(8,128)(2,1)S(1)} %get-tuple-element.169), channel_id=1, source_target_pairs={{0,16},{8,24},{16,0},{24,8},{1,17},{9,25},{17,1},{25,9},{2,18},{10... | collective-permute-start | bytes 983048 | tf_op jit(solution)/shard_map/ppermute | solution.py:34
  822.3 28.7 %collective-permute-start.98 = (bf16[256,640]{0,1:T(8,128)(2,1)S(1)}, bf16[256,640]{0,1:T(8,128)(2,1)S(1)}, u32[]{:S(2)}, u32[]{:S(2)}) collective-permute-start(bf16[256,640]{0,1:T(8,128)(2,1)S(1)} %get-tuple-element.167), channel_id=1, source_target_pairs={{0,8},{8,16},{16,24},{24,0},{1,9},{9,17},{17,25},{25,1},{2,10},{10... | collective-permute-start | bytes 983048 | tf_op jit(solution)/shard_map/ppermute | solution.py:34
  822.9 54.2 %collective-permute-start.97 = (f32[2,64,1024]{2,1,0:T(8,128)S(1)}, f32[2,64,1024]{2,1,0:T(8,128)S(1)}, u32[]{:S(2)}, u32[]{:S(2)}) collective-permute-start(f32[2,64,1024]{2,1,0:T(8,128)S(1)} %fusion.62), channel_id=1, source_target_pairs={{0,1},{1,0},{2,3},{3,2},{4,5},{5,4},{6,7},{7,6},{8,9},{9,8},{10,11... | collective-permute-start | bytes 1572872 | tf_op jit(solution)/shard_map/ppermute | solution.py:29
  (245 other events, 2725.6 us)

commit v2 on v1

v2 whole, which is shorter than its diff:
```python
import jax
import jax.numpy as jnp
from jax import lax
from jax.experimental import pallas as pl
from jax.experimental.pallas import tpu as pltpu
from jax.sharding import Mesh
from jax.sharding import PartitionSpec as P

HD = 64
HALF = 64
BLK = 128
TEAM = 4
LOCAL = 2 * TEAM
MASKED = -1e30
BF = jnp.bfloat16
F32 = jnp.float32
CHAINS = 1


def mm(a, b, ca, cb):
    return lax.dot_general(a, b, (((ca,), (cb,)), ((), ())), preferred_element_type=F32)


def hop_team(x, k):
    return lax.ppermute(x, ("y", "x"), [(i, i ^ k) for i in range(TEAM)])


def hop_core(x):
    return lax.ppermute(x, "c", [(0, 1), (1, 0)])


def hop_z(x, s):
    n = lax.axis_size("z")
    return lax.ppermute(x, "z", [(i, (i + s) % n) for i in range(n)])


def step_z(x, by):
    n = lax.axis_size("z")
    return lax.ppermute(x, "z", [(i, i + by) for i in range(n) if 0 <= i + by < n])


def out(shape, dtype):
    return jax.ShapeDtypeStruct(shape, dtype)


def call(name, body, ids, ins, outs, scratch=(), flops=0):
    def kernel(*refs):
        n_in, n_out = len(ins), len(outs)
        body(refs[0], refs[1 : 1 + n_in], refs[1 + n_in : 1 + n_in + n_out], refs[1 + n_in + n_out :])

    moved = sum(a.size * a.dtype.itemsize for a in ins) + sum(
        o.size * jnp.dtype(o.dtype).itemsize for o in outs
    )
    vmem = pl.BlockSpec(memory_space=pltpu.VMEM)
    return pl.pallas_call(
        kernel,
        name=name,
        in_specs=[pl.BlockSpec(memory_space=pltpu.SMEM)] + [vmem] * len(ins),
        out_specs=[vmem] * len(outs),
        out_shape=list(outs),
        scratch_shapes=list(scratch),
        compiler_params=pltpu.CompilerParams(vmem_limit_bytes=24 * 1024 * 1024),
        cost_estimate=pl.CostEstimate(flops=flops, bytes_accessed=moved, transcendentals=0),
    )(ids, *ins)


def aligned(start, size):
    return pl.ds(pl.multiple_of(start, size), size)


def norm_parts(v):
    cent = v - jnp.mean(v, axis=-1, keepdims=True)
    rstd = lax.rsqrt(jnp.mean(cent * cent, axis=-1, keepdims=True) + 1e-05)
    return cent * rstd, rstd


def gelu_parts(gate):
    cdf = 0.5 * (1.0 + lax.erf(gate * 0.7071067811865476))
    return gate * cdf, cdf + gate * jnp.exp(-0.5 * gate * gate) * 0.3989422804014327


def swap_halves(v):
    width = v.shape[-1]
    lane = lax.broadcasted_iota(jnp.int32, v.shape, 1) % HD
    return jnp.where(
        lane < HD // 2, pltpu.roll(v, width - HD // 2, 1), pltpu.roll(v, HD // 2, 1)
    )


def true_rows(ids, n, sub, mb, b):
    blk = (ids[2] ^ (b % 2)) * TEAM + (ids[1] ^ (b // 2))
    return aligned((blk * n + mb) * sub, sub)


def tiles_of(refs, tile):
    rows = refs[0].shape[0]
    per = max(1, tile // rows)
    for first in range(0, len(refs), per):
        group = [r[...] for r in refs[first : first + per]]
        yield slice(first * rows, (first + per) * rows), (
            group[0] if per == 1 else jnp.concatenate(group, axis=0)
        )


def store_partial(p_refs, where, value):
    half = p_refs[0].shape[0]
    which = where.start // half
    p_refs[which][where.start - which * half : where.stop - which * half, :] = value.astype(BF)


def start_body(ids, ins, outs, scratch):
    tokens, grads, w_qkv, w_out, w_in, w_down = ins
    t, c = ids[1], ids[2]
    n, half = tokens.shape[0], tokens.shape[1] // 2
    for src, dst in ((tokens, outs[0]), (grads, outs[1])):
        for mb in range(n):
            dst[mb * half : (mb + 1) * half] = src[mb, aligned(c * half, half)]
    packs = outs[2:]
    layers, hc = w_qkv.shape[0], w_qkv.shape[3] // TEAM
    real, units = w_in.shape[3], scratch[0].shape[1] // TEAM
    scratch[0][...] = jnp.zeros(scratch[0].shape, BF)
    for layer in range(layers):
        for k in range(TEAM):
            dst = packs[layer * TEAM + k]
            cols = aligned((t ^ k) * hc, hc)
            for i in range(3):
                dst[:, i * hc : (i + 1) * hc] = w_qkv[layer, i, :, cols]
            dst[:, 3 * hc : 4 * hc] = w_out[layer, :, cols]
        for i in range(3):
            scratch[0][:, :real] = w_down[layer] if i == 2 else w_in[layer, i]
            for k in range(TEAM):
                cols = pl.ds(pl.multiple_of((t ^ k) * units, 128), units)
                packs[(layers + layer) * TEAM + k][:, i * units : (i + 1) * units] = scratch[0][:, cols]


def plane_body(ids, ins, outs, scratch):
    rows = ins[0].shape[0]
    for k in range(TEAM):
        outs[0][aligned((ids[1] ^ k) * rows, rows)] = ins[k][...]


def full_body(ids, ins, outs, scratch):
    rows, nz = ins[0].shape[0], len(ins)
    for s in range(nz):
        src = lax.rem(ids[0] - s + nz, nz)
        outs[0][aligned(src * rows, rows)] = ins[s][...]


def qkv_body(row, raw, n, sub):
    def body(ids, ins, outs, scratch):
        blocks, (gains, w, cos, sin) = ins[:LOCAL], ins[LOCAL:]
        a_ref, qkv_ref, lo_ref, hi_ref = outs
        hc = w.shape[1] // 4
        for where, tile in tiles_of(blocks, 256):
            if raw:
                tile = (norm_parts(tile.astype(F32))[0] * gains[row : row + 1]).astype(BF)
            a_ref[where] = tile
            r = mm(tile, w[:, : 3 * hc], 1, 0)
            cs, sn = cos[where], sin[where]
            q, k = r[:, :hc], r[:, hc : 2 * hc]
            qkv_ref[where, :hc] = (q * cs + swap_halves(q) * sn).astype(BF)
            qkv_ref[where, hc : 2 * hc] = (k * cs + swap_halves(k) * sn).astype(BF)
            qkv_ref[where, 2 * hc :] = r[:, 2 * hc :].astype(BF)
        per = BLK // sub
        for mb in range(n):
            for i in range(per):
                dst = slice(mb * BLK + i * sub, mb * BLK + (i + 1) * sub)
                lo_ref[dst] = qkv_ref[true_rows(ids, n, sub, mb, LOCAL - per + i), hc:]
                hi_ref[dst] = qkv_ref[true_rows(ids, n, sub, mb, i), hc:]

    return body


def fill_band(ids, mb, n, sub, qkv, lo, hi, kb, vb):
    hc = kb.shape[1]
    edge = slice(mb * BLK, (mb + 1) * BLK)
    last = BLK + LOCAL * sub
    kb[:BLK], vb[:BLK] = lo[edge, :hc], lo[edge, hc:]
    kb[last:], vb[last:] = hi[edge, :hc], hi[edge, hc:]
    for b in range(LOCAL):
        src = true_rows(ids, n, sub, mb, b)
        dst = slice(BLK + b * sub, BLK + (b + 1) * sub)
        kb[dst] = qkv[src, hc : 2 * hc]
        vb[dst] = qkv[src, 2 * hc :]


def allowed_of(mb, i, col, row, windowed):
    ok = col[mb, BLK + i * BLK : 2 * BLK + i * BLK, :] == row[mb, :, i * BLK : (i + 3) * BLK]
    if windowed:
        shape = (BLK, 3 * BLK)
        gap = lax.broadcasted_iota(jnp.int32, shape, 1) - lax.broadcasted_iota(jnp.int32, shape, 0)
        ok = ok & (gap <= BLK + HALF) & (gap >= BLK - HALF)
    return ok


def take(ids, ref, n, sub, mb, i, lanes):
    per = BLK // sub
    return jnp.concatenate(
        [ref[true_rows(ids, n, sub, mb, per * i + e), lanes] for e in range(per)], axis=0
    )


def put(ids, ref, n, sub, mb, i, lanes, value):
    for e in range(BLK // sub):
        per = BLK // sub
        ref[true_rows(ids, n, sub, mb, per * i + e), lanes] = value[e * sub : (e + 1) * sub]


def probs_of(qh, k, ok):
    s = jnp.where(ok, 0.125 * mm(qh, k, 1, 1), MASKED)
    e = jnp.exp(s - jnp.max(s, axis=1, keepdims=True))
    return e / jnp.sum(e, axis=1, keepdims=True)


def attn_body(windowed, n, sub):
    def body(ids, ins, outs, scratch):
        qkv, lo, hi, col, row, w = ins
        ctx_ref = outs[0]
        kb, vb = scratch
        hc = kb.shape[1]
        head_of = lax.broadcasted_iota(jnp.int32, (BLK, hc), 1) // HD
        for mb in range(n):
            fill_band(ids, mb, n, sub, qkv, lo, hi, kb, vb)
            for i in range(LOCAL * sub // BLK):
                ok = allowed_of(mb, i, col, row, windowed)
                q = take(ids, qkv, n, sub, mb, i, slice(0, hc))
                band = slice(i * BLK, (i + 3) * BLK)
                k, v = kb[band], vb[band]
                ctx = jnp.zeros((BLK, hc), F32)
                for h in range(hc // HD):
                    qh = jnp.where(head_of == h, q, jnp.zeros_like(q))
                    p = probs_of(qh, k, ok).astype(BF)
                    ctx = jnp.where(head_of == h, mm(p, v, 1, 0), ctx)
                put(ids, ctx_ref, n, sub, mb, i, slice(0, hc), ctx.astype(BF))
        total = ctx_ref.shape[0]
        for first in range(0, total, 256):
            where = slice(first, first + 256)
            store_partial(outs[1:], where, mm(ctx_ref[where], w[:, 3 * hc :], 1, 1))

    return body


def fold_body(ids, ins, outs, scratch):
    rows = outs[0].shape[0]
    for k in range(TEAM):
        where = slice(k * rows, (k + 1) * rows)
        both = ins[0][where].astype(F32) + ins[1][where].astype(F32)
        outs[k][...] = both.astype(outs[k].dtype)


def total_of(refs):
    value = refs[0][...].astype(F32)
    for r in refs[1:]:
        value = value + r[...].astype(F32)
    return value


def resid_body(row):
    def body(ids, ins, outs, scratch):
        x = ins[0][...].astype(F32) + total_of(ins[1 : 1 + TEAM])
        if row is None:
            outs[0][...] = x.astype(BF)
        else:
            outs[0][...] = x
            outs[1][...] = (norm_parts(x)[0] * ins[-1][row : row + 1]).astype(BF)

    return body


def mlp_body(ids, ins, outs, scratch):
    blocks, w = ins[:LOCAL], ins[LOCAL]
    b_ref, gu_ref, hid_ref = outs[:3]
    units = w.shape[1] // 3
    for where, tile in tiles_of(blocks, 256):
        b_ref[where] = tile
        gu = mm(tile, w[:, : 2 * units], 1, 0)
        gu_ref[where] = gu
        hid = (gelu_parts(gu[:, :units])[0] * gu[:, units:]).astype(BF)
        hid_ref[where] = hid
        store_partial(outs[3:], where, mm(hid, w[:, 2 * units :], 1, 1))


def mlp_back_body(ids, ins, outs, scratch):
    blocks, (gu_ref, w) = ins[:LOCAL], ins[LOCAL:]
    dy_ref, dgu_ref = outs[:2]
    units = w.shape[1] // 3
    for where, tile in tiles_of(blocks, 256):
        dy_ref[where] = tile
        dhid = mm(tile, w[:, 2 * units :], 1, 0)
        act, slope = gelu_parts(gu_ref[where, :units])
        dgu_ref[where, :units] = (dhid * gu_ref[where, units:] * slope).astype(BF)
        dgu_ref[where, units:] = (dhid * act).astype(BF)
        store_partial(outs[2:], where, mm(dgu_ref[where], w[:, : 2 * units], 1, 1))


def norm_back_body(row):
    def body(ids, ins, outs, scratch):
        dout = total_of(ins[:TEAM])
        v, dy, gains = ins[TEAM:]
        xhat, rstd = norm_parts(v[...].astype(F32))
        outs[0][...] = jnp.sum(dout * xhat, axis=0, keepdims=True)
        dx = dout * gains[row : row + 1]
        m1 = jnp.mean(dx, axis=-1, keepdims=True)
        m2 = jnp.mean(dx * xhat, axis=-1, keepdims=True)
        dv = dy[...].astype(F32) + rstd * (dx - m1 - xhat * m2)
        outs[1][...] = dv
        if len(outs) > 2:
            outs[2][...] = dv.astype(BF)

    return body


def attn_back_body(windowed, n, sub):
    def body(ids, ins, outs, scratch):
        blocks, (qkv, lo, hi, col, row, w, cos, sin) = ins[:LOCAL], ins[LOCAL:]
        dm_ref, dq_ref, dkv_ref, dlo_ref, dhi_ref = outs
        kb, vb, dctx, dqs, dkb, dvb = scratch
        hc = kb.shape[1]
        for where, tile in tiles_of(blocks, 256):
            dm_ref[where] = tile
            dctx[where] = mm(tile, w[:, 3 * hc :], 1, 0).astype(BF)
        head_of = lax.broadcasted_iota(jnp.int32, (BLK, hc), 1) // HD
        last = BLK + LOCAL * sub
        for mb in range(n):
            fill_band(ids, mb, n, sub, qkv, lo, hi, kb, vb)
            dkb[...] = jnp.zeros(dkb.shape, F32)
            dvb[...] = jnp.zeros(dvb.shape, F32)
            for i in range(LOCAL * sub // BLK):
                ok = allowed_of(mb, i, col, row, windowed)
                q = take(ids, qkv, n, sub, mb, i, slice(0, hc))
                do = take(ids, dctx, n, sub, mb, i, slice(0, hc))
                band = slice(i * BLK, (i + 3) * BLK)
                k, v = kb[band], vb[band]
                dq = jnp.zeros((BLK, hc), F32)
                dk = dkb[band]
                dv = dvb[band]
                for h in range(hc // HD):
                    mine = head_of == h
                    qh = jnp.where(mine, q, jnp.zeros_like(q))
                    doh = jnp.where(mine, do, jnp.zeros_like(do))
                    p = probs_of(qh, k, ok)
                    dp = mm(doh, v, 1, 1)
                    ds = (p * (dp - jnp.sum(p * dp, axis=1, keepdims=True))).astype(BF)
                    dq = jnp.where(mine, mm(ds, k, 1, 0), dq)
                    dk = dk + mm(ds, qh, 0, 0)
                    dv = dv + mm(p.astype(BF), doh, 0, 0)
                put(ids, dqs, n, sub, mb, i, slice(0, hc), 0.125 * dq)
                dkb[band] = dk
                dvb[band] = dv
            edge = slice(mb * BLK, (mb + 1) * BLK)
            dlo_ref[edge, :hc] = (0.125 * dkb[:BLK]).astype(BF)
            dlo_ref[edge, hc:] = dvb[:BLK].astype(BF)
            dhi_ref[edge, :hc] = (0.125 * dkb[last:]).astype(BF)
            dhi_ref[edge, hc:] = dvb[last:].astype(BF)
            for b in range(LOCAL):
                src = slice(BLK + b * sub, BLK + (b + 1) * sub)
                dst = true_rows(ids, n, sub, mb, b)
                dkv_ref[dst, :hc] = 0.125 * dkb[src]
                dkv_ref[dst, hc:] = dvb[src]
        for first in range(0, dqs.shape[0], 256):
            where = slice(first, first + 256)
            g = dqs[where]
            dq_ref[where] = (g * cos[where] + swap_halves(g * sin[where])).astype(BF)

    return body


def qkv_back_body(n, sub):
    def body(ids, ins, outs, scratch):
        dq, dkv, from_next, from_prev, w, cos, sin = ins
        dqkv_ref = outs[0]
        acc = scratch[0]
        hc = w.shape[1] // 4
        acc[...] = dkv[...]
        per = BLK // sub
        for mb in range(n):
            for i in range(per):
                src = slice(mb * BLK + i * sub, mb * BLK + (i + 1) * sub)
                first = true_rows(ids, n, sub, mb, i)
                acc[first] = acc[first] + from_prev[src].astype(F32)
                end = true_rows(ids, n, sub, mb, LOCAL - per + i)
                acc[end] = acc[end] + from_next[src].astype(F32)
        for first in range(0, acc.shape[0], 256):
            where = slice(first, first + 256)
            g = acc[where, :hc]
            dqkv_ref[where, :hc] = dq[where]
            dqkv_ref[where, hc : 2 * hc] = (g * cos[where] + swap_halves(g * sin[where])).astype(BF)
            dqkv_ref[where, 2 * hc :] = acc[where, hc:].astype(BF)
            store_partial(outs[1:], where, mm(dqkv_ref[where], w[:, : 3 * hc], 1, 1))

    return body


def weight_grad_body(ids, ins, outs, scratch):
    full = scratch[0]
    chains = [ins[i : i + 4] for i in range(0, len(ins), 4)]
    cut = chains[0][1].shape[1]
    step = 256
    for first in range(0, full.shape[0], step):
        where = slice(first, first + step)
        full[where, :cut] = sum(mm(c[0][:, where], c[1][...], 0, 0) for c in chains).astype(BF)
        full[where, cut:] = sum(mm(c[2][:, where], c[3][...], 0, 0) for c in chains).astype(BF)
    nz = len(outs)
    span = outs[0].shape[0]
    for s in range(nz):
        outs[s][...] = full[aligned(lax.rem(ids[0] + s, nz) * span, span)]


def plane_sum_body(ids, ins, outs, scratch):
    scratch[0][...] = total_of(ins)
    rows = outs[0].shape[0]
    for k in range(TEAM):
        outs[k][...] = scratch[0][aligned((ids[1] ^ k) * rows, rows)].astype(outs[k].dtype)


def finish_body(ids, ins, outs, scratch):
    g_qkv, g_out, g_in, g_down = outs
    wide = scratch[0]
    layers, hc = g_qkv.shape[0], g_qkv.shape[3] // TEAM
    real, units = g_down.shape[2], wide.shape[1] // TEAM
    for layer in range(layers):
        attn = ins[layer * TEAM : (layer + 1) * TEAM]
        ffn = ins[(layers + layer) * TEAM : (layers + layer + 1) * TEAM]
        for k in range(TEAM):
            cols = aligned((ids[1] ^ k) * hc, hc)
            for i in range(3):
                g_qkv[layer, i, :, cols] = attn[k][:, i * hc : (i + 1) * hc].astype(F32)
            g_out[layer, :, cols] = attn[k][:, 3 * hc :].astype(F32)
        for i in range(3):
            for k in range(TEAM):
                cols = pl.ds(pl.multiple_of((ids[1] ^ k) * units, 128), units)
                wide[:, cols] = ffn[k][:, i * units : (i + 1) * units].astype(F32)
            if i == 2:
                g_down[layer] = wide[:, :real]
            else:
                g_in[layer, i] = wide[:, :real]


def join_body(ids, ins, outs, scratch):
    n, half = outs[0].shape[0], outs[0].shape[1] // 2
    c = ids[2]
    for mb in range(n):
        rows = slice(mb * half, (mb + 1) * half)
        outs[0][mb, aligned(c * half, half)] = ins[0][rows]
        outs[0][mb, aligned((1 - c) * half, half)] = ins[1][rows]


def shards(tokens, cu_seqlens, attn_gain, mlp_gain, w_qkv, w_attn_out, w_ffn_in, w_ffn_out, out_grad):
    nz = lax.axis_size("z")
    z = lax.axis_index("z")
    t = lax.axis_index("y") * 2 + lax.axis_index("x")
    c = lax.axis_index("c")
    ids = jnp.stack([z, t, c]).astype(jnp.int32)
    micro, chip_rows, feat = tokens.shape
    layers, d_rows = w_qkv.shape[0], w_qkv.shape[2]
    hc = w_qkv.shape[3] // TEAM
    sub = chip_rows // 2
    real = w_ffn_in.shape[3]
    units = -(-real // (TEAM * 128)) * 128
    team_rows = TEAM * chip_rows
    per_chain = micro // CHAINS
    n = per_chain
    own = n * sub
    rows = LOCAL * own
    aw, fw = 4 * hc, 3 * units

    started = call(
        "start", start_body, ids,
        [tokens, out_grad, w_qkv, w_attn_out, w_ffn_in, w_ffn_out],
        [out((micro * sub, feat), BF)] * 2
        + [out((d_rows, aw), BF)] * (layers * TEAM)
        + [out((d_rows, fw), BF)] * (layers * TEAM),
        [pltpu.VMEM((d_rows, TEAM * units), BF)],
    )
    tok_own, grad_own = started[:2]
    packs = started[2:]

    def blocks_of(x):
        mine = [x] + [hop_team(x, k) for k in range(1, TEAM)]
        return mine + [hop_core(b) for b in mine]

    def chain_rows(x, i):
        return x[i * own : (i + 1) * own]

    tok_blocks = [blocks_of(chain_rows(tok_own, i)) for i in range(CHAINS)]

    def assemble(pieces, name):
        width = pieces[0].shape[1]
        got = [pieces[0]] + [hop_team(pieces[k], k) for k in range(1, TEAM)]
        plane = call("plane_" + name, plane_body, ids, got, [out((TEAM * d_rows, width), BF)])[0]
        planes = [plane] + [hop_z(plane, s) for s in range(1, nz)]
        return call("full_" + name, full_body, ids, planes, [out((nz * TEAM * d_rows, width), BF)])[0]

    owned = jnp.concatenate([attn_gain, mlp_gain, attn_gain, mlp_gain], axis=0).astype(F32)[: 4 * layers]
    spot = lax.broadcasted_iota(jnp.int32, (1, feat), 1) // d_rows == z * TEAM + t
    gains = jnp.where(spot, jnp.tile(owned, (1, feat // d_rows)), 0.0)
    gains = gains + hop_team(gains, 1)
    gains = gains + hop_team(gains, 2)
    gains = sum([gains] + [hop_z(gains, s) for s in range(1, nz)])

    attn_w, ffn_w = [None] * layers, [None] * layers
    for layer in range(layers):
        attn_w[layer] = assemble(packs[layer * TEAM : (layer + 1) * TEAM], "a" + str(layer))
        ffn_w[layer] = assemble(
            packs[(layers + layer) * TEAM : (layers + layer + 1) * TEAM], "f" + str(layer)
        )
    grad_blocks = [blocks_of(chain_rows(grad_own, i)) for i in range(CHAINS)]

    band_index = z * team_rows - BLK + jnp.arange(team_rows + 2 * BLK, dtype=jnp.int32)
    inside = (band_index >= 0) & (band_index < cu_seqlens[0, -1])
    docs = jnp.sum((band_index[None, :, None] >= cu_seqlens[:, None, 1:-1]).astype(jnp.int32), axis=2)
    docs = jnp.where(inside[None], docs, -1)
    block = jnp.arange(LOCAL, dtype=jnp.int32)
    true_block = ((block % TEAM) ^ t) * 2 + ((block // TEAM) ^ c)
    index = z * team_rows + true_block[:, None] * sub + jnp.arange(sub, dtype=jnp.int32)[None]
    begin = jnp.max(
        jnp.where(
            index[:, None, :, None] >= cu_seqlens[None, :, None, :-1], cu_seqlens[None, :, None, :-1], 0
        ),
        axis=3,
    )
    offsets = (index[:, None] - begin).astype(F32)
    lane = jnp.arange(hc, dtype=jnp.int32) % HD
    sign = jnp.where(lane < HD // 2, -1.0, 1.0)

    state = []
    for i in range(CHAINS):
        mbs = slice(i * n, (i + 1) * n)
        tables = []
        for layer in range(layers):
            base = 10000.0 if layer % 2 == 0 else 160000.0
            inv = base ** (-((lane % (HD // 2)).astype(F32) * 2.0 / HD))
            ang = offsets[:, mbs].reshape(rows, 1) * inv
            tables.append((jnp.cos(ang), jnp.sin(ang) * sign))
        state.append(
            {
                "tables": tables,
                "col": docs[mbs, :, None],
                "row": docs[mbs, None, :],
                "x": chain_rows(tok_own, i),
                "blocks": tok_blocks[i],
                "saved": [],
            }
        )

    partial_out = [out((rows // 2, feat), BF)] * 2
    band = pltpu.VMEM((team_rows + 2 * BLK, hc), BF)
    band32 = pltpu.VMEM((team_rows + 2 * BLK, hc), F32)

    def fold(parts, name):
        got = hop_core(parts[1])
        h = call(
            "fold_" + name, fold_body, ids, [parts[0], got],
            [out((own, feat), F32)] + [out((own, feat), BF)] * (TEAM - 1),
        )
        return [h[0]] + [hop_team(h[k], k) for k in range(1, TEAM)]

    def forward_attn(st, layer):
        windowed = layer % 2 == 0
        w = attn_w[layer]
        cos, sin = st["tables"][layer]
        a, qkv, lo, hi = call(
            "qkv", qkv_body(layer, layer == 0, n, sub), ids, st["blocks"] + [gains, w, cos, sin],
            [out((rows, feat), BF), out((rows, 3 * hc), BF)] + [out((n * BLK, 2 * hc), BF)] * 2,
            flops=2 * rows * feat * 3 * hc,
        )
        lo, hi = step_z(lo, 1), step_z(hi, -1)
        ctx, *parts = call(
            "attn", attn_body(windowed, n, sub), ids, [qkv, lo, hi, st["col"], st["row"], w],
            [out((rows, hc), BF)] + partial_out, [band] * 2, flops=4 * rows * feat * hc,
        )
        terms = fold(parts, "attn")
        mid, b = call(
            "mid", resid_body(layers + layer), ids, [st["x"]] + terms + [gains],
            [out((own, feat), F32), out((own, feat), BF)],
        )
        st["saved"].append([st["x"], a, qkv, lo, hi, ctx, mid])
        st["x"] = mid
        st["blocks"] = blocks_of(b)

    def forward_mlp(st, layer):
        b, gu, hid, *parts = call(
            "mlp", mlp_body, ids, st["blocks"] + [ffn_w[layer]],
            [out((rows, feat), BF), out((rows, 2 * units), F32), out((rows, units), BF)] + partial_out,
            flops=6 * rows * feat * units,
        )
        st["saved"][layer] += [b, gu, hid]
        terms = fold(parts, "mlp")
        if layer + 1 < layers:
            st["x"], a = call(
                "next", resid_body(layer + 1), ids, [st["x"]] + terms + [gains],
                [out((own, feat), F32), out((own, feat), BF)],
            )
            st["blocks"] = blocks_of(a)
        else:
            st["x"] = call("last", resid_body(None), ids, [st["x"]] + terms, [out((own, feat), BF)])[0]

    for layer in range(layers):
        for st in state:
            forward_attn(st, layer)
        for st in state:
            forward_mlp(st, layer)

    def join(parts, dtype):
        x = parts[0] if CHAINS == 1 else jnp.concatenate(parts, axis=0)
        return call("join", join_body, ids, [x, hop_core(x)], [out((micro, chip_rows, feat), dtype)])[0]

    hidden_out = join([st["x"] for st in state], BF)

    for i, st in enumerate(state):
        st["dy"] = chain_rows(grad_own, i)
        st["blocks"] = grad_blocks[i]

    def collect(ins, width, name):
        flops = 2 * rows * CHAINS * feat * width
        pieces = call(
            "wgrad_" + name, weight_grad_body, ids, ins, [out((TEAM * d_rows, width), BF)] * nz,
            [pltpu.VMEM((nz * TEAM * d_rows, width), BF)], flops=flops,
        )
        got = [pieces[0]] + [hop_z(pieces[s], s) for s in range(1, nz)]
        mine = call(
            "zsum_" + name, plane_sum_body, ids, got,
            [out((d_rows, width), F32)] + [out((d_rows, width), BF)] * (TEAM - 1),
            [pltpu.VMEM((TEAM * d_rows, width), F32)],
        )
        return [mine[0]] + [hop_team(mine[k], k) for k in range(1, TEAM)]

    gain_rows = [None] * (2 * layers)

    def backward_mlp(st, layer):
        b, gu, hid = st["saved"][layer][7:]
        dy, dgu, *parts = call(
            "mlp_back", mlp_back_body, ids, st["blocks"] + [gu, ffn_w[layer]],
            [out((rows, feat), BF), out((rows, 2 * units), BF)] + partial_out,
            flops=6 * rows * feat * units,
        )
        terms = fold(parts, "mlp_back")
        dg, dmid, dmb = call(
            "mid_back", norm_back_body(layers + layer), ids, terms + [st["saved"][layer][6], st["dy"], gains],
            [out((1, feat), F32), out((own, feat), F32), out((own, feat), BF)],
        )
        old = gain_rows[layers + layer]
        gain_rows[layers + layer] = dg if old is None else old + dg
        st["dy"] = dmid
        st["blocks"] = blocks_of(dmb)
        return [b, dgu, dy, hid]

    def backward_attn(st, layer):
        windowed = layer % 2 == 0
        w = attn_w[layer]
        cos, sin = st["tables"][layer]
        x_in, a, qkv, lo, hi, ctx = st["saved"][layer][:6]
        dm, dq, dkv, dlo, dhi = call(
            "attn_back", attn_back_body(windowed, n, sub), ids,
            st["blocks"] + [qkv, lo, hi, st["col"], st["row"], w, cos, sin],
            [out((rows, feat), BF), out((rows, hc), BF), out((rows, 2 * hc), F32)]
            + [out((n * BLK, 2 * hc), BF)] * 2,
            [band] * 2 + [pltpu.VMEM((rows, hc), BF), pltpu.VMEM((rows, hc), F32)] + [band32] * 2,
            flops=6 * rows * feat * hc,
        )
        from_next, from_prev = step_z(dlo, -1), step_z(dhi, 1)
        dqkv, *parts = call(
            "qkv_back", qkv_back_body(n, sub), ids, [dq, dkv, from_next, from_prev, w, cos, sin],
            [out((rows, 3 * hc), BF)] + partial_out, [pltpu.VMEM((rows, 2 * hc), F32)],
            flops=6 * rows * feat * hc,
        )
        terms = fold(parts, "qkv_back")
        low = [out((own, feat), BF)] if layer > 0 else []
        dg, st["dy"], *dyb = call(
            "in_back", norm_back_body(layer), ids, terms + [x_in, st["dy"], gains],
            [out((1, feat), F32), out((own, feat), F32)] + low,
        )
        old = gain_rows[layer]
        gain_rows[layer] = dg if old is None else old + dg
        if layer > 0:
            st["blocks"] = blocks_of(dyb[0])
        return [a, dqkv, dm, ctx]

    attn_parts, ffn_parts = [None] * layers, [None] * layers
    for layer in reversed(range(layers)):
        ins = sum([backward_mlp(st, layer) for st in state], [])
        ffn_parts[layer] = collect(ins, fw, "f" + str(layer))
        ins = sum([backward_attn(st, layer) for st in state], [])
        attn_parts[layer] = collect(ins, aw, "a" + str(layer))

    input_grad = join([st["dy"] for st in state], F32)

    dgain = jnp.concatenate(gain_rows + gain_rows, axis=0)[: 4 * layers]
    dgain = dgain + hop_core(dgain)
    dgain = dgain + hop_team(dgain, 1)
    dgain = dgain + hop_team(dgain, 2)
    dgain = sum([dgain] + [hop_z(dgain, s) for s in range(1, nz)])
    dgain = lax.dynamic_slice_in_dim(dgain, (z * TEAM + t) * d_rows, d_rows, axis=1)

    g_qkv, g_out, g_in, g_down = call(
        "finish", finish_body, ids, sum(attn_parts, []) + sum(ffn_parts, []),
        [out(w_qkv.shape, F32), out(w_attn_out.shape, F32), out(w_ffn_in.shape, F32), out(w_ffn_out.shape, F32)],
        [pltpu.VMEM((d_rows, TEAM * units), F32)],
    )
    return (
        hidden_out,
        input_grad,
        dgain[:layers],
        dgain[layers : 2 * layers],
        g_qkv,
        g_out,
        g_in,
        g_down,
    )


def solution(mesh):
    dp, tensor = mesh.devices.shape
    fine = Mesh(mesh.devices.reshape(dp // TEAM, 2, 2, tensor), ("z", "y", "x", "c"))
    rows = ("z", "y", "x")
    in_specs = (
        P(None, rows, None),
        P(),
        P(None, rows),
        P(None, rows),
        P(None, None, rows, "c"),
        P(None, rows, "c"),
        P(None, None, rows, "c"),
        P(None, rows, "c"),
        P(None, rows, None),
    )
    out_specs = (
        P(None, rows, None),
        P(None, rows, None),
        P(None, rows),
        P(None, rows),
        P(None, None, rows, "c"),
        P(None, rows, "c"),
        P(None, None, rows, "c"),
        P(None, rows, "c"),
    )
    return jax.shard_map(shards, mesh=fine, in_specs=in_specs, out_specs=out_specs, check_vma=False)
```

time: 892 us -> 638 us (0.72)
  local copies, waits for them, and re-layouts: 215 us -> 19.6 us
  other arithmetic: 92.8 us -> 7.22 us
  Pallas kernels: 28.8 us -> 105 us
  waiting for transfers between devices: 347 us -> 290 us
  starting transfers between devices: 159 us -> 206 us
  matrix products: 30.1 us -> 0 us
    ppermute x24 -> x30, waiting for transfers between devices: 222 us -> 101 us  [hop_z(): return lax.ppermute(x, 'z', [(i, (i + s) % n) for i in range(n)])]
    pallas_call x4 -> x48, Pallas kernels: 28.8 us -> 105 us  [call(): pl.pallas_call(kernel, name=name, in_specs=[pl.BlockSpec(memory_space=plt...]
    dynamic_update_slice x79 -> x0, local copies, waits for them, and re-layouts: 60.1 us -> none  [the longest x49 31.5 us: columns(): lax.dynamic_update_slice(full, parts[k][:, lo:lo + width], (0, (t ^ k) *...]
    slice x68 -> x1, local copies, waits for them, and re-layouts: 58 us -> 0.58 us  [shards(): dgain[layers:2 * layers]]
    another operation x78 -> x2, local copies, waits for them, and re-layouts: 41.6 us -> 0.09 us  [shards(): gains = jnp.where(spot, jnp.tile(owned, (1, feat // d_rows)), 0.0)]
    dot_general x24 -> x0, matrix products: 30.1 us -> none  [mm(): lax.dot_general(a, b, (((ca,), (cb,)), ((), ())), preferred_element_type=...]
    ppermute x24 -> x30, starting transfers between devices: 45.9 us -> 75.3 us  [hop_z(): return lax.ppermute(x, 'z', [(i, (i + s) % n) for i in range(n)])]
    ppermute x72 -> x76, waiting for transfers between devices: 99.7 us -> 128 us  [hop_team(): return lax.ppermute(x, ('y', 'x'), [(i, i ^ k) for i in range(TEAM)])]
  transfers between devices with their start and end apart: 124 -> 157, of which waited for: 53 -> 65; matrix products, arithmetic and copies ran while one was open for 30% -> 2% of each run, Pallas kernels for 2% -> 9%
where the time goes in v2:
time: 638 us; the launch traced here: 630 us
  waiting for transfers between devices  290 us (45%)
  starting transfers between devices  206 us (32%)
  Pallas kernels  105 us (16%)
  local copies, waits for them, and re-layouts  19.6 us (3%)
  other arithmetic  7.22 us (1%)
    ppermute x76, waiting for transfers between devices, hop_team(): return lax.ppermute(x, ('y', 'x'), [(i, i ^ k) for i in range(TEAM)])  128 us
    pallas_call x48, Pallas kernels, call(): pl.pallas_call(kernel, name=name, in_specs=[pl.BlockSpec(memory_space=plt...  105 us
    ppermute x30, waiting for transfers between devices, hop_z(): return lax.ppermute(x, 'z', [(i, (i + s) % n) for i in range(n)])  101 us
    ppermute x76, starting transfers between devices, hop_team(): return lax.ppermute(x, ('y', 'x'), [(i, i ^ k) for i in range(TEAM)])  93.5 us
    ppermute x30, starting transfers between devices, hop_z(): return lax.ppermute(x, 'z', [(i, (i + s) % n) for i in range(n)])  75.3 us
    ppermute x8, waiting for transfers between devices, step_z(): lax.ppermute(x, 'z', [(i, i + by) for i in range(n) if 0 <= i + by < n])  45.5 us
    ppermute x8, starting transfers between devices, step_z(): lax.ppermute(x, 'z', [(i, i + by) for i in range(n) if 0 <= i + by < n])  30.2 us
    unnamed x86, local copies, waits for them, and re-layouts  16.3 us
  transfers between devices with their start and end apart: 157, of which 65 were waited for; matrix products, arithmetic and copies ran while one was open for 2% of the time, Pallas kernels for 9%

profile of v2, /device:TPU:0, one launch (start us, length us, event | category | flops | bytes accessed | tf_op | source)
XLA Modules:
  0.0 630.4 jit_solution(17247096088349964826)
XLA Ops:
  39.8 12.6 %collective-permute-done.16.refs_3_ = bf16[256,512]{1,0:T(8,128)(2,1)S(1)} collective-permute-done((bf16[256,512]{1,0:T(8,128)(2,1)S(1)}, bf16[256,512]{1,0:T(8,128)(2,1)S(1)}, u32[]{:S(2)}, u32[]{:S(2)}) %collective-permute-start.16) | collective-permute-done | bytes 262176 | tf_op jit(solution)/shard_map/ppermute | solution.py:34
  65.7 6.8 %attn.2 = (bf16[1024,128]{1,0:T(8,128)(2,1)S(1)}, bf16[512,1024]{1,0:T(8,128)(2,1)S(1)}, bf16[512,1024]{1,0:T(8,128)(2,1)S(1)}) custom-call(s32[3]{0:T(128)S(1)} %pad_add_fusion.refs_0_, bf16[1024,384]{1,0:T(8,128)(2,1)S(1)} %get-tuple-element.164.refs_1_.refs_9_, bf16[256,256]{1,0:T(8,128)(2,1)S(1)} %collective-permute-done.18.refs_2_.refs_10_, ...), custom_call_target="tpu_custom_call" | custom-call | flops 536870912 | bytes 4468736 | tf_op jit(solution)/shard_map/attn/pallas_call | solution.py:55
  90.8 5.8 collective-permute-done.21.refs_3_
  104.8 32.5 %collective-permute-done.35.refs_3_ = bf16[256,1152]{1,0:T(8,128)(2,1)S(1)} collective-permute-done((bf16[256,1152]{1,0:T(8,128)(2,1)S(1)}, bf16[256,1152]{1,0:T(8,128)(2,1)S(1)}, u32[]{:S(2)}, u32[]{:S(2)}) %collective-permute-start.35) | collective-permute-done | bytes 589856 | tf_op jit(solution)/shard_map/ppermute | solution.py:34
  153.9 9.9 %collective-permute-done.48.refs_2_ = bf16[64,512]{1,0:T(8,128)(2,1)S(1)} collective-permute-done((bf16[64,512]{1,0:T(8,128)(2,1)S(1)}, bf16[64,512]{1,0:T(8,128)(2,1)S(1)}, u32[]{:S(2)}, u32[]{:S(2)}) %collective-permute-start.48) | collective-permute-done | bytes 65568 | tf_op jit(solution)/shard_map/ppermute | solution.py:25
  177.9 10.2 %collective-permute-start.51 = (bf16[256,512]{1,0:T(8,128)(2,1)S(1)}, bf16[256,512]{1,0:T(8,128)(2,1)S(1)}, u32[]{:S(2)}, u32[]{:S(2)}) collective-permute-start(bf16[256,512]{1,0:T(8,128)(2,1)S(1)} %plane_a1.1.refs_1_), channel_id=1, source_target_pairs={{0,8},{8,16},{16,24},{24,0},{1,9},{9,17},{17,25},{25,1},{2,10},{10... | collective-permute-start | bytes 786440 | tf_op jit(solution)/shard_map/ppermute | solution.py:34
  201.5 4.4 collective-permute-done.55.refs_3_.refs_11_
  205.9 6.8 %attn.3 = (bf16[1024,128]{1,0:T(8,128)(2,1)S(1)}, bf16[512,1024]{1,0:T(8,128)(2,1)S(1)}, bf16[512,1024]{1,0:T(8,128)(2,1)S(1)}) custom-call(s32[3]{0:T(128)S(1)} %pad_add_fusion.refs_0_, bf16[1024,384]{1,0:T(8,128)(2,1)S(1)} %get-tuple-element.191.refs_1_.refs_9_, bf16[256,256]{1,0:T(8,128)(2,1)S(1)} %collective-permute-done.54.refs_2_.refs_10_, ...), custom_call_target="tpu_custom_call" | custom-call | flops 536870912 | bytes 4468736 | tf_op jit(solution)/shard_map/attn/pallas_call | solution.py:55
  219.5 8.3 %collective-permute-done.68.refs_3_ = bf16[64,1152]{1,0:T(8,128)(2,1)S(1)} collective-permute-done((bf16[64,1152]{1,0:T(8,128)(2,1)S(1)}, bf16[64,1152]{1,0:T(8,128)(2,1)S(1)}, u32[]{:S(2)}, u32[]{:S(2)}) %collective-permute-start.68) | collective-permute-done | bytes 147488 | tf_op jit(solution)/shard_map/ppermute | solution.py:25
  237.3 4.5 collective-permute-done.58.refs_4_
  243.6 9.3 %collective-permute-start.70 = (bf16[256,1152]{1,0:T(8,128)(2,1)S(1)}, bf16[256,1152]{1,0:T(8,128)(2,1)S(1)}, u32[]{:S(2)}, u32[]{:S(2)}) collective-permute-start(bf16[256,1152]{1,0:T(8,128)(2,1)S(1)} %plane_f1.1.refs_1_), channel_id=1, source_target_pairs={{0,8},{8,16},{16,24},{24,0},{1,9},{9,17},{17,25},{25,1},{2,10},{10... | collective-permute-start | bytes 1769480 | tf_op jit(solution)/shard_map/ppermute | solution.py:34
  257.4 17.8 %collective-permute-done.71.refs_3_ = bf16[256,1152]{1,0:T(8,128)(2,1)S(1)} collective-permute-done((bf16[256,1152]{1,0:T(8,128)(2,1)S(1)}, bf16[256,1152]{1,0:T(8,128)(2,1)S(1)}, u32[]{:S(2)}, u32[]{:S(2)}) %collective-permute-start.71) | collective-permute-done | bytes 589856 | tf_op jit(solution)/shard_map/ppermute | solution.py:34
  298.9 5.6 collective-permute-done.86.refs_2_
  304.5 6.4 %collective-permute-done.87.refs_3_ = bf16[128,1024]{1,0:T(8,128)(2,1)S(1)} collective-permute-done((bf16[128,1024]{1,0:T(8,128)(2,1)S(1)}, bf16[128,1024]{1,0:T(8,128)(2,1)S(1)}, u32[]{:S(2)}, u32[]{:S(2)}) %collective-permute-start.87) | collective-permute-done | bytes 262176 | tf_op jit(solution)/shard_map/ppermute | solution.py:25
  315.5 6.7 %collective-permute-done.91.refs_4_ = bf16[128,1024]{1,0:T(8,128)(2,1)S(1)} collective-permute-done((bf16[128,1024]{1,0:T(8,128)(2,1)S(1)}, bf16[128,1024]{1,0:T(8,128)(2,1)S(1)}, u32[]{:S(2)}, u32[]{:S(2)}) %collective-permute-start.91) | collective-permute-done | bytes 262176 | tf_op jit(solution)/shard_map/ppermute | solution.py:25
  328.0 10.5 %attn_back.2 = (bf16[1024,1024]{1,0:T(8,128)(2,1)S(1)}, bf16[1024,128]{1,0:T(8,128)(2,1)S(1)}, f32[1024,256]{1,0:T(8,128)S(1)}, bf16[256,256]{1,0:T(8,128)(2,1)S(1)}, bf16[256,256]{1,0:T(8,128)(2,1)S(1)}) custom-call(s32[3]{0:T(128)S(1)} %pad_add_fusion.refs_0_, bf16[128,1024]{1,0:T(8,128)(2,1)S(1)} %get-tuple-element.220.refs_1_, ...), custom_call_target="tpu_custom_call" | custom-call | flops 805306368 | bytes 8925184 | tf_op jit(solution)/shard_map/attn_back/pallas_call | solution.py:55
  339.8 4.6 collective-permute-start.97
  356.2 5.7 collective-permute-done.99.refs_2_
  361.9 4.9 collective-permute-done.100.refs_3_
  371.4 6.7 %collective-permute-done.104.refs_4_ = bf16[128,1024]{1,0:T(8,128)(2,1)S(1)} collective-permute-done((bf16[128,1024]{1,0:T(8,128)(2,1)S(1)}, bf16[128,1024]{1,0:T(8,128)(2,1)S(1)}, u32[]{:S(2)}, u32[]{:S(2)}) %collective-permute-start.104) | collective-permute-done | bytes 262176 | tf_op jit(solution)/shard_map/ppermute | solution.py:25
  394.9 5.7 collective-permute-done.110.refs_2_
  400.6 6.1 collective-permute-done.111.refs_3_
  411.8 6.2 collective-permute-done.115.refs_4_
  431.4 10.1 %attn_back.3 = (bf16[1024,1024]{1,0:T(8,128)(2,1)S(1)}, bf16[1024,128]{1,0:T(8,128)(2,1)S(1)}, f32[1024,256]{1,0:T(8,128)S(1)}, bf16[256,256]{1,0:T(8,128)(2,1)S(1)}, bf16[256,256]{1,0:T(8,128)(2,1)S(1)}) custom-call(s32[3]{0:T(128)S(1)} %pad_add_fusion.refs_0_, bf16[128,1024]{1,0:T(8,128)(2,1)S(1)} %get-tuple-element.241.refs_1_, ...), custom_call_target="tpu_custom_call" | custom-call | flops 805306368 | bytes 8925184 | tf_op jit(solution)/shard_map/attn_back/pallas_call | solution.py:55
  442.8 28.5 %collective-permute-done.120.refs_3_ = bf16[256,256]{1,0:T(8,128)(2,1)S(1)} collective-permute-done((bf16[256,256]{1,0:T(8,128)(2,1)S(1)}, bf16[256,256]{1,0:T(8,128)(2,1)S(1)}, u32[]{:S(2)}, u32[]{:S(2)}) %collective-permute-start.120) | collective-permute-done | bytes 131104 | tf_op jit(solution)/shard_map/ppermute | solution.py:39
  471.2 15.2 %collective-permute-start.121 = (bf16[256,256]{1,0:T(8,128)(2,1)S(1)}, bf16[256,256]{1,0:T(8,128)(2,1)S(1)}, u32[]{:S(2)}, u32[]{:S(2)}) collective-permute-start(bf16[256,256]{1,0:T(8,128)(2,1)S(1)} %get-tuple-element.245), channel_id=1, source_target_pairs={{0,8},{8,16},{16,24},{1,9},{9,17},{17,25},{2,10},{10,18},{18,26},{... | collective-permute-start | bytes 393224 | tf_op jit(solution)/shard_map/ppermute | solution.py:39
  497.5 7.1 %collective-permute-done.154.refs_14_ = bf16[64,1152]{1,0:T(8,128)(2,1)S(1)} collective-permute-done((bf16[64,1152]{1,0:T(8,128)(2,1)S(1)}, bf16[64,1152]{1,0:T(8,128)(2,1)S(1)}, u32[]{:S(2)}, u32[]{:S(2)}) %collective-permute-start.154) | collective-permute-done | bytes 147488 | tf_op jit(solution)/shard_map/ppermute | solution.py:25
  512.6 4.7 wgrad_f0.1
  526.7 18.5 %collective-permute-done.140.refs_3_ = bf16[256,512]{1,0:T(8,128)(2,1)S(1)} collective-permute-done((bf16[256,512]{1,0:T(8,128)(2,1)S(1)}, bf16[256,512]{1,0:T(8,128)(2,1)S(1)}, u32[]{:S(2)}, u32[]{:S(2)}) %collective-permute-start.140) | collective-permute-done | bytes 262176 | tf_op jit(solution)/shard_map/ppermute | solution.py:34
  565.4 8.4 %collective-permute-done.146.refs_3_ = bf16[256,1152]{1,0:T(8,128)(2,1)S(1)} collective-permute-done((bf16[256,1152]{1,0:T(8,128)(2,1)S(1)}, bf16[256,1152]{1,0:T(8,128)(2,1)S(1)}, u32[]{:S(2)}, u32[]{:S(2)}) %collective-permute-start.146) | collective-permute-done | bytes 589856 | tf_op jit(solution)/shard_map/ppermute | solution.py:34
  573.8 12.5 %collective-permute-start.133 = (bf16[256,512]{1,0:T(8,128)(2,1)}, bf16[256,512]{1,0:T(8,128)(2,1)}, u32[]{:S(2)}, u32[]{:S(2)}) collective-permute-start(bf16[256,512]{1,0:T(8,128)(2,1)} %get-tuple-element.263), channel_id=1, source_target_pairs={{0,8},{8,16},{16,24},{24,0},{1,9},{9,17},{17,25},{25,1},{2,10},{10... | collective-permute-start | bytes 786440 | tf_op jit(solution)/shard_map/ppermute | solution.py:34
  613.7 6.6 %collective-permute-start.132 = (f32[8,1024]{1,0:T(8,128)}, f32[8,1024]{1,0:T(8,128)S(1)}, u32[]{:S(2)}, u32[]{:S(2)}) collective-permute-start(f32[8,1024]{1,0:T(8,128)} %add.175), channel_id=1, source_target_pairs={{0,24},{8,0},{16,8},{24,16},{1,25},{9,1},{17,9},{25,17},{2,26},{10... | collective-permute-start | bytes 98312 | tf_op jit(solution)/shard_map/ppermute | solution.py:34
  (449 shorter events, 319.2 us)
Async XLA Ops:
  32.3 20.0 %collective-permute-start.16 = (bf16[256,512]{1,0:T(8,128)(2,1)S(1)}, bf16[256,512]{1,0:T(8,128)(2,1)S(1)}, u32[]{:S(2)}, u32[]{:S(2)}) collective-permute-start(bf16[256,512]{1,0:T(8,128)(2,1)S(1)} %plane_a0.1.refs_1_), channel_id=1, source_target_pairs={{0,16},{8,24},{16,0},{24,8},{1,17},{9,25},{17,1},{25,9},{2,18},{10... | collective-permute-start | bytes 786440 | tf_op jit(solution)/shard_map/ppermute | solution.py:34
  83.7 20.7 %collective-permute-start.36 = (bf16[256,1152]{1,0:T(8,128)(2,1)S(1)}, bf16[256,1152]{1,0:T(8,128)(2,1)S(1)}, u32[]{:S(2)}, u32[]{:S(2)}) collective-permute-start(bf16[256,1152]{1,0:T(8,128)(2,1)S(1)} %plane_f0.1.refs_1_), channel_id=1, source_target_pairs={{0,24},{8,0},{16,8},{24,16},{1,25},{9,1},{17,9},{25,17},{2,26},{10... | collective-permute-start | bytes 1769480 | tf_op jit(solution)/shard_map/ppermute | solution.py:34
  83.8 53.5 %collective-permute-start.35 = (bf16[256,1152]{1,0:T(8,128)(2,1)S(1)}, bf16[256,1152]{1,0:T(8,128)(2,1)S(1)}, u32[]{:S(2)}, u32[]{:S(2)}) collective-permute-start(bf16[256,1152]{1,0:T(8,128)(2,1)S(1)} %plane_f0.1.refs_1_), channel_id=1, source_target_pairs={{0,16},{8,24},{16,0},{24,8},{1,17},{9,25},{17,1},{25,9},{2,18},{10... | collective-permute-start | bytes 1769480 | tf_op jit(solution)/shard_map/ppermute | solution.py:34
  96.6 41.7 %collective-permute-start.34 = (bf16[256,1152]{1,0:T(8,128)(2,1)S(1)}, bf16[256,1152]{1,0:T(8,128)(2,1)S(1)}, u32[]{:S(2)}, u32[]{:S(2)}) collective-permute-start(bf16[256,1152]{1,0:T(8,128)(2,1)S(1)} %plane_f0.1.refs_1_), channel_id=1, source_target_pairs={{0,8},{8,16},{16,24},{24,0},{1,9},{9,17},{17,25},{25,1},{2,10},{10... | collective-permute-start | bytes 1769480 | tf_op jit(solution)/shard_map/ppermute | solution.py:34
  101.2 36.1 %collective-permute-start.26 = (bf16[128,1024]{1,0:T(8,128)(2,1)S(1)}, bf16[128,1024]{1,0:T(8,128)(2,1)S(1)}, u32[]{:S(2)}, u32[]{:S(2)}) collective-permute-start(bf16[128,1024]{1,0:T(8,128)(2,1)S(1)} %get-tuple-element.174.refs_1_), channel_id=1, source_target_pairs={{0,6},{2,4},{4,2},{6,0},{1,7},{3,5},{5,3},{7,1},{8,14},{10,12},{12... | collective-permute-start | bytes 786440 | tf_op jit(solution)/shard_map/ppermute | solution.py:25
  102.8 35.0 %collective-permute-start.25 = (bf16[128,1024]{1,0:T(8,128)(2,1)S(1)}, bf16[128,1024]{1,0:T(8,128)(2,1)S(1)}, u32[]{:S(2)}, u32[]{:S(2)}) collective-permute-start(bf16[128,1024]{1,0:T(8,128)(2,1)S(1)} %get-tuple-element.174.refs_1_), channel_id=1, source_target_pairs={{0,4},{2,6},{4,0},{6,2},{1,5},{3,7},{5,1},{7,3},{8,12},{10,14},{12... | collective-permute-start | bytes 786440 | tf_op jit(solution)/shard_map/ppermute | solution.py:25
  104.4 33.4 %collective-permute-start.24 = (bf16[128,1024]{1,0:T(8,128)(2,1)S(1)}, bf16[128,1024]{1,0:T(8,128)(2,1)S(1)}, u32[]{:S(2)}, u32[]{:S(2)}) collective-permute-start(bf16[128,1024]{1,0:T(8,128)(2,1)S(1)} %get-tuple-element.174.refs_1_), channel_id=1, source_target_pairs={{0,2},{2,0},{4,6},{6,4},{1,3},{3,1},{5,7},{7,5},{8,10},{10,8},{12,... | collective-permute-start | bytes 786440 | tf_op jit(solution)/shard_map/ppermute | solution.py:25
  148.3 21.4 %collective-permute-start.38 = (bf16[128,1024]{1,0:T(8,128)(2,1)S(1)}, bf16[128,1024]{1,0:T(8,128)(2,1)S(1)}, u32[]{:S(2)}, u32[]{:S(2)}) collective-permute-start(bf16[128,1024]{1,0:T(8,128)(2,1)S(1)} %get-tuple-element.182), channel_id=1, source_target_pairs={{0,2},{2,0},{4,6},{6,4},{1,3},{3,1},{5,7},{7,5},{8,10},{10,8},{12,... | collective-permute-start | bytes 786440 | tf_op jit(solution)/shard_map/ppermute | solution.py:25
  148.7 21.0 %collective-permute-start.39 = (bf16[128,1024]{1,0:T(8,128)(2,1)S(1)}, bf16[128,1024]{1,0:T(8,128)(2,1)S(1)}, u32[]{:S(2)}, u32[]{:S(2)}) collective-permute-start(bf16[128,1024]{1,0:T(8,128)(2,1)S(1)} %get-tuple-element.183), channel_id=1, source_target_pairs={{0,4},{2,6},{4,0},{6,2},{1,5},{3,7},{5,1},{7,3},{8,12},{10,14},{12... | collective-permute-start | bytes 786440 | tf_op jit(solution)/shard_map/ppermute | solution.py:25
  169.6 21.0 %collective-permute-start.52 = (bf16[256,512]{1,0:T(8,128)(2,1)S(1)}, bf16[256,512]{1,0:T(8,128)(2,1)S(1)}, u32[]{:S(2)}, u32[]{:S(2)}) collective-permute-start(bf16[256,512]{1,0:T(8,128)(2,1)S(1)} %plane_a1.1.refs_1_), channel_id=1, source_target_pairs={{0,16},{8,24},{16,0},{24,8},{1,17},{9,25},{17,1},{25,9},{2,18},{10... | collective-permute-start | bytes 786440 | tf_op jit(solution)/shard_map/ppermute | solution.py:34
  170.6 20.1 %collective-permute-start.43 = (bf16[128,1024]{1,0:T(8,128)(2,1)S(1)}, bf16[128,1024]{1,0:T(8,128)(2,1)S(1)}, u32[]{:S(2)}, u32[]{:S(2)}) collective-permute-start(bf16[128,1024]{1,0:T(8,128)(2,1)S(1)} %get-tuple-element.186.refs_1_), channel_id=1, source_target_pairs={{0,6},{2,4},{4,2},{6,0},{1,7},{3,5},{5,3},{7,1},{8,14},{10,12},{12... | collective-permute-start | bytes 786440 | tf_op jit(solution)/shard_map/ppermute | solution.py:25
  228.4 27.4 %collective-permute-start.72 = (bf16[256,1152]{1,0:T(8,128)(2,1)S(1)}, bf16[256,1152]{1,0:T(8,128)(2,1)S(1)}, u32[]{:S(2)}, u32[]{:S(2)}) collective-permute-start(bf16[256,1152]{1,0:T(8,128)(2,1)S(1)} %plane_f1.1.refs_1_), channel_id=1, source_target_pairs={{0,24},{8,0},{16,8},{24,16},{1,25},{9,1},{17,9},{25,17},{2,26},{10... | collective-permute-start | bytes 1769480 | tf_op jit(solution)/shard_map/ppermute | solution.py:34
  232.8 42.3 %collective-permute-start.71 = (bf16[256,1152]{1,0:T(8,128)(2,1)S(1)}, bf16[256,1152]{1,0:T(8,128)(2,1)S(1)}, u32[]{:S(2)}, u32[]{:S(2)}) collective-permute-start(bf16[256,1152]{1,0:T(8,128)(2,1)S(1)} %plane_f1.1.refs_1_), channel_id=1, source_target_pairs={{0,16},{8,24},{16,0},{24,8},{1,17},{9,25},{17,1},{25,9},{2,18},{10... | collective-permute-start | bytes 1769480 | tf_op jit(solution)/shard_map/ppermute | solution.py:34
  243.6 32.5 %collective-permute-start.70 = (bf16[256,1152]{1,0:T(8,128)(2,1)S(1)}, bf16[256,1152]{1,0:T(8,128)(2,1)S(1)}, u32[]{:S(2)}, u32[]{:S(2)}) collective-permute-start(bf16[256,1152]{1,0:T(8,128)(2,1)S(1)} %plane_f1.1.refs_1_), channel_id=1, source_target_pairs={{0,8},{8,16},{16,24},{24,0},{1,9},{9,17},{17,25},{25,1},{2,10},{10... | collective-permute-start | bytes 1769480 | tf_op jit(solution)/shard_map/ppermute | solution.py:34
  253.8 21.3 %collective-permute-start.62 = (bf16[128,1024]{1,0:T(8,128)(2,1)S(1)}, bf16[128,1024]{1,0:T(8,128)(2,1)S(1)}, u32[]{:S(2)}, u32[]{:S(2)}) collective-permute-start(bf16[128,1024]{1,0:T(8,128)(2,1)S(1)} %get-tuple-element.201.refs_1_), channel_id=1, source_target_pairs={{0,6},{2,4},{4,2},{6,0},{1,7},{3,5},{5,3},{7,1},{8,14},{10,12},{12... | collective-permute-start | bytes 786440 | tf_op jit(solution)/shard_map/ppermute | solution.py:25
  411.3 80.2 %collective-permute-start.73 = (bf16[512,1024]{1,0:T(8,128)(2,1)S(1)}, bf16[512,1024]{1,0:T(8,128)(2,1)S(1)}, u32[]{:S(2)}, u32[]{:S(2)}) collective-permute-start(bf16[512,1024]{1,0:T(8,128)(2,1)S(1)} %get-tuple-element.207), channel_id=1, source_target_pairs={{0,1},{1,0},{2,3},{3,2},{4,5},{5,4},{6,7},{7,6},{8,9},{9,8},{10,11... | collective-permute-start | bytes 3145736 | tf_op jit(solution)/shard_map/ppermute | solution.py:29
  426.1 66.8 %collective-permute-start.151 = (bf16[256,1152]{1,0:T(8,128)(2,1)S(1)}, bf16[256,1152]{1,0:T(8,128)(2,1)S(1)}, u32[]{:S(2)}, u32[]{:S(2)}) collective-permute-start(bf16[256,1152]{1,0:T(8,128)(2,1)S(1)} %get-tuple-element.299), channel_id=1, source_target_pairs={{0,8},{8,16},{16,24},{24,0},{1,9},{9,17},{17,25},{25,1},{2,10},{10... | collective-permute-start | bytes 1769480 | tf_op jit(solution)/shard_map/ppermute | solution.py:34
  428.6 64.3 %collective-permute-start.152 = (bf16[256,1152]{1,0:T(8,128)(2,1)S(1)}, bf16[256,1152]{1,0:T(8,128)(2,1)S(1)}, u32[]{:S(2)}, u32[]{:S(2)}) collective-permute-start(bf16[256,1152]{1,0:T(8,128)(2,1)S(1)} %get-tuple-element.300), channel_id=1, source_target_pairs={{0,16},{8,24},{16,0},{24,8},{1,17},{9,25},{17,1},{25,9},{2,18},{10... | collective-permute-start | bytes 1769480 | tf_op jit(solution)/shard_map/ppermute | solution.py:34
  428.6 64.3 %collective-permute-start.153 = (bf16[256,1152]{1,0:T(8,128)(2,1)S(1)}, bf16[256,1152]{1,0:T(8,128)(2,1)S(1)}, u32[]{:S(2)}, u32[]{:S(2)}) collective-permute-start(bf16[256,1152]{1,0:T(8,128)(2,1)S(1)} %get-tuple-element.301), channel_id=1, source_target_pairs={{0,24},{8,0},{16,8},{24,16},{1,25},{9,1},{17,9},{25,17},{2,26},{10... | collective-permute-start | bytes 1769480 | tf_op jit(solution)/shard_map/ppermute | solution.py:34
  441.5 29.8 %collective-permute-start.120 = (bf16[256,256]{1,0:T(8,128)(2,1)S(1)}, bf16[256,256]{1,0:T(8,128)(2,1)S(1)}, u32[]{:S(2)}, u32[]{:S(2)}) collective-permute-start(bf16[256,256]{1,0:T(8,128)(2,1)S(1)} %get-tuple-element.244), channel_id=1, source_target_pairs={{8,0},{16,8},{24,16},{9,1},{17,9},{25,17},{10,2},{18,10},{26,18},{... | collective-permute-start | bytes 393224 | tf_op jit(solution)/shard_map/ppermute | solution.py:39
  491.4 57.7 %collective-permute-start.122 = (bf16[512,1024]{1,0:T(8,128)(2,1)S(1)}, bf16[512,1024]{1,0:T(8,128)(2,1)S(1)}, u32[]{:S(2)}, u32[]{:S(2)}) collective-permute-start(bf16[512,1024]{1,0:T(8,128)(2,1)S(1)} %get-tuple-element.247), channel_id=1, source_target_pairs={{0,1},{1,0},{2,3},{3,2},{4,5},{5,4},{6,7},{7,6},{8,9},{9,8},{10,11... | collective-permute-start | bytes 3145736 | tf_op jit(solution)/shard_map/ppermute | solution.py:29
  492.3 20.4 %collective-permute-start.74 = (bf16[128,1024]{1,0:T(8,128)(2,1)S(1)}, bf16[128,1024]{1,0:T(8,128)(2,1)S(1)}, u32[]{:S(2)}, u32[]{:S(2)}) collective-permute-start(bf16[128,1024]{1,0:T(8,128)(2,1)S(1)} %get-tuple-element.209), channel_id=1, source_target_pairs={{0,2},{2,0},{4,6},{6,4},{1,3},{3,1},{5,7},{7,5},{8,10},{10,8},{12,... | collective-permute-start | bytes 786440 | tf_op jit(solution)/shard_map/ppermute | solution.py:25
  512.6 32.6 %collective-permute-start.140 = (bf16[256,512]{1,0:T(8,128)(2,1)S(1)}, bf16[256,512]{1,0:T(8,128)(2,1)S(1)}, u32[]{:S(2)}, u32[]{:S(2)}) collective-permute-start(bf16[256,512]{1,0:T(8,128)(2,1)S(1)} %get-tuple-element.276), channel_id=1, source_target_pairs={{0,16},{8,24},{16,0},{24,8},{1,17},{9,25},{17,1},{25,9},{2,18},{10... | collective-permute-start | bytes 786440 | tf_op jit(solution)/shard_map/ppermute | solution.py:34
  518.6 41.8 %collective-permute-start.145 = (bf16[256,1152]{1,0:T(8,128)(2,1)S(1)}, bf16[256,1152]{1,0:T(8,128)(2,1)S(1)}, u32[]{:S(2)}, u32[]{:S(2)}) collective-permute-start(bf16[256,1152]{1,0:T(8,128)(2,1)S(1)} %get-tuple-element.287), channel_id=1, source_target_pairs={{0,8},{8,16},{16,24},{24,0},{1,9},{9,17},{17,25},{25,1},{2,10},{10... | collective-permute-start | bytes 1769480 | tf_op jit(solution)/shard_map/ppermute | solution.py:34
  521.1 25.2 %collective-permute-start.141 = (bf16[256,512]{1,0:T(8,128)(2,1)S(1)}, bf16[256,512]{1,0:T(8,128)(2,1)S(1)}, u32[]{:S(2)}, u32[]{:S(2)}) collective-permute-start(bf16[256,512]{1,0:T(8,128)(2,1)S(1)} %get-tuple-element.277), channel_id=1, source_target_pairs={{0,24},{8,0},{16,8},{24,16},{1,25},{9,1},{17,9},{25,17},{2,26},{10... | collective-permute-start | bytes 786440 | tf_op jit(solution)/shard_map/ppermute | solution.py:34
  522.4 51.4 %collective-permute-start.146 = (bf16[256,1152]{1,0:T(8,128)(2,1)S(1)}, bf16[256,1152]{1,0:T(8,128)(2,1)S(1)}, u32[]{:S(2)}, u32[]{:S(2)}) collective-permute-start(bf16[256,1152]{1,0:T(8,128)(2,1)S(1)} %get-tuple-element.288), channel_id=1, source_target_pairs={{0,16},{8,24},{16,0},{24,8},{1,17},{9,25},{17,1},{25,9},{2,18},{10... | collective-permute-start | bytes 1769480 | tf_op jit(solution)/shard_map/ppermute | solution.py:34
  546.3 48.1 %collective-permute-start.147 = (bf16[256,1152]{1,0:T(8,128)(2,1)}, bf16[256,1152]{1,0:T(8,128)(2,1)S(1)}, u32[]{:S(2)}, u32[]{:S(2)}) collective-permute-start(bf16[256,1152]{1,0:T(8,128)(2,1)} %get-tuple-element.289), channel_id=1, source_target_pairs={{0,24},{8,0},{16,8},{24,16},{1,25},{9,1},{17,9},{25,17},{2,26},{10... | collective-permute-start | bytes 1769480 | tf_op jit(solution)/shard_map/ppermute | solution.py:34
  551.4 34.9 %collective-permute-start.123 = (bf16[128,1024]{1,0:T(8,128)(2,1)S(1)}, bf16[128,1024]{1,0:T(8,128)(2,1)S(1)}, u32[]{:S(2)}, u32[]{:S(2)}) collective-permute-start(bf16[128,1024]{1,0:T(8,128)(2,1)S(1)} %get-tuple-element.249), channel_id=1, source_target_pairs={{0,2},{2,0},{4,6},{6,4},{1,3},{3,1},{5,7},{7,5},{8,10},{10,8},{12,... | collective-permute-start | bytes 786440 | tf_op jit(solution)/shard_map/ppermute | solution.py:25
  558.6 31.1 %collective-permute-start.124 = (bf16[128,1024]{1,0:T(8,128)(2,1)S(1)}, bf16[128,1024]{1,0:T(8,128)(2,1)S(1)}, u32[]{:S(2)}, u32[]{:S(2)}) collective-permute-start(bf16[128,1024]{1,0:T(8,128)(2,1)S(1)} %get-tuple-element.250), channel_id=1, source_target_pairs={{0,4},{2,6},{4,0},{6,2},{1,5},{3,7},{5,1},{7,3},{8,12},{10,14},{12... | collective-permute-start | bytes 786440 | tf_op jit(solution)/shard_map/ppermute | solution.py:25
  560.4 29.3 %collective-permute-start.125 = (bf16[128,1024]{1,0:T(8,128)(2,1)S(1)}, bf16[128,1024]{1,0:T(8,128)(2,1)S(1)}, u32[]{:S(2)}, u32[]{:S(2)}) collective-permute-start(bf16[128,1024]{1,0:T(8,128)(2,1)S(1)} %get-tuple-element.251), channel_id=1, source_target_pairs={{0,6},{2,4},{4,2},{6,0},{1,7},{3,5},{5,3},{7,1},{8,14},{10,12},{12... | collective-permute-start | bytes 786440 | tf_op jit(solution)/shard_map/ppermute | solution.py:25
  573.8 24.6 %collective-permute-start.133 = (bf16[256,512]{1,0:T(8,128)(2,1)}, bf16[256,512]{1,0:T(8,128)(2,1)}, u32[]{:S(2)}, u32[]{:S(2)}) collective-permute-start(bf16[256,512]{1,0:T(8,128)(2,1)} %get-tuple-element.263), channel_id=1, source_target_pairs={{0,8},{8,16},{16,24},{24,0},{1,9},{9,17},{17,25},{25,1},{2,10},{10... | collective-permute-start | bytes 786440 | tf_op jit(solution)/shard_map/ppermute | solution.py:34
  603.6 25.0 %collective-permute-start.126 = (f32[128,1024]{1,0:T(8,128)S(1)}, f32[128,1024]{1,0:T(8,128)S(1)}, u32[]{:S(2)}, u32[]{:S(2)}) collective-permute-start(f32[128,1024]{1,0:T(8,128)S(1)} %get-tuple-element.253.refs_1_), channel_id=1, source_target_pairs={{0,1},{1,0},{2,3},{3,2},{4,5},{5,4},{6,7},{7,6},{8,9},{9,8},{10,11... | collective-permute-start | bytes 1572872 | tf_op jit(solution)/shard_map/ppermute | solution.py:29
  (168 other events, 1716.6 us)

commit v3 on v2

--- a/solution.py
+++ b/solution.py
@@ -31,7 +31,7 @@
 
 def hop_z(x, s):
     n = lax.axis_size("z")
-    return lax.ppermute(x, "z", [(i, (i + s) % n) for i in range(n)])
+    return lax.ppermute(x, "z", [(i, i ^ s if n == 4 else (i + s) % n) for i in range(n)])
 
 
 def step_z(x, by):
@@ -43,25 +43,30 @@
     return jax.ShapeDtypeStruct(shape, dtype)
 
 
-def call(name, body, ids, ins, outs, scratch=(), flops=0):
+def call(name, body, ids, ins, outs, scratch=(), flops=0, after=()):
+    ins, after = list(ins), list(after)
+
     def kernel(*refs):
         n_in, n_out = len(ins), len(outs)
-        body(refs[0], refs[1 : 1 + n_in], refs[1 + n_in : 1 + n_in + n_out], refs[1 + n_in + n_out :])
+        rest = refs[1 + n_in + len(after) :]
+        body(refs[0], refs[1 : 1 + n_in], rest[:n_out], rest[n_out:])
 
     moved = sum(a.size * a.dtype.itemsize for a in ins) + sum(
         o.size * jnp.dtype(o.dtype).itemsize for o in outs
     )
     vmem = pl.BlockSpec(memory_space=pltpu.VMEM)
-    return pl.pallas_call(
+    results = pl.pallas_call(
         kernel,
         name=name,
-        in_specs=[pl.BlockSpec(memory_space=pltpu.SMEM)] + [vmem] * len(ins),
+        in_specs=[pl.BlockSpec(memory_space=pltpu.SMEM)] + [vmem] * len(ins)
+        + [pl.BlockSpec(memory_space=pl.ANY)] * len(after),
         out_specs=[vmem] * len(outs),
         out_shape=list(outs),
         scratch_shapes=list(scratch),
         compiler_params=pltpu.CompilerParams(vmem_limit_bytes=24 * 1024 * 1024),
         cost_estimate=pl.CostEstimate(flops=flops, bytes_accessed=moved, transcendentals=0),
-    )(ids, *ins)
+    )(ids, *ins, *after)
+    return list(results)
 
 
 def aligned(start, size):
@@ -108,8 +113,14 @@
     p_refs[which][where.start - which * half : where.stop - which * half, :] = value.astype(BF)
 
 
+def lane_picks(count):
+    shape = (count, 128)
+    row, lane = (lax.broadcasted_iota(jnp.int32, shape, d) for d in (0, 1))
+    return jnp.where(row == lane, 1.0, 0.0).astype(BF)
+
+
 def start_body(ids, ins, outs, scratch):
-    tokens, grads, w_qkv, w_out, w_in, w_down = ins
+    tokens, grads, gains, w_qkv, w_out, w_in, w_down = ins
     t, c = ids[1], ids[2]
     n, half = tokens.shape[0], tokens.shape[1] // 2
     for src, dst in ((tokens, outs[0]), (grads, outs[1])):
@@ -126,6 +137,8 @@
             for i in range(3):
                 dst[:, i * hc : (i + 1) * hc] = w_qkv[layer, i, :, cols]
             dst[:, 3 * hc : 4 * hc] = w_out[layer, :, cols]
+            if layer == 0:
+                dst[:, 4 * hc :] = mm(gains[...], lane_picks(gains.shape[0]), 0, 0).astype(BF)
         for i in range(3):
             scratch[0][:, :real] = w_down[layer] if i == 2 else w_in[layer, i]
             for k in range(TEAM):
@@ -142,8 +155,22 @@
 def full_body(ids, ins, outs, scratch):
     rows, nz = ins[0].shape[0], len(ins)
     for s in range(nz):
-        src = lax.rem(ids[0] - s + nz, nz)
+        src = ids[0] ^ s if nz == 4 else lax.rem(ids[0] - s + nz, nz)
         outs[0][aligned(src * rows, rows)] = ins[s][...]
+
+
+def full_gains_body(ids, ins, outs, scratch):
+    rows, nz = ins[0].shape[0], len(ins)
+    width = outs[0].shape[1]
+    for s in range(nz):
+        src = ids[0] ^ s if nz == 4 else lax.rem(ids[0] - s + nz, nz)
+        outs[0][aligned(src * rows, rows)] = ins[s][:, :width]
+        scratch[0][aligned(src * rows, rows)] = ins[s][:, width:]
+    outs[1][...] = mm(lane_picks(outs[1].shape[0]), scratch[0][...], 1, 1)
+
+
+def add_body(ids, ins, outs, scratch):
+    outs[0][...] = total_of(ins).astype(BF)
 
 
 def qkv_body(row, raw, n, sub):
@@ -403,7 +430,8 @@
     nz = len(outs)
     span = outs[0].shape[0]
     for s in range(nz):
-        outs[s][...] = full[aligned(lax.rem(ids[0] + s, nz) * span, span)]
+        dst = ids[0] ^ s if nz == 4 else lax.rem(ids[0] + s, nz)
+        outs[s][...] = full[aligned(dst * span, span)]
 
 
 def plane_sum_body(ids, ins, outs, scratch):
@@ -464,11 +492,13 @@
     rows = LOCAL * own
     aw, fw = 4 * hc, 3 * units
 
+    owned = jnp.concatenate([attn_gain, mlp_gain, attn_gain, mlp_gain], axis=0)[: 4 * layers]
     started = call(
         "start", start_body, ids,
-        [tokens, out_grad, w_qkv, w_attn_out, w_ffn_in, w_ffn_out],
+        [tokens, out_grad, owned, w_qkv, w_attn_out, w_ffn_in, w_ffn_out],
         [out((micro * sub, feat), BF)] * 2
-        + [out((d_rows, aw), BF)] * (layers * TEAM)
+        + [out((d_rows, aw + 128), BF)] * TEAM
+        + [out((d_rows, aw), BF)] * ((layers - 1) * TEAM)
         + [out((d_rows, fw), BF)] * (layers * TEAM),
         [pltpu.VMEM((d_rows, TEAM * units), BF)],
     )
@@ -484,26 +514,41 @@
 
     tok_blocks = [blocks_of(chain_rows(tok_own, i)) for i in range(CHAINS)]
 
-    def assemble(pieces, name):
+    def plane_of(pieces, name, after=()):
         width = pieces[0].shape[1]
         got = [pieces[0]] + [hop_team(pieces[k], k) for k in range(1, TEAM)]
-        plane = call("plane_" + name, plane_body, ids, got, [out((TEAM * d_rows, width), BF)])[0]
-        planes = [plane] + [hop_z(plane, s) for s in range(1, nz)]
-        return call("full_" + name, full_body, ids, planes, [out((nz * TEAM * d_rows, width), BF)])[0]
-
-    owned = jnp.concatenate([attn_gain, mlp_gain, attn_gain, mlp_gain], axis=0).astype(F32)[: 4 * layers]
-    spot = lax.broadcasted_iota(jnp.int32, (1, feat), 1) // d_rows == z * TEAM + t
-    gains = jnp.where(spot, jnp.tile(owned, (1, feat // d_rows)), 0.0)
-    gains = gains + hop_team(gains, 1)
-    gains = gains + hop_team(gains, 2)
-    gains = sum([gains] + [hop_z(gains, s) for s in range(1, nz)])
-
-    attn_w, ffn_w = [None] * layers, [None] * layers
-    for layer in range(layers):
-        attn_w[layer] = assemble(packs[layer * TEAM : (layer + 1) * TEAM], "a" + str(layer))
-        ffn_w[layer] = assemble(
-            packs[(layers + layer) * TEAM : (layers + layer + 1) * TEAM], "f" + str(layer)
-        )
+        return call("plane_" + name, plane_body, ids, got, [out((TEAM * d_rows, width), BF)], after=after)[0]
+
+    def full_of(plane, name, relay=True):
+        width = plane.shape[1]
+        if nz == 4 and relay:
+            far = hop_z(plane, 2)
+            planes = [plane, hop_z(plane, 1), far, hop_z(far, 1)]
+        else:
+            far = plane
+            planes = [plane] + [hop_z(plane, s) for s in range(1, nz)]
+        full = call("full_" + name, full_body, ids, planes, [out((nz * TEAM * d_rows, width), BF)])[0]
+        return full, far
+
+    def pack(kind, layer):
+        first = (kind * layers + layer) * TEAM
+        return packs[first : first + TEAM]
+
+    planes_a, planes_f = [plane_of(pack(0, 0), "a0")], [plane_of(pack(1, 0), "f0")]
+    planes = [planes_a[0]] + [hop_z(planes_a[0], s) for s in range(1, nz)]
+    wa0, gains = call(
+        "full_a0", full_gains_body, ids, planes,
+        [out((feat, aw), BF), out((4 * layers, feat), F32)], [pltpu.VMEM((feat, 128), BF)],
+    )
+    attn_w, ffn_w, far_f = [wa0], [], []
+    for i in range(layers):
+        if i > 0:
+            planes_a.append(plane_of(pack(0, i), "a" + str(i), ffn_w[i - 1 :]))
+            attn_w.append(full_of(planes_a[i], "a" + str(i), False)[0])
+            planes_f.append(plane_of(pack(1, i), "f" + str(i), attn_w[i:]))
+        w, far = full_of(planes_f[i], "f" + str(i))
+        ffn_w.append(w)
+        far_f.append(far)
     grad_blocks = [blocks_of(chain_rows(grad_own, i)) for i in range(CHAINS)]
 
     band_index = z * team_rows - BLK + jnp.arange(team_rows + 2 * BLK, dtype=jnp.int32)
@@ -547,11 +592,11 @@
     band = pltpu.VMEM((team_rows + 2 * BLK, hc), BF)
     band32 = pltpu.VMEM((team_rows + 2 * BLK, hc), F32)
 
-    def fold(parts, name):
+    def fold(parts, name, after=()):
         got = hop_core(parts[1])
         h = call(
             "fold_" + name, fold_body, ids, [parts[0], got],
-            [out((own, feat), F32)] + [out((own, feat), BF)] * (TEAM - 1),
+            [out((own, feat), F32)] + [out((own, feat), BF)] * (TEAM - 1), after=after,
         )
         return [h[0]] + [hop_team(h[k], k) for k in range(1, TEAM)]
 
@@ -562,7 +607,7 @@
         a, qkv, lo, hi = call(
             "qkv", qkv_body(layer, layer == 0, n, sub), ids, st["blocks"] + [gains, w, cos, sin],
             [out((rows, feat), BF), out((rows, 3 * hc), BF)] + [out((n * BLK, 2 * hc), BF)] * 2,
-            flops=2 * rows * feat * 3 * hc,
+            flops=2 * rows * feat * 3 * hc, after=[planes_f[0] if layer == 0 else far_f[layer]],
         )
         lo, hi = step_z(lo, 1), step_z(hi, -1)
         ctx, *parts = call(
@@ -590,6 +635,7 @@
             st["x"], a = call(
                 "next", resid_body(layer + 1), ids, [st["x"]] + terms + [gains],
                 [out((own, feat), F32), out((own, feat), BF)],
+                after=[attn_w[layer + 1], planes_f[layer + 1]],
             )
             st["blocks"] = blocks_of(a)
         else:
@@ -611,13 +657,21 @@
         st["dy"] = chain_rows(grad_own, i)
         st["blocks"] = grad_blocks[i]
 
-    def collect(ins, width, name):
-        flops = 2 * rows * CHAINS * feat * width
-        pieces = call(
+    def weight_pieces(ins, width, name):
+        return call(
             "wgrad_" + name, weight_grad_body, ids, ins, [out((TEAM * d_rows, width), BF)] * nz,
-            [pltpu.VMEM((nz * TEAM * d_rows, width), BF)], flops=flops,
-        )
-        got = [pieces[0]] + [hop_z(pieces[s], s) for s in range(1, nz)]
+            [pltpu.VMEM((nz * TEAM * d_rows, width), BF)], flops=2 * rows * CHAINS * feat * width,
+        )
+
+    def relay(pieces, name):
+        if nz != 4:
+            return [pieces[0]] + [hop_z(pieces[s], s) for s in range(1, nz)]
+        near = hop_z(pieces[1], 1)
+        far = call("relay_" + name, add_body, ids, [pieces[2], hop_z(pieces[3], 1)], [out(pieces[2].shape, BF)])[0]
+        return [pieces[0], near, hop_z(far, 2)]
+
+    def z_sum(got, name):
+        width = got[0].shape[1]
         mine = call(
             "zsum_" + name, plane_sum_body, ids, got,
             [out((d_rows, width), F32)] + [out((d_rows, width), BF)] * (TEAM - 1),
@@ -627,61 +681,64 @@
 
     gain_rows = [None] * (2 * layers)
 
-    def backward_mlp(st, layer):
-        b, gu, hid = st["saved"][layer][7:]
+    def add_gain(row, dg):
+        gain_rows[row] = dg if gain_rows[row] is None else gain_rows[row] + dg
+
+    attn_parts, ffn_parts = [None] * layers, [None] * layers
+    st = state[0]
+    wait_mlp, wait_fold, wait_mid = [], [], []
+    for layer in reversed(range(layers)):
+        w = attn_w[layer]
+        cos, sin = st["tables"][layer]
+        x_in, a, qkv, lo, hi, ctx, mid, b, gu, hid = st["saved"][layer]
         dy, dgu, *parts = call(
             "mlp_back", mlp_back_body, ids, st["blocks"] + [gu, ffn_w[layer]],
             [out((rows, feat), BF), out((rows, 2 * units), BF)] + partial_out,
-            flops=6 * rows * feat * units,
-        )
-        terms = fold(parts, "mlp_back")
+            flops=6 * rows * feat * units, after=wait_mlp,
+        )
+        terms = fold(parts, "mlp_back", wait_fold)
+        pieces = weight_pieces([b, dgu, dy, hid], fw, "f" + str(layer))
         dg, dmid, dmb = call(
-            "mid_back", norm_back_body(layers + layer), ids, terms + [st["saved"][layer][6], st["dy"], gains],
+            "mid_back", norm_back_body(layers + layer), ids, terms + [mid, st["dy"], gains],
             [out((1, feat), F32), out((own, feat), F32), out((own, feat), BF)],
-        )
-        old = gain_rows[layers + layer]
-        gain_rows[layers + layer] = dg if old is None else old + dg
-        st["dy"] = dmid
-        st["blocks"] = blocks_of(dmb)
-        return [b, dgu, dy, hid]
-
-    def backward_attn(st, layer):
-        windowed = layer % 2 == 0
-        w = attn_w[layer]
-        cos, sin = st["tables"][layer]
-        x_in, a, qkv, lo, hi, ctx = st["saved"][layer][:6]
+            after=pieces + wait_mid,
+        )
+        add_gain(layers + layer, dg)
+        relayed = relay(pieces, "f" + str(layer))
         dm, dq, dkv, dlo, dhi = call(
-            "attn_back", attn_back_body(windowed, n, sub), ids,
-            st["blocks"] + [qkv, lo, hi, st["col"], st["row"], w, cos, sin],
+            "attn_back", attn_back_body(layer % 2 == 0, n, sub), ids,
+            blocks_of(dmb) + [qkv, lo, hi, st["col"], st["row"], w, cos, sin],
             [out((rows, feat), BF), out((rows, hc), BF), out((rows, 2 * hc), F32)]
             + [out((n * BLK, 2 * hc), BF)] * 2,
             [band] * 2 + [pltpu.VMEM((rows, hc), BF), pltpu.VMEM((rows, hc), F32)] + [band32] * 2,
             flops=6 * rows * feat * hc,
         )
         from_next, from_prev = step_z(dlo, -1), step_z(dhi, 1)
+        ffn_parts[layer] = z_sum(relayed, "f" + str(layer))
         dqkv, *parts = call(
             "qkv_back", qkv_back_body(n, sub), ids, [dq, dkv, from_next, from_prev, w, cos, sin],
             [out((rows, 3 * hc), BF)] + partial_out, [pltpu.VMEM((rows, 2 * hc), F32)],
             flops=6 * rows * feat * hc,
-        )
-        terms = fold(parts, "qkv_back")
+            after=ffn_parts[layer][:1] + ([st["x"]] if layer + 1 == layers else []),
+        )
+        pieces = weight_pieces([a, dqkv, dm, ctx], aw, "a" + str(layer))
+        terms = fold(parts, "qkv_back", pieces if layer == 0 else [])
         low = [out((own, feat), BF)] if layer > 0 else []
         dg, st["dy"], *dyb = call(
-            "in_back", norm_back_body(layer), ids, terms + [x_in, st["dy"], gains],
-            [out((1, feat), F32), out((own, feat), F32)] + low,
-        )
-        old = gain_rows[layer]
-        gain_rows[layer] = dg if old is None else old + dg
+            "in_back", norm_back_body(layer), ids, terms + [x_in, dmid, gains],
+            [out((1, feat), F32), out((own, feat), F32)] + low, after=pieces + ffn_parts[layer],
+        )
+        add_gain(layer, dg)
         if layer > 0:
             st["blocks"] = blocks_of(dyb[0])
-        return [a, dqkv, dm, ctx]
-
-    attn_parts, ffn_parts = [None] * layers, [None] * layers
-    for layer in reversed(range(layers)):
-        ins = sum([backward_mlp(st, layer) for st in state], [])
-        ffn_parts[layer] = collect(ins, fw, "f" + str(layer))
-        ins = sum([backward_attn(st, layer) for st in state], [])
-        attn_parts[layer] = collect(ins, aw, "a" + str(layer))
+            relayed = relay(pieces, "a" + str(layer))
+            attn_parts[layer] = z_sum(relayed, "a" + str(layer))
+            wait_mlp = relayed[1:2]
+            wait_fold = attn_parts[layer][:1]
+            wait_mid = attn_parts[layer]
+        else:
+            got = [pieces[0]] + [hop_z(pieces[s], s) for s in range(1, nz)]
+            attn_parts[layer] = z_sum(got, "a" + str(layer))
 
     input_grad = join([st["dy"] for st in state], F32)
 

time: 638 us -> 546 us (0.86)
  starting transfers between devices: 206 us -> 159 us
  waiting for transfers between devices: 290 us -> 254 us
  local copies, waits for them, and re-layouts: 19.6 us -> 13.2 us
    ppermute x8, waiting for transfers between devices: 45.5 us -> 12.1 us  [step_z(): lax.ppermute(x, 'z', [(i, i + by) for i in range(n) if 0 <= i + by < n])]
    ppermute x30 -> x27, starting transfers between devices: 75.3 us -> 49.1 us  [hop_z(): lax.ppermute(x, 'z', [(i, i ^ s if n == 4 else (i + s) % n) for i in rang...]
    ppermute x76 -> x74, waiting for transfers between devices: 128 us -> 144 us  [hop_team(): return lax.ppermute(x, ('y', 'x'), [(i, i ^ k) for i in range(TEAM)])]
    ppermute x8, starting transfers between devices: 30.2 us -> 16.4 us  [step_z(): lax.ppermute(x, 'z', [(i, i + by) for i in range(n) if 0 <= i + by < n])]
    ppermute x30 -> x27, waiting for transfers between devices: 101 us -> 89.6 us  [hop_z(): lax.ppermute(x, 'z', [(i, i ^ s if n == 4 else (i + s) % n) for i in rang...]
    ppermute x43, waiting for transfers between devices: 16 us -> 8.83 us  [hop_core(): return lax.ppermute(x, 'c', [(0, 1), (1, 0)])]
    ppermute x76 -> x74, starting transfers between devices: 93.5 us -> 87.5 us  [hop_team(): return lax.ppermute(x, ('y', 'x'), [(i, i ^ k) for i in range(TEAM)])]
    unnamed x86 -> x44, local copies, waits for them, and re-layouts: 16.3 us -> 10.6 us
  transfers between devices with their start and end apart: 157 -> 152, of which waited for: 65 -> 58; matrix products, arithmetic and copies ran while one was open for 2% -> 1% of each run, Pallas kernels for 9% -> 12%
where the time goes in v3:
time: 546 us; the launch traced here: 539 us
  waiting for transfers between devices  254 us (47%)
  starting transfers between devices  159 us (29%)
  Pallas kernels  104 us (19%)
  local copies, waits for them, and re-layouts  13.2 us (2%)
  other arithmetic  5.88 us (1%)
    ppermute x74, waiting for transfers between devices, hop_team(): return lax.ppermute(x, ('y', 'x'), [(i, i ^ k) for i in range(TEAM)])  144 us
    pallas_call x51, Pallas kernels, call(): pl.pallas_call(kernel, name=name, in_specs=[pl.BlockSpec(memory_space=plt...  104 us
    ppermute x27, waiting for transfers between devices, hop_z(): lax.ppermute(x, 'z', [(i, i ^ s if n == 4 else (i + s) % n) for i in rang...  89.6 us
    ppermute x74, starting transfers between devices, hop_team(): return lax.ppermute(x, ('y', 'x'), [(i, i ^ k) for i in range(TEAM)])  87.5 us
    ppermute x27, starting transfers between devices, hop_z(): lax.ppermute(x, 'z', [(i, i ^ s if n == 4 else (i + s) % n) for i in rang...  49.1 us
    ppermute x8, starting transfers between devices, step_z(): lax.ppermute(x, 'z', [(i, i + by) for i in range(n) if 0 <= i + by < n])  16.4 us
    ppermute x8, waiting for transfers between devices, step_z(): lax.ppermute(x, 'z', [(i, i + by) for i in range(n) if 0 <= i + by < n])  12.1 us
  transfers between devices with their start and end apart: 152, of which 58 were waited for; matrix products, arithmetic and copies ran while one was open for 1% of the time, Pallas kernels for 12%

profile of v3, /device:TPU:0, one launch (start us, length us, event | category | flops | bytes accessed | tf_op | source)
XLA Modules:
  0.0 539.2 jit_solution(3943303301930652434)
XLA Ops:
  42.1 14.6 %collective-permute-done.11.refs_3_ = bf16[256,640]{1,0:T(8,128)(2,1)S(1)} collective-permute-done((bf16[256,640]{1,0:T(8,128)(2,1)S(1)}, bf16[256,640]{1,0:T(8,128)(2,1)S(1)}, u32[]{:S(2)}, u32[]{:S(2)}) %collective-permute-start.11) | collective-permute-done | bytes 327712 | tf_op jit(solution)/shard_map/ppermute | solution.py:34
  70.5 6.8 %attn.2 = (bf16[1024,128]{1,0:T(8,128)(2,1)S(1)}, bf16[512,1024]{1,0:T(8,128)(2,1)S(1)}, bf16[512,1024]{1,0:T(8,128)(2,1)S(1)}) custom-call(s32[3]{0:T(128)S(1)} %pad_add_fusion.refs_0_, bf16[1024,384]{1,0:T(8,128)(2,1)S(1)} %get-tuple-element.172.refs_1_.refs_9_, bf16[256,256]{1,0:T(8,128)(2,1)S(1)} %collective-permute-done.16.refs_2_.refs_10_, ...), custom_call_target="tpu_custom_call" | custom-call | flops 536870912 | bytes 4468736 | tf_op jit(solution)/shard_map/attn/pallas_call | solution.py:58
  85.2 22.3 %collective-permute-done.30.refs_3_ = bf16[256,1152]{1,0:T(8,128)(2,1)S(1)} collective-permute-done((bf16[256,1152]{1,0:T(8,128)(2,1)S(1)}, bf16[256,1152]{1,0:T(8,128)(2,1)S(1)}, u32[]{:S(2)}, u32[]{:S(2)}) %collective-permute-start.30) | collective-permute-done | bytes 589856 | tf_op jit(solution)/shard_map/ppermute | solution.py:34
  111.9 6.6 %collective-permute-done.24.refs_4_ = bf16[128,1024]{1,0:T(8,128)(2,1)S(1)} collective-permute-done((bf16[128,1024]{1,0:T(8,128)(2,1)S(1)}, bf16[128,1024]{1,0:T(8,128)(2,1)S(1)}, u32[]{:S(2)}, u32[]{:S(2)}) %collective-permute-start.24) | collective-permute-done | bytes 262176 | tf_op jit(solution)/shard_map/ppermute | solution.py:25
  118.6 4.4 collective-permute-done.23.refs_3_
  150.9 11.3 %collective-permute-done.40.refs_3_ = bf16[256,512]{1,0:T(8,128)(2,1)S(1)} collective-permute-done((bf16[256,512]{1,0:T(8,128)(2,1)S(1)}, bf16[256,512]{1,0:T(8,128)(2,1)S(1)}, u32[]{:S(2)}, u32[]{:S(2)}) %collective-permute-start.40) | collective-permute-done | bytes 262176 | tf_op jit(solution)/shard_map/ppermute | solution.py:34
  165.2 5.2 collective-permute-done.43.refs_3_
  176.9 6.7 %collective-permute-done.47.refs_4_ = bf16[128,1024]{1,0:T(8,128)(2,1)S(1)} collective-permute-done((bf16[128,1024]{1,0:T(8,128)(2,1)S(1)}, bf16[128,1024]{1,0:T(8,128)(2,1)S(1)}, u32[]{:S(2)}, u32[]{:S(2)}) %collective-permute-start.47) | collective-permute-done | bytes 262176 | tf_op jit(solution)/shard_map/ppermute | solution.py:25
  183.5 4.3 collective-permute-done.46.refs_3_
  188.4 10.2 %collective-permute-done.52.refs_13_.refs_3_ = bf16[256,1152]{1,0:T(8,128)(2,1)S(1)} collective-permute-done((bf16[256,1152]{1,0:T(8,128)(2,1)S(1)}, bf16[256,1152]{1,0:T(8,128)(2,1)S(1)}, u32[]{:S(2)}, u32[]{:S(2)}) %collective-permute-start.52) | collective-permute-done | bytes 589856 | tf_op jit(solution)/shard_map/ppermute | solution.py:34
  204.7 4.4 collective-permute-done.54.refs_3_.refs_11_
  209.1 6.8 %attn.3 = (bf16[1024,128]{1,0:T(8,128)(2,1)S(1)}, bf16[512,1024]{1,0:T(8,128)(2,1)S(1)}, bf16[512,1024]{1,0:T(8,128)(2,1)S(1)}) custom-call(s32[3]{0:T(128)S(1)} %pad_add_fusion.refs_0_, bf16[1024,384]{1,0:T(8,128)(2,1)S(1)} %get-tuple-element.199.refs_1_.refs_9_, bf16[256,256]{1,0:T(8,128)(2,1)S(1)} %collective-permute-done.53.refs_2_.refs_10_, ...), custom_call_target="tpu_custom_call" | custom-call | flops 536870912 | bytes 4468736 | tf_op jit(solution)/shard_map/attn/pallas_call | solution.py:58
  229.4 10.6 %collective-permute-done.57.refs_4_ = bf16[128,1024]{1,0:T(8,128)(2,1)S(1)} collective-permute-done((bf16[128,1024]{1,0:T(8,128)(2,1)S(1)}, bf16[128,1024]{1,0:T(8,128)(2,1)S(1)}, u32[]{:S(2)}, u32[]{:S(2)}) %collective-permute-start.57) | collective-permute-done | bytes 262176 | tf_op jit(solution)/shard_map/ppermute | solution.py:25
  243.9 4.2 collective-permute-done.74.refs_3_
  251.2 5.5 %collective-permute-done.60.refs_3_ = bf16[128,1024]{1,0:T(8,128)(2,1)S(1)} collective-permute-done((bf16[128,1024]{1,0:T(8,128)(2,1)S(1)}, bf16[128,1024]{1,0:T(8,128)(2,1)S(1)}, u32[]{:S(2)}, u32[]{:S(2)}) %collective-permute-start.60) | collective-permute-done | bytes 262176 | tf_op jit(solution)/shard_map/ppermute | solution.py:25
  264.6 4.2 mlp_back.2
  273.5 4.2 collective-permute-start.94
  282.0 5.7 %collective-permute-done.81.refs_2_ = bf16[128,1024]{1,0:T(8,128)(2,1)S(1)} collective-permute-done((bf16[128,1024]{1,0:T(8,128)(2,1)S(1)}, bf16[128,1024]{1,0:T(8,128)(2,1)S(1)}, u32[]{:S(2)}, u32[]{:S(2)}) %collective-permute-start.81) | collective-permute-done | bytes 262176 | tf_op jit(solution)/shard_map/ppermute | solution.py:25
  287.7 4.3 collective-permute-done.82.refs_3_
  304.5 5.1 collective-permute-done.85.refs_3_
  314.4 10.1 %attn_back.2 = (bf16[1024,1024]{1,0:T(8,128)(2,1)S(1)}, bf16[1024,128]{1,0:T(8,128)(2,1)S(1)}, f32[1024,256]{1,0:T(8,128)S(1)}, bf16[256,256]{1,0:T(8,128)(2,1)S(1)}, bf16[256,256]{1,0:T(8,128)(2,1)S(1)}) custom-call(s32[3]{0:T(128)S(1)} %pad_add_fusion.refs_0_, bf16[128,1024]{1,0:T(8,128)(2,1)S(1)} %get-tuple-element.232.refs_1_, ...), custom_call_target="tpu_custom_call" | custom-call | flops 805306368 | bytes 8925184 | tf_op jit(solution)/shard_map/attn_back/pallas_call | solution.py:58
  347.0 12.5 %collective-permute-done.101.refs_14_.refs_15_ = bf16[64,1152]{1,0:T(8,128)(2,1)S(1)} collective-permute-done((bf16[64,1152]{1,0:T(8,128)(2,1)S(1)}, bf16[64,1152]{1,0:T(8,128)(2,1)S(1)}, u32[]{:S(2)}, u32[]{:S(2)}) %collective-permute-start.101) | collective-permute-done | bytes 147488 | tf_op jit(solution)/shard_map/ppermute | solution.py:25
  366.7 4.2 collective-permute-done.105.refs_4_
  376.3 4.1 mlp_back.3
  383.1 6.8 %collective-permute-done.112.refs_2_ = bf16[256,512]{1,0:T(8,128)(2,1)S(1)} collective-permute-done((bf16[256,512]{1,0:T(8,128)(2,1)S(1)}, bf16[256,512]{1,0:T(8,128)(2,1)S(1)}, u32[]{:S(2)}, u32[]{:S(2)}) %collective-permute-start.112) | collective-permute-done | bytes 262176 | tf_op jit(solution)/shard_map/ppermute | solution.py:34
  398.2 7.0 %collective-permute-done.113.refs_3_ = bf16[256,512]{1,0:T(8,128)(2,1)S(1)} collective-permute-done((bf16[256,512]{1,0:T(8,128)(2,1)S(1)}, bf16[256,512]{1,0:T(8,128)(2,1)S(1)}, u32[]{:S(2)}, u32[]{:S(2)}) %collective-permute-start.113) | collective-permute-done | bytes 262176 | tf_op jit(solution)/shard_map/ppermute | solution.py:34
  411.6 9.7 %collective-permute-done.117.refs_13_.refs_6_ = bf16[64,512]{1,0:T(8,128)(2,1)S(1)} collective-permute-done((bf16[64,512]{1,0:T(8,128)(2,1)S(1)}, bf16[64,512]{1,0:T(8,128)(2,1)S(1)}, u32[]{:S(2)}, u32[]{:S(2)}) %collective-permute-start.117) | collective-permute-done | bytes 65568 | tf_op jit(solution)/shard_map/ppermute | solution.py:25
  442.1 5.1 collective-permute-done.121.refs_3_
  449.1 10.1 %attn_back.3 = (bf16[1024,1024]{1,0:T(8,128)(2,1)S(1)}, bf16[1024,128]{1,0:T(8,128)(2,1)S(1)}, f32[1024,256]{1,0:T(8,128)S(1)}, bf16[256,256]{1,0:T(8,128)(2,1)S(1)}, bf16[256,256]{1,0:T(8,128)(2,1)S(1)}) custom-call(s32[3]{0:T(128)S(1)} %pad_add_fusion.refs_0_, bf16[128,1024]{1,0:T(8,128)(2,1)S(1)} %get-tuple-element.277.refs_1_, ...), custom_call_target="tpu_custom_call" | custom-call | flops 805306368 | bytes 8925184 | tf_op jit(solution)/shard_map/attn_back/pallas_call | solution.py:58
  460.5 4.8 collective-permute-start.128
  480.7 15.1 %collective-permute-done.137.refs_14_.refs_11_ = bf16[64,1152]{1,0:T(8,128)(2,1)S(1)} collective-permute-done((bf16[64,1152]{1,0:T(8,128)(2,1)S(1)}, bf16[64,1152]{1,0:T(8,128)(2,1)S(1)}, u32[]{:S(2)}, u32[]{:S(2)}) %collective-permute-start.137) | collective-permute-done | bytes 147488 | tf_op jit(solution)/shard_map/ppermute | solution.py:25
  509.0 10.4 %collective-permute-done.147.refs_3_ = bf16[256,512]{1,0:T(8,128)(2,1)} collective-permute-done((bf16[256,512]{1,0:T(8,128)(2,1)S(1)}, bf16[256,512]{1,0:T(8,128)(2,1)}, u32[]{:S(2)}, u32[]{:S(2)}) %collective-permute-start.147) | collective-permute-done | bytes 262176 | tf_op jit(solution)/shard_map/ppermute | solution.py:34
  (393 shorter events, 289.6 us)
Async XLA Ops:
  33.3 23.5 %collective-permute-start.11 = (bf16[256,640]{1,0:T(8,128)(2,1)S(1)}, bf16[256,640]{1,0:T(8,128)(2,1)S(1)}, u32[]{:S(2)}, u32[]{:S(2)}) collective-permute-start(bf16[256,640]{1,0:T(8,128)(2,1)S(1)} %plane_a0.1.refs_1_), channel_id=1, source_target_pairs={{0,16},{8,24},{16,0},{24,8},{1,17},{9,25},{17,1},{25,9},{2,18},{10... | collective-permute-start | bytes 983048 | tf_op jit(solution)/shard_map/ppermute | solution.py:34
  77.4 30.1 %collective-permute-start.30 = (bf16[256,1152]{1,0:T(8,128)(2,1)S(1)}, bf16[256,1152]{1,0:T(8,128)(2,1)S(1)}, u32[]{:S(2)}, u32[]{:S(2)}) collective-permute-start(bf16[256,1152]{1,0:T(8,128)(2,1)S(1)} %plane_f0.1.refs_13_.refs_1_), channel_id=1, source_target_pairs={{0,16},{8,24},{16,0},{24,8},{1,17},{9,25},{17,1},{25,9},{2,18},{10... | collective-permute-start | bytes 1769480 | tf_op jit(solution)/shard_map/ppermute | solution.py:34
  80.8 31.1 %collective-permute-start.29 = (bf16[256,1152]{1,0:T(8,128)(2,1)S(1)}, bf16[256,1152]{1,0:T(8,128)(2,1)S(1)}, u32[]{:S(2)}, u32[]{:S(2)}) collective-permute-start(bf16[256,1152]{1,0:T(8,128)(2,1)S(1)} %plane_f0.1.refs_13_.refs_1_), channel_id=1, source_target_pairs={{0,8},{8,0},{16,24},{24,16},{1,9},{9,1},{17,25},{25,17},{2,10},{10... | collective-permute-start | bytes 1769480 | tf_op jit(solution)/shard_map/ppermute | solution.py:34
  81.6 25.9 %collective-permute-start.19 = (bf16[128,1024]{1,0:T(8,128)(2,1)S(1)}, bf16[128,1024]{1,0:T(8,128)(2,1)S(1)}, u32[]{:S(2)}, u32[]{:S(2)}) collective-permute-start(bf16[128,1024]{1,0:T(8,128)(2,1)S(1)} %get-tuple-element.178), channel_id=1, source_target_pairs={{0,2},{2,0},{4,6},{6,4},{1,3},{3,1},{5,7},{7,5},{8,10},{10,8},{12,... | collective-permute-start | bytes 786440 | tf_op jit(solution)/shard_map/ppermute | solution.py:25
  82.6 24.9 %collective-permute-start.20 = (bf16[128,1024]{1,0:T(8,128)(2,1)S(1)}, bf16[128,1024]{1,0:T(8,128)(2,1)S(1)}, u32[]{:S(2)}, u32[]{:S(2)}) collective-permute-start(bf16[128,1024]{1,0:T(8,128)(2,1)S(1)} %get-tuple-element.179), channel_id=1, source_target_pairs={{0,4},{2,6},{4,0},{6,2},{1,5},{3,7},{5,1},{7,3},{8,12},{10,14},{12... | collective-permute-start | bytes 786440 | tf_op jit(solution)/shard_map/ppermute | solution.py:25
  84.0 23.5 %collective-permute-start.21 = (bf16[128,1024]{1,0:T(8,128)(2,1)S(1)}, bf16[128,1024]{1,0:T(8,128)(2,1)S(1)}, u32[]{:S(2)}, u32[]{:S(2)}) collective-permute-start(bf16[128,1024]{1,0:T(8,128)(2,1)S(1)} %get-tuple-element.180), channel_id=1, source_target_pairs={{0,6},{2,4},{4,2},{6,0},{1,7},{3,5},{5,3},{7,1},{8,14},{10,12},{12... | collective-permute-start | bytes 786440 | tf_op jit(solution)/shard_map/ppermute | solution.py:25
  138.7 23.5 %collective-permute-start.40 = (bf16[256,512]{1,0:T(8,128)(2,1)S(1)}, bf16[256,512]{1,0:T(8,128)(2,1)S(1)}, u32[]{:S(2)}, u32[]{:S(2)}) collective-permute-start(bf16[256,512]{1,0:T(8,128)(2,1)S(1)} %plane_a1.1.refs_1_), channel_id=1, source_target_pairs={{0,16},{8,24},{16,0},{24,8},{1,17},{9,25},{17,1},{25,9},{2,18},{10... | collective-permute-start | bytes 786440 | tf_op jit(solution)/shard_map/ppermute | solution.py:34
  140.5 22.5 %collective-permute-start.39 = (bf16[256,512]{1,0:T(8,128)(2,1)S(1)}, bf16[256,512]{1,0:T(8,128)(2,1)S(1)}, u32[]{:S(2)}, u32[]{:S(2)}) collective-permute-start(bf16[256,512]{1,0:T(8,128)(2,1)S(1)} %plane_a1.1.refs_1_), channel_id=1, source_target_pairs={{0,8},{8,0},{16,24},{24,16},{1,9},{9,1},{17,25},{25,17},{2,10},{10... | collective-permute-start | bytes 786440 | tf_op jit(solution)/shard_map/ppermute | solution.py:34
  143.4 29.0 %collective-permute-start.33 = (bf16[128,1024]{1,0:T(8,128)(2,1)S(1)}, bf16[128,1024]{1,0:T(8,128)(2,1)S(1)}, u32[]{:S(2)}, u32[]{:S(2)}) collective-permute-start(bf16[128,1024]{1,0:T(8,128)(2,1)S(1)} %get-tuple-element.186), channel_id=1, source_target_pairs={{0,2},{2,0},{4,6},{6,4},{1,3},{3,1},{5,7},{7,5},{8,10},{10,8},{12,... | collective-permute-start | bytes 786440 | tf_op jit(solution)/shard_map/ppermute | solution.py:25
  148.5 24.0 %collective-permute-start.34 = (bf16[128,1024]{1,0:T(8,128)(2,1)S(1)}, bf16[128,1024]{1,0:T(8,128)(2,1)S(1)}, u32[]{:S(2)}, u32[]{:S(2)}) collective-permute-start(bf16[128,1024]{1,0:T(8,128)(2,1)S(1)} %get-tuple-element.187), channel_id=1, source_target_pairs={{0,4},{2,6},{4,0},{6,2},{1,5},{3,7},{5,1},{7,3},{8,12},{10,14},{12... | collective-permute-start | bytes 786440 | tf_op jit(solution)/shard_map/ppermute | solution.py:25
  149.1 23.3 %collective-permute-start.35 = (bf16[128,1024]{1,0:T(8,128)(2,1)S(1)}, bf16[128,1024]{1,0:T(8,128)(2,1)S(1)}, u32[]{:S(2)}, u32[]{:S(2)}) collective-permute-start(bf16[128,1024]{1,0:T(8,128)(2,1)S(1)} %get-tuple-element.188), channel_id=1, source_target_pairs={{0,6},{2,4},{4,2},{6,0},{1,7},{3,5},{5,3},{7,1},{8,14},{10,12},{12... | collective-permute-start | bytes 786440 | tf_op jit(solution)/shard_map/ppermute | solution.py:25
  171.0 27.6 %collective-permute-start.52 = (bf16[256,1152]{1,0:T(8,128)(2,1)S(1)}, bf16[256,1152]{1,0:T(8,128)(2,1)S(1)}, u32[]{:S(2)}, u32[]{:S(2)}) collective-permute-start(bf16[256,1152]{1,0:T(8,128)(2,1)S(1)} %plane_f1.1.refs_8_.refs_1_), channel_id=1, source_target_pairs={{0,16},{8,24},{16,0},{24,8},{1,17},{9,25},{17,1},{25,9},{2,18},{10... | collective-permute-start | bytes 1769480 | tf_op jit(solution)/shard_map/ppermute | solution.py:34
  176.9 21.7 %collective-permute-start.48 = (bf16[128,1024]{1,0:T(8,128)(2,1)S(1)}, bf16[128,1024]{1,0:T(8,128)(2,1)S(1)}, u32[]{:S(2)}, u32[]{:S(2)}) collective-permute-start(bf16[128,1024]{1,0:T(8,128)(2,1)S(1)} %get-tuple-element.198.refs_1_), channel_id=1, source_target_pairs={{0,1},{1,0},{2,3},{3,2},{4,5},{5,4},{6,7},{7,6},{8,9},{9,8},{10,11... | collective-permute-start | bytes 786440 | tf_op jit(solution)/shard_map/ppermute | solution.py:29
  222.9 27.1 %collective-permute-start.66 = (bf16[256,1152]{1,0:T(8,128)(2,1)S(1)}, bf16[256,1152]{1,0:T(8,128)(2,1)S(1)}, u32[]{:S(2)}, u32[]{:S(2)}) collective-permute-start(bf16[256,1152]{1,0:T(8,128)(2,1)S(1)} %plane_f1.1.refs_8_.refs_1_), channel_id=1, source_target_pairs={{0,8},{8,0},{16,24},{24,16},{1,9},{9,1},{17,25},{25,17},{2,10},{10... | collective-permute-start | bytes 1769480 | tf_op jit(solution)/shard_map/ppermute | solution.py:34
  269.2 28.7 %collective-permute-start.68 = (bf16[512,1024]{1,0:T(8,128)(2,1)S(1)}, bf16[512,1024]{1,0:T(8,128)(2,1)S(1)}, u32[]{:S(2)}, u32[]{:S(2)}) collective-permute-start(bf16[512,1024]{1,0:T(8,128)(2,1)S(1)} %get-tuple-element.211), channel_id=1, source_target_pairs={{0,1},{1,0},{2,3},{3,2},{4,5},{5,4},{6,7},{7,6},{8,9},{9,8},{10,11... | collective-permute-start | bytes 3145736 | tf_op jit(solution)/shard_map/ppermute | solution.py:29
  273.5 23.4 %collective-permute-start.94 = (bf16[256,1152]{1,0:T(8,128)(2,1)S(1)}, bf16[256,1152]{1,0:T(8,128)(2,1)S(1)}, u32[]{:S(2)}, u32[]{:S(2)}) collective-permute-start(bf16[256,1152]{1,0:T(8,128)(2,1)S(1)} %get-tuple-element.231.refs_11_), channel_id=1, source_target_pairs={{0,8},{8,0},{16,24},{24,16},{1,9},{9,1},{17,25},{25,17},{2,10},{10... | collective-permute-start | bytes 1769480 | tf_op jit(solution)/shard_map/ppermute | solution.py:34
  297.9 26.6 %collective-permute-start.93 = (bf16[256,1152]{1,0:T(8,128)(2,1)S(1)}, bf16[256,1152]{1,0:T(8,128)(2,1)S(1)}, u32[]{:S(2)}, u32[]{:S(2)}) collective-permute-start(bf16[256,1152]{1,0:T(8,128)(2,1)S(1)} %get-tuple-element.229.refs_9_), channel_id=1, source_target_pairs={{0,8},{8,0},{16,24},{24,16},{1,9},{9,1},{17,25},{25,17},{2,10},{10... | collective-permute-start | bytes 1769480 | tf_op jit(solution)/shard_map/ppermute | solution.py:34
  298.9 28.8 %collective-permute-start.95 = (bf16[256,1152]{1,0:T(8,128)(2,1)S(1)}, bf16[256,1152]{1,0:T(8,128)(2,1)S(1)}, u32[]{:S(2)}, u32[]{:S(2)}) collective-permute-start(bf16[256,1152]{1,0:T(8,128)(2,1)S(1)} %relay_f1.1), channel_id=1, source_target_pairs={{0,16},{8,24},{16,0},{24,8},{1,17},{9,25},{17,1},{25,9},{2,18},{10... | collective-permute-start | bytes 1769480 | tf_op jit(solution)/shard_map/ppermute | solution.py:34
  338.5 21.1 %collective-permute-start.97 = (bf16[128,1024]{1,0:T(8,128)(2,1)S(1)}, bf16[128,1024]{1,0:T(8,128)(2,1)S(1)}, u32[]{:S(2)}, u32[]{:S(2)}) collective-permute-start(bf16[128,1024]{1,0:T(8,128)(2,1)S(1)} %get-tuple-element.241), channel_id=1, source_target_pairs={{0,2},{2,0},{4,6},{6,4},{1,3},{3,1},{5,7},{7,5},{8,10},{10,8},{12,... | collective-permute-start | bytes 786440 | tf_op jit(solution)/shard_map/ppermute | solution.py:25
  380.5 25.7 %collective-permute-start.111 = (bf16[512,1024]{1,0:T(8,128)(2,1)S(1)}, bf16[512,1024]{1,0:T(8,128)(2,1)S(1)}, u32[]{:S(2)}, u32[]{:S(2)}) collective-permute-start(bf16[512,1024]{1,0:T(8,128)(2,1)S(1)} %get-tuple-element.259), channel_id=1, source_target_pairs={{0,1},{1,0},{2,3},{3,2},{4,5},{5,4},{6,7},{7,6},{8,9},{9,8},{10,11... | collective-permute-start | bytes 3145736 | tf_op jit(solution)/shard_map/ppermute | solution.py:29
  396.4 39.1 %collective-permute-start.130 = (bf16[256,1152]{1,0:T(8,128)(2,1)S(1)}, bf16[256,1152]{1,0:T(8,128)(2,1)S(1)}, u32[]{:S(2)}, u32[]{:S(2)}) collective-permute-start(bf16[256,1152]{1,0:T(8,128)(2,1)S(1)} %get-tuple-element.273.refs_11_), channel_id=1, source_target_pairs={{0,8},{8,0},{16,24},{24,16},{1,9},{9,1},{17,25},{25,17},{2,10},{10... | collective-permute-start | bytes 1769480 | tf_op jit(solution)/shard_map/ppermute | solution.py:34
  407.0 23.8 %collective-permute-start.114 = (bf16[128,1024]{1,0:T(8,128)(2,1)S(1)}, bf16[128,1024]{1,0:T(8,128)(2,1)S(1)}, u32[]{:S(2)}, u32[]{:S(2)}) collective-permute-start(bf16[128,1024]{1,0:T(8,128)(2,1)S(1)} %get-tuple-element.262), channel_id=1, source_target_pairs={{0,2},{2,0},{4,6},{6,4},{1,3},{3,1},{5,7},{7,5},{8,10},{10,8},{12,... | collective-permute-start | bytes 786440 | tf_op jit(solution)/shard_map/ppermute | solution.py:25
  408.1 22.7 %collective-permute-start.115 = (bf16[128,1024]{1,0:T(8,128)(2,1)S(1)}, bf16[128,1024]{1,0:T(8,128)(2,1)S(1)}, u32[]{:S(2)}, u32[]{:S(2)}) collective-permute-start(bf16[128,1024]{1,0:T(8,128)(2,1)S(1)} %get-tuple-element.263), channel_id=1, source_target_pairs={{0,4},{2,6},{4,0},{6,2},{1,5},{3,7},{5,1},{7,3},{8,12},{10,14},{12... | collective-permute-start | bytes 786440 | tf_op jit(solution)/shard_map/ppermute | solution.py:25
  409.4 21.4 %collective-permute-start.116 = (bf16[128,1024]{1,0:T(8,128)(2,1)S(1)}, bf16[128,1024]{1,0:T(8,128)(2,1)S(1)}, u32[]{:S(2)}, u32[]{:S(2)}) collective-permute-start(bf16[128,1024]{1,0:T(8,128)(2,1)S(1)} %get-tuple-element.264), channel_id=1, source_target_pairs={{0,6},{2,4},{4,2},{6,0},{1,7},{3,5},{5,3},{7,1},{8,14},{10,12},{12... | collective-permute-start | bytes 786440 | tf_op jit(solution)/shard_map/ppermute | solution.py:25
  435.5 29.8 %collective-permute-start.129 = (bf16[256,1152]{1,0:T(8,128)(2,1)S(1)}, bf16[256,1152]{1,0:T(8,128)(2,1)S(1)}, u32[]{:S(2)}, u32[]{:S(2)}) collective-permute-start(bf16[256,1152]{1,0:T(8,128)(2,1)S(1)} %get-tuple-element.271.refs_9_), channel_id=1, source_target_pairs={{0,8},{8,0},{16,24},{24,16},{1,9},{9,1},{17,25},{25,17},{2,10},{10... | collective-permute-start | bytes 1769480 | tf_op jit(solution)/shard_map/ppermute | solution.py:34
  437.3 29.9 %collective-permute-start.131 = (bf16[256,1152]{1,0:T(8,128)(2,1)S(1)}, bf16[256,1152]{1,0:T(8,128)(2,1)S(1)}, u32[]{:S(2)}, u32[]{:S(2)}) collective-permute-start(bf16[256,1152]{1,0:T(8,128)(2,1)S(1)} %relay_f0.1), channel_id=1, source_target_pairs={{0,16},{8,24},{16,0},{24,8},{1,17},{9,25},{17,1},{25,9},{2,18},{10... | collective-permute-start | bytes 1769480 | tf_op jit(solution)/shard_map/ppermute | solution.py:34
  474.7 25.4 %collective-permute-start.133 = (bf16[128,1024]{1,0:T(8,128)(2,1)S(1)}, bf16[128,1024]{1,0:T(8,128)(2,1)S(1)}, u32[]{:S(2)}, u32[]{:S(2)}) collective-permute-start(bf16[128,1024]{1,0:T(8,128)(2,1)S(1)} %get-tuple-element.294), channel_id=1, source_target_pairs={{0,2},{2,0},{4,6},{6,4},{1,3},{3,1},{5,7},{7,5},{8,10},{10,8},{12,... | collective-permute-start | bytes 786440 | tf_op jit(solution)/shard_map/ppermute | solution.py:25
  475.8 24.5 %collective-permute-start.134 = (bf16[128,1024]{1,0:T(8,128)(2,1)S(1)}, bf16[128,1024]{1,0:T(8,128)(2,1)S(1)}, u32[]{:S(2)}, u32[]{:S(2)}) collective-permute-start(bf16[128,1024]{1,0:T(8,128)(2,1)S(1)} %get-tuple-element.295), channel_id=1, source_target_pairs={{0,4},{2,6},{4,0},{6,2},{1,5},{3,7},{5,1},{7,3},{8,12},{10,14},{12... | collective-permute-start | bytes 786440 | tf_op jit(solution)/shard_map/ppermute | solution.py:25
  477.0 23.3 %collective-permute-start.135 = (bf16[128,1024]{1,0:T(8,128)(2,1)S(1)}, bf16[128,1024]{1,0:T(8,128)(2,1)S(1)}, u32[]{:S(2)}, u32[]{:S(2)}) collective-permute-start(bf16[128,1024]{1,0:T(8,128)(2,1)S(1)} %get-tuple-element.296), channel_id=1, source_target_pairs={{0,6},{2,4},{4,2},{6,0},{1,7},{3,5},{5,3},{7,1},{8,14},{10,12},{12... | collective-permute-start | bytes 786440 | tf_op jit(solution)/shard_map/ppermute | solution.py:25
  498.0 21.5 %collective-permute-start.147 = (bf16[256,512]{1,0:T(8,128)(2,1)S(1)}, bf16[256,512]{1,0:T(8,128)(2,1)}, u32[]{:S(2)}, u32[]{:S(2)}) collective-permute-start(bf16[256,512]{1,0:T(8,128)(2,1)S(1)} %get-tuple-element.291.refs_5_.refs_10_), channel_id=1, source_target_pairs={{0,16},{8,24},{16,0},{24,8},{1,17},{9,25},{17,1},{25,9},{2,18},{10... | collective-permute-start | bytes 786440 | tf_op jit(solution)/shard_map/ppermute | solution.py:34
  500.3 24.0 %collective-permute-start.72 = (bf16[128,1024]{1,0:T(8,128)(2,1)S(1)}, bf16[128,1024]{1,0:T(8,128)(2,1)}, u32[]{:S(2)}, u32[]{:S(2)}) collective-permute-start(bf16[128,1024]{1,0:T(8,128)(2,1)S(1)} %last.1.refs_1_.refs_9_), channel_id=1, source_target_pairs={{0,1},{1,0},{2,3},{3,2},{4,5},{5,4},{6,7},{7,6},{8,9},{9,8},{10,11... | collective-permute-start | bytes 786440 | tf_op jit(solution)/shard_map/ppermute | solution.py:29
  507.6 29.1 %collective-permute-start.139 = (f32[128,1024]{1,0:T(8,128)}, f32[128,1024]{1,0:T(8,128)}, u32[]{:S(2)}, u32[]{:S(2)}) collective-permute-start(f32[128,1024]{1,0:T(8,128)} %copy-done.3), channel_id=1, source_target_pairs={{0,1},{1,0},{2,3},{3,2},{4,5},{5,4},{6,7},{7,6},{8,9},{9,8},{10,11... | collective-permute-start | bytes 1572872 | tf_op jit(solution)/shard_map/ppermute | solution.py:29
  (142 other events, 1367.7 us)

commit v4 on v3

--- a/solution.py
+++ b/solution.py
@@ -113,37 +113,40 @@
     p_refs[which][where.start - which * half : where.stop - which * half, :] = value.astype(BF)
 
 
-def lane_picks(count):
-    shape = (count, 128)
-    row, lane = (lax.broadcasted_iota(jnp.int32, shape, d) for d in (0, 1))
-    return jnp.where(row == lane, 1.0, 0.0).astype(BF)
+def start_attn_body(ids, ins, outs, scratch):
+    w_qkv, w_out = ins
+    layers, hc = w_qkv.shape[0], w_qkv.shape[3] // TEAM
+    for layer in range(layers):
+        for k in range(TEAM):
+            cols = aligned((ids[1] ^ k) * hc, hc)
+            if layer == 0:
+                dst, rest, at = outs[k], outs[TEAM + k], 0
+            else:
+                dst = rest = outs[(layer + 1) * TEAM + k]
+                at = 3 * hc
+            for i in range(3):
+                dst[:, i * hc : (i + 1) * hc] = w_qkv[layer, i, :, cols]
+            rest[:, at : at + hc] = w_out[layer, :, cols]
 
 
 def start_body(ids, ins, outs, scratch):
-    tokens, grads, gains, w_qkv, w_out, w_in, w_down = ins
+    tokens, grads, w_in, w_down, owned = ins
     t, c = ids[1], ids[2]
     n, half = tokens.shape[0], tokens.shape[1] // 2
     for src, dst in ((tokens, outs[0]), (grads, outs[1])):
         for mb in range(n):
             dst[mb * half : (mb + 1) * half] = src[mb, aligned(c * half, half)]
-    packs = outs[2:]
-    layers, hc = w_qkv.shape[0], w_qkv.shape[3] // TEAM
+    spot = lax.broadcasted_iota(jnp.int32, owned.shape, 1) // w_in.shape[2] == ids[0] * TEAM + t
+    outs[2][...] = jnp.where(spot, owned[...], 0.0)
+    packs = outs[3:]
     real, units = w_in.shape[3], scratch[0].shape[1] // TEAM
     scratch[0][...] = jnp.zeros(scratch[0].shape, BF)
-    for layer in range(layers):
-        for k in range(TEAM):
-            dst = packs[layer * TEAM + k]
-            cols = aligned((t ^ k) * hc, hc)
-            for i in range(3):
-                dst[:, i * hc : (i + 1) * hc] = w_qkv[layer, i, :, cols]
-            dst[:, 3 * hc : 4 * hc] = w_out[layer, :, cols]
-            if layer == 0:
-                dst[:, 4 * hc :] = mm(gains[...], lane_picks(gains.shape[0]), 0, 0).astype(BF)
+    for layer in range(w_in.shape[0]):
         for i in range(3):
             scratch[0][:, :real] = w_down[layer] if i == 2 else w_in[layer, i]
             for k in range(TEAM):
                 cols = pl.ds(pl.multiple_of((t ^ k) * units, 128), units)
-                packs[(layers + layer) * TEAM + k][:, i * units : (i + 1) * units] = scratch[0][:, cols]
+                packs[layer * TEAM + k][:, i * units : (i + 1) * units] = scratch[0][:, cols]
 
 
 def plane_body(ids, ins, outs, scratch):
@@ -159,16 +162,6 @@
         outs[0][aligned(src * rows, rows)] = ins[s][...]
 
 
-def full_gains_body(ids, ins, outs, scratch):
-    rows, nz = ins[0].shape[0], len(ins)
-    width = outs[0].shape[1]
-    for s in range(nz):
-        src = ids[0] ^ s if nz == 4 else lax.rem(ids[0] - s + nz, nz)
-        outs[0][aligned(src * rows, rows)] = ins[s][:, :width]
-        scratch[0][aligned(src * rows, rows)] = ins[s][:, width:]
-    outs[1][...] = mm(lane_picks(outs[1].shape[0]), scratch[0][...], 1, 1)
-
-
 def add_body(ids, ins, outs, scratch):
     outs[0][...] = total_of(ins).astype(BF)
 
@@ -177,7 +170,7 @@
     def body(ids, ins, outs, scratch):
         blocks, (gains, w, cos, sin) = ins[:LOCAL], ins[LOCAL:]
         a_ref, qkv_ref, lo_ref, hi_ref = outs
-        hc = w.shape[1] // 4
+        hc = cos.shape[1]
         for where, tile in tiles_of(blocks, 256):
             if raw:
                 tile = (norm_parts(tile.astype(F32))[0] * gains[row : row + 1]).astype(BF)
@@ -211,12 +204,18 @@
         vb[dst] = qkv[src, 2 * hc :]
 
 
+def keys_of(i, windowed):
+    return slice(i * BLK + BLK - HALF, (i + 2) * BLK + HALF) if windowed else slice(i * BLK, (i + 3) * BLK)
+
+
 def allowed_of(mb, i, col, row, windowed):
-    ok = col[mb, BLK + i * BLK : 2 * BLK + i * BLK, :] == row[mb, :, i * BLK : (i + 3) * BLK]
+    keys = keys_of(0, windowed)
+    width = keys.stop - keys.start
+    ok = col[mb, BLK + i * BLK : 2 * BLK + i * BLK, :] == row[mb, :, i * BLK : i * BLK + width]
     if windowed:
-        shape = (BLK, 3 * BLK)
+        shape = (BLK, width)
         gap = lax.broadcasted_iota(jnp.int32, shape, 1) - lax.broadcasted_iota(jnp.int32, shape, 0)
-        ok = ok & (gap <= BLK + HALF) & (gap >= BLK - HALF)
+        ok = ok & (gap <= 2 * HALF) & (gap >= 0)
     return ok
 
 
@@ -234,9 +233,9 @@
 
 
 def probs_of(qh, k, ok):
-    s = jnp.where(ok, 0.125 * mm(qh, k, 1, 1), MASKED)
+    s = jnp.where(ok, mm(qh, k, 1, 1), MASKED)
     e = jnp.exp(s - jnp.max(s, axis=1, keepdims=True))
-    return e / jnp.sum(e, axis=1, keepdims=True)
+    return e * (1.0 / jnp.sum(e, axis=1, keepdims=True))
 
 
 def attn_body(windowed, n, sub):
@@ -250,8 +249,8 @@
             fill_band(ids, mb, n, sub, qkv, lo, hi, kb, vb)
             for i in range(LOCAL * sub // BLK):
                 ok = allowed_of(mb, i, col, row, windowed)
-                q = take(ids, qkv, n, sub, mb, i, slice(0, hc))
-                band = slice(i * BLK, (i + 3) * BLK)
+                q = take(ids, qkv, n, sub, mb, i, slice(0, hc)) * jnp.asarray(0.125, BF)
+                band = keys_of(i, windowed)
                 k, v = kb[band], vb[band]
                 ctx = jnp.zeros((BLK, hc), F32)
                 for h in range(hc // HD):
@@ -262,7 +261,7 @@
         total = ctx_ref.shape[0]
         for first in range(0, total, 256):
             where = slice(first, first + 256)
-            store_partial(outs[1:], where, mm(ctx_ref[where], w[:, 3 * hc :], 1, 1))
+            store_partial(outs[1:], where, mm(ctx_ref[where], w[:, w.shape[1] - hc :], 1, 1))
 
     return body
 
@@ -345,7 +344,7 @@
         hc = kb.shape[1]
         for where, tile in tiles_of(blocks, 256):
             dm_ref[where] = tile
-            dctx[where] = mm(tile, w[:, 3 * hc :], 1, 0).astype(BF)
+            dctx[where] = mm(tile, w[:, w.shape[1] - hc :], 1, 0).astype(BF)
         head_of = lax.broadcasted_iota(jnp.int32, (BLK, hc), 1) // HD
         last = BLK + LOCAL * sub
         for mb in range(n):
@@ -354,9 +353,9 @@
             dvb[...] = jnp.zeros(dvb.shape, F32)
             for i in range(LOCAL * sub // BLK):
                 ok = allowed_of(mb, i, col, row, windowed)
-                q = take(ids, qkv, n, sub, mb, i, slice(0, hc))
+                q = take(ids, qkv, n, sub, mb, i, slice(0, hc)) * jnp.asarray(0.125, BF)
                 do = take(ids, dctx, n, sub, mb, i, slice(0, hc))
-                band = slice(i * BLK, (i + 3) * BLK)
+                band = keys_of(i, windowed)
                 k, v = kb[band], vb[band]
                 dq = jnp.zeros((BLK, hc), F32)
                 dk = dkb[band]
@@ -375,14 +374,14 @@
                 dkb[band] = dk
                 dvb[band] = dv
             edge = slice(mb * BLK, (mb + 1) * BLK)
-            dlo_ref[edge, :hc] = (0.125 * dkb[:BLK]).astype(BF)
+            dlo_ref[edge, :hc] = dkb[:BLK].astype(BF)
             dlo_ref[edge, hc:] = dvb[:BLK].astype(BF)
-            dhi_ref[edge, :hc] = (0.125 * dkb[last:]).astype(BF)
+            dhi_ref[edge, :hc] = dkb[last:].astype(BF)
             dhi_ref[edge, hc:] = dvb[last:].astype(BF)
             for b in range(LOCAL):
                 src = slice(BLK + b * sub, BLK + (b + 1) * sub)
                 dst = true_rows(ids, n, sub, mb, b)
-                dkv_ref[dst, :hc] = 0.125 * dkb[src]
+                dkv_ref[dst, :hc] = dkb[src]
                 dkv_ref[dst, hc:] = dvb[src]
         for first in range(0, dqs.shape[0], 256):
             where = slice(first, first + 256)
@@ -397,7 +396,7 @@
         dq, dkv, from_next, from_prev, w, cos, sin = ins
         dqkv_ref = outs[0]
         acc = scratch[0]
-        hc = w.shape[1] // 4
+        hc = cos.shape[1]
         acc[...] = dkv[...]
         per = BLK // sub
         for mb in range(n):
@@ -493,31 +492,37 @@
     aw, fw = 4 * hc, 3 * units
 
     owned = jnp.concatenate([attn_gain, mlp_gain, attn_gain, mlp_gain], axis=0)[: 4 * layers]
-    started = call(
-        "start", start_body, ids,
-        [tokens, out_grad, owned, w_qkv, w_attn_out, w_ffn_in, w_ffn_out],
-        [out((micro * sub, feat), BF)] * 2
-        + [out((d_rows, aw + 128), BF)] * TEAM
-        + [out((d_rows, aw), BF)] * ((layers - 1) * TEAM)
-        + [out((d_rows, fw), BF)] * (layers * TEAM),
-        [pltpu.VMEM((d_rows, TEAM * units), BF)],
-    )
-    tok_own, grad_own = started[:2]
-    packs = started[2:]
-
-    def blocks_of(x):
-        mine = [x] + [hop_team(x, k) for k in range(1, TEAM)]
-        return mine + [hop_core(b) for b in mine]
-
-    def chain_rows(x, i):
-        return x[i * own : (i + 1) * own]
-
-    tok_blocks = [blocks_of(chain_rows(tok_own, i)) for i in range(CHAINS)]
+    owned = jnp.tile(owned.astype(F32), (1, feat // d_rows))
+    packs_a = call(
+        "start_attn", start_attn_body, ids, [w_qkv, w_attn_out],
+        [out((d_rows, 3 * hc), BF)] * TEAM
+        + [out((d_rows, hc), BF)] * TEAM
+        + [out((d_rows, aw), BF)] * ((layers - 1) * TEAM),
+    )
 
     def plane_of(pieces, name, after=()):
         width = pieces[0].shape[1]
         got = [pieces[0]] + [hop_team(pieces[k], k) for k in range(1, TEAM)]
         return call("plane_" + name, plane_body, ids, got, [out((TEAM * d_rows, width), BF)], after=after)[0]
+
+    plane_qkv = plane_of(packs_a[:TEAM], "q0")
+    tok_own, grad_own, gains, *packs_f = call(
+        "start", start_body, ids, [tokens, out_grad, w_ffn_in, w_ffn_out, owned],
+        [out((micro * sub, feat), BF)] * 2
+        + [out((4 * layers, feat), F32)]
+        + [out((d_rows, fw), BF)] * (layers * TEAM),
+        [pltpu.VMEM((d_rows, TEAM * units), BF)], after=[plane_qkv],
+    )
+    plane_out = plane_of(packs_a[TEAM : 2 * TEAM], "o0")
+
+    def blocks_of(x):
+        mine = [x] + [hop_team(x, k) for k in range(1, TEAM)]
+        return mine + [hop_core(b) for b in mine]
+
+    def chain_rows(x, i):
+        return x[i * own : (i + 1) * own]
+
+    tok_blocks = [blocks_of(chain_rows(tok_own, i)) for i in range(CHAINS)]
 
     def full_of(plane, name, relay=True):
         width = plane.shape[1]
@@ -530,22 +535,24 @@
         full = call("full_" + name, full_body, ids, planes, [out((nz * TEAM * d_rows, width), BF)])[0]
         return full, far
 
+    gains = sum([gains] + [hop_team(gains, k) for k in range(1, TEAM)])
+    gains = sum([gains] + [hop_z(gains, s) for s in range(1, nz)])
+
     def pack(kind, layer):
-        first = (kind * layers + layer) * TEAM
-        return packs[first : first + TEAM]
-
-    planes_a, planes_f = [plane_of(pack(0, 0), "a0")], [plane_of(pack(1, 0), "f0")]
-    planes = [planes_a[0]] + [hop_z(planes_a[0], s) for s in range(1, nz)]
-    wa0, gains = call(
-        "full_a0", full_gains_body, ids, planes,
-        [out((feat, aw), BF), out((4 * layers, feat), F32)], [pltpu.VMEM((feat, 128), BF)],
-    )
-    attn_w, ffn_w, far_f = [wa0], [], []
+        if kind == 0:
+            return packs_a[(layer + 1) * TEAM : (layer + 2) * TEAM]
+        return packs_f[layer * TEAM : (layer + 1) * TEAM]
+
+    w_q0 = full_of(plane_qkv, "q0", False)[0]
+    w_o0 = full_of(plane_out, "o0", False)[0]
+    planes_a, planes_f = [plane_out], [plane_of(pack(1, 0), "f0")]
+    attn_w, ffn_w, far_f = [(w_q0, w_o0)], [], []
     for i in range(layers):
         if i > 0:
             planes_a.append(plane_of(pack(0, i), "a" + str(i), ffn_w[i - 1 :]))
-            attn_w.append(full_of(planes_a[i], "a" + str(i), False)[0])
-            planes_f.append(plane_of(pack(1, i), "f" + str(i), attn_w[i:]))
+            full = full_of(planes_a[i], "a" + str(i), False)[0]
+            attn_w.append((full, full))
+            planes_f.append(plane_of(pack(1, i), "f" + str(i), [full]))
         w, far = full_of(planes_f[i], "f" + str(i))
         ffn_w.append(w)
         far_f.append(far)
@@ -581,7 +588,7 @@
             {
                 "tables": tables,
                 "col": docs[mbs, :, None],
-                "row": docs[mbs, None, :],
+                "row": [docs[mbs, None, BLK - HALF :], docs[mbs, None, :]],
                 "x": chain_rows(tok_own, i),
                 "blocks": tok_blocks[i],
                 "saved": [],
@@ -602,17 +609,18 @@
 
     def forward_attn(st, layer):
         windowed = layer % 2 == 0
-        w = attn_w[layer]
+        w3, wo = attn_w[layer]
         cos, sin = st["tables"][layer]
         a, qkv, lo, hi = call(
-            "qkv", qkv_body(layer, layer == 0, n, sub), ids, st["blocks"] + [gains, w, cos, sin],
+            "qkv", qkv_body(layer, layer == 0, n, sub), ids, st["blocks"] + [gains, w3, cos, sin],
             [out((rows, feat), BF), out((rows, 3 * hc), BF)] + [out((n * BLK, 2 * hc), BF)] * 2,
-            flops=2 * rows * feat * 3 * hc, after=[planes_f[0] if layer == 0 else far_f[layer]],
+            flops=2 * rows * feat * 3 * hc, after=[planes_f[0]] if layer == 0 else [],
         )
         lo, hi = step_z(lo, 1), step_z(hi, -1)
         ctx, *parts = call(
-            "attn", attn_body(windowed, n, sub), ids, [qkv, lo, hi, st["col"], st["row"], w],
+            "attn", attn_body(windowed, n, sub), ids, [qkv, lo, hi, st["col"], st["row"][layer % 2], wo],
             [out((rows, hc), BF)] + partial_out, [band] * 2, flops=4 * rows * feat * hc,
+            after=[far_f[layer]] if layer > 0 else [],
         )
         terms = fold(parts, "attn")
         mid, b = call(
@@ -635,7 +643,7 @@
             st["x"], a = call(
                 "next", resid_body(layer + 1), ids, [st["x"]] + terms + [gains],
                 [out((own, feat), F32), out((own, feat), BF)],
-                after=[attn_w[layer + 1], planes_f[layer + 1]],
+                after=[attn_w[layer + 1][0], planes_f[layer + 1]],
             )
             st["blocks"] = blocks_of(a)
         else:
@@ -686,9 +694,9 @@
 
     attn_parts, ffn_parts = [None] * layers, [None] * layers
     st = state[0]
-    wait_mlp, wait_fold, wait_mid = [], [], []
+    wait_mlp, wait_fold, wait_mid, wait_attn = [], [], [], []
     for layer in reversed(range(layers)):
-        w = attn_w[layer]
+        w3, wo = attn_w[layer]
         cos, sin = st["tables"][layer]
         x_in, a, qkv, lo, hi, ctx, mid, b, gu, hid = st["saved"][layer]
         dy, dgu, *parts = call(
@@ -707,7 +715,7 @@
         relayed = relay(pieces, "f" + str(layer))
         dm, dq, dkv, dlo, dhi = call(
             "attn_back", attn_back_body(layer % 2 == 0, n, sub), ids,
-            blocks_of(dmb) + [qkv, lo, hi, st["col"], st["row"], w, cos, sin],
+            blocks_of(dmb) + [qkv, lo, hi, st["col"], st["row"][layer % 2], wo, cos, sin],
             [out((rows, feat), BF), out((rows, hc), BF), out((rows, 2 * hc), F32)]
             + [out((n * BLK, 2 * hc), BF)] * 2,
             [band] * 2 + [pltpu.VMEM((rows, hc), BF), pltpu.VMEM((rows, hc), F32)] + [band32] * 2,
@@ -716,17 +724,20 @@
         from_next, from_prev = step_z(dlo, -1), step_z(dhi, 1)
         ffn_parts[layer] = z_sum(relayed, "f" + str(layer))
         dqkv, *parts = call(
-            "qkv_back", qkv_back_body(n, sub), ids, [dq, dkv, from_next, from_prev, w, cos, sin],
+            "qkv_back", qkv_back_body(n, sub), ids, [dq, dkv, from_next, from_prev, w3, cos, sin],
             [out((rows, 3 * hc), BF)] + partial_out, [pltpu.VMEM((rows, 2 * hc), F32)],
             flops=6 * rows * feat * hc,
-            after=ffn_parts[layer][:1] + ([st["x"]] if layer + 1 == layers else []),
+            after=ffn_parts[layer][:1] + wait_attn + ([st["x"]] if layer + 1 == layers else []),
         )
         pieces = weight_pieces([a, dqkv, dm, ctx], aw, "a" + str(layer))
         terms = fold(parts, "qkv_back", pieces if layer == 0 else [])
+        if layer == 0:
+            got = [pieces[0]] + [hop_z(pieces[s], s) for s in range(1, nz)]
+            pieces = got
         low = [out((own, feat), BF)] if layer > 0 else []
         dg, st["dy"], *dyb = call(
             "in_back", norm_back_body(layer), ids, terms + [x_in, dmid, gains],
-            [out((1, feat), F32), out((own, feat), F32)] + low, after=pieces + ffn_parts[layer],
+            [out((1, feat), F32), out((own, feat), F32)] + low, after=pieces,
         )
         add_gain(layer, dg)
         if layer > 0:
@@ -734,18 +745,17 @@
             relayed = relay(pieces, "a" + str(layer))
             attn_parts[layer] = z_sum(relayed, "a" + str(layer))
             wait_mlp = relayed[1:2]
-            wait_fold = attn_parts[layer][:1]
-            wait_mid = attn_parts[layer]
+            wait_fold = ffn_parts[layer]
+            wait_mid = attn_parts[layer][:1]
+            wait_attn = attn_parts[layer]
         else:
-            got = [pieces[0]] + [hop_z(pieces[s], s) for s in range(1, nz)]
             attn_parts[layer] = z_sum(got, "a" + str(layer))
 
     input_grad = join([st["dy"] for st in state], F32)
 
     dgain = jnp.concatenate(gain_rows + gain_rows, axis=0)[: 4 * layers]
     dgain = dgain + hop_core(dgain)
-    dgain = dgain + hop_team(dgain, 1)
-    dgain = dgain + hop_team(dgain, 2)
+    dgain = sum([dgain] + [hop_team(dgain, k) for k in range(1, TEAM)])
     dgain = sum([dgain] + [hop_z(dgain, s) for s in range(1, nz)])
     dgain = lax.dynamic_slice_in_dim(dgain, (z * TEAM + t) * d_rows, d_rows, axis=1)
 

time: 546 us -> 528 us (0.967)
  waiting for transfers between devices: 254 us -> 204 us
  starting transfers between devices: 159 us -> 178 us
  local copies, waits for them, and re-layouts: 13.2 us -> 23.9 us
    ppermute x74 -> x81, waiting for transfers between devices: 144 us -> 110 us  [hop_team(): return lax.ppermute(x, ('y', 'x'), [(i, i ^ k) for i in range(TEAM)])]
    ppermute x27 -> x33, waiting for transfers between devices: 89.6 us -> 75.9 us  [hop_z(): lax.ppermute(x, 'z', [(i, i ^ s if n == 4 else (i + s) % n) for i in rang...]
    unnamed x44 -> x80, local copies, waits for them, and re-layouts: 10.6 us -> 20.4 us
    ppermute x74 -> x81, starting transfers between devices: 87.5 us -> 96.6 us  [hop_team(): return lax.ppermute(x, ('y', 'x'), [(i, i ^ k) for i in range(TEAM)])]
    ppermute x8, starting transfers between devices: 16.4 us -> 23.3 us  [step_z(): lax.ppermute(x, 'z', [(i, i + by) for i in range(n) if 0 <= i + by < n])]
    ppermute x8, waiting for transfers between devices: 12.1 us -> 6.09 us  [step_z(): lax.ppermute(x, 'z', [(i, i + by) for i in range(n) if 0 <= i + by < n])]
    ppermute x27 -> x33, starting transfers between devices: 49.1 us -> 52.2 us  [hop_z(): lax.ppermute(x, 'z', [(i, i ^ s if n == 4 else (i + s) % n) for i in rang...]
    pallas_call x51 -> x54, Pallas kernels: 104 us -> 103 us  [call(): pl.pallas_call(kernel, name=name, in_specs=[pl.BlockSpec(memory_space=plt...]
  transfers between devices with their start and end apart: 152 -> 165, of which waited for: 58 -> 55; matrix products, arithmetic and copies ran while one was open for 1% -> 2% of each run, Pallas kernels for 12% -> 14%
where the time goes in v4:
time: 528 us; the launch traced here: 520 us
  waiting for transfers between devices  204 us (39%)
  starting transfers between devices  178 us (34%)
  Pallas kernels  103 us (20%)
  local copies, waits for them, and re-layouts  23.9 us (5%)
  other arithmetic  8.59 us (2%)
    ppermute x81, waiting for transfers between devices, hop_team(): return lax.ppermute(x, ('y', 'x'), [(i, i ^ k) for i in range(TEAM)])  110 us
    pallas_call x54, Pallas kernels, call(): pl.pallas_call(kernel, name=name, in_specs=[pl.BlockSpec(memory_space=plt...  103 us
    ppermute x81, starting transfers between devices, hop_team(): return lax.ppermute(x, ('y', 'x'), [(i, i ^ k) for i in range(TEAM)])  96.6 us
    ppermute x33, waiting for transfers between devices, hop_z(): lax.ppermute(x, 'z', [(i, i ^ s if n == 4 else (i + s) % n) for i in rang...  75.9 us
    ppermute x33, starting transfers between devices, hop_z(): lax.ppermute(x, 'z', [(i, i ^ s if n == 4 else (i + s) % n) for i in rang...  52.2 us
    ppermute x8, starting transfers between devices, step_z(): lax.ppermute(x, 'z', [(i, i + by) for i in range(n) if 0 <= i + by < n])  23.3 us
    unnamed x80, local copies, waits for them, and re-layouts  20.4 us
    ppermute x43, waiting for transfers between devices, hop_core(): return lax.ppermute(x, 'c', [(0, 1), (1, 0)])  11.9 us
  transfers between devices with their start and end apart: 165, of which 55 were waited for; matrix products, arithmetic and copies ran while one was open for 2% of the time, Pallas kernels for 14%

profile of v4, /device:TPU:0, one launch (start us, length us, event | category | flops | bytes accessed | tf_op | source)
XLA Modules:
  0.0 520.1 jit_solution(15770667963436175290)
XLA Ops:
  58.8 4.4 collective-permute-done.17.refs_3_
  82.2 4.3 collective-permute-done.23.refs_3_.refs_11_
  97.1 22.3 %collective-permute-done.42.refs_3_ = bf16[256,1152]{1,0:T(8,128)(2,1)S(1)} collective-permute-done((bf16[256,1152]{1,0:T(8,128)(2,1)S(1)}, bf16[256,1152]{1,0:T(8,128)(2,1)S(1)}, u32[]{:S(2)}, u32[]{:S(2)}) %collective-permute-start.42) | collective-permute-done | bytes 589856 | tf_op jit(solution)/shard_map/ppermute | solution.py:34
  123.9 6.7 %collective-permute-done.36.refs_4_ = bf16[128,1024]{1,0:T(8,128)(2,1)S(1)} collective-permute-done((bf16[128,1024]{1,0:T(8,128)(2,1)S(1)}, bf16[128,1024]{1,0:T(8,128)(2,1)S(1)}, u32[]{:S(2)}, u32[]{:S(2)}) %collective-permute-start.36) | collective-permute-done | bytes 262176 | tf_op jit(solution)/shard_map/ppermute | solution.py:25
  130.5 4.3 collective-permute-done.35.refs_3_
  136.7 4.1 mlp.2
  163.1 11.0 %collective-permute-done.52.refs_3_ = bf16[256,512]{1,0:T(8,128)(2,1)S(1)} collective-permute-done((bf16[256,512]{1,0:T(8,128)(2,1)S(1)}, bf16[256,512]{1,0:T(8,128)(2,1)S(1)}, u32[]{:S(2)}, u32[]{:S(2)}) %collective-permute-start.52) | collective-permute-done | bytes 262176 | tf_op jit(solution)/shard_map/ppermute | solution.py:34
  177.4 4.9 collective-permute-done.55.refs_3_
  188.8 3.9 collective-permute-done.59.refs_4_
  199.4 6.4 %collective-permute-start.64 = (bf16[256,256]{1,0:T(8,128)(2,1)S(1)}, bf16[256,256]{1,0:T(8,128)(2,1)S(1)}, u32[]{:S(2)}, u32[]{:S(2)}) collective-permute-start(bf16[256,256]{1,0:T(8,128)(2,1)S(1)} %get-tuple-element.206), channel_id=1, source_target_pairs={{0,8},{8,16},{16,24},{1,9},{9,17},{17,25},{2,10},{10,18},{18,26},{... | collective-permute-start | bytes 393224 | tf_op jit(solution)/shard_map/ppermute | solution.py:39
  207.4 8.3 %collective-permute-done.66.refs_7_.refs_3_ = bf16[256,1152]{1,0:T(8,128)(2,1)S(1)} collective-permute-done((bf16[256,1152]{1,0:T(8,128)(2,1)S(1)}, bf16[256,1152]{1,0:T(8,128)(2,1)S(1)}, u32[]{:S(2)}, u32[]{:S(2)}) %collective-permute-start.66) | collective-permute-done | bytes 589856 | tf_op jit(solution)/shard_map/ppermute | solution.py:34
  217.0 6.8 %attn.3 = (bf16[1024,128]{1,0:T(8,128)(2,1)S(1)}, bf16[512,1024]{1,0:T(8,128)(2,1)S(1)}, bf16[512,1024]{1,0:T(8,128)(2,1)S(1)}) custom-call(s32[3]{0:T(128)S(1)} %pad_add_fusion.refs_0_, bf16[1024,384]{1,0:T(8,128)(2,1)S(1)} %get-tuple-element.205.refs_1_.refs_9_, bf16[256,256]{1,0:T(8,128)(2,1)S(1)} %collective-permute-done.64.refs_2_.refs_10_, ...), custom_call_target="tpu_custom_call" | custom-call | flops 536870912 | bytes 4468736 | tf_op jit(solution)/shard_map/attn/pallas_call | solution.py:58
  237.5 10.8 %collective-permute-done.69.refs_4_ = bf16[128,1024]{1,0:T(8,128)(2,1)S(1)} collective-permute-done((bf16[128,1024]{1,0:T(8,128)(2,1)S(1)}, bf16[128,1024]{1,0:T(8,128)(2,1)S(1)}, u32[]{:S(2)}, u32[]{:S(2)}) %collective-permute-start.69) | collective-permute-done | bytes 262176 | tf_op jit(solution)/shard_map/ppermute | solution.py:25
  250.5 8.7 %collective-permute-done.86.refs_3_ = bf16[128,1024]{1,0:T(8,128)(2,1)S(1)} collective-permute-done((bf16[128,1024]{1,0:T(8,128)(2,1)S(1)}, bf16[128,1024]{1,0:T(8,128)(2,1)S(1)}, u32[]{:S(2)}, u32[]{:S(2)}) %collective-permute-start.86) | collective-permute-done | bytes 262176 | tf_op jit(solution)/shard_map/ppermute | solution.py:25
  260.4 6.6 %collective-permute-done.72.refs_3_ = bf16[128,1024]{1,0:T(8,128)(2,1)S(1)} collective-permute-done((bf16[128,1024]{1,0:T(8,128)(2,1)S(1)}, bf16[128,1024]{1,0:T(8,128)(2,1)S(1)}, u32[]{:S(2)}, u32[]{:S(2)}) %collective-permute-start.72) | collective-permute-done | bytes 262176 | tf_op jit(solution)/shard_map/ppermute | solution.py:25
  269.5 4.1 mlp.3
  278.8 4.2 mlp_back.2
  295.2 5.7 %collective-permute-done.93.refs_2_ = bf16[128,1024]{1,0:T(8,128)(2,1)S(1)} collective-permute-done((bf16[128,1024]{1,0:T(8,128)(2,1)S(1)}, bf16[128,1024]{1,0:T(8,128)(2,1)S(1)}, u32[]{:S(2)}, u32[]{:S(2)}) %collective-permute-start.93) | collective-permute-done | bytes 262176 | tf_op jit(solution)/shard_map/ppermute | solution.py:25
  300.9 5.4 %collective-permute-done.95.refs_4_ = bf16[128,1024]{1,0:T(8,128)(2,1)S(1)} collective-permute-done((bf16[128,1024]{1,0:T(8,128)(2,1)S(1)}, bf16[128,1024]{1,0:T(8,128)(2,1)S(1)}, u32[]{:S(2)}, u32[]{:S(2)}) %collective-permute-start.95) | collective-permute-done | bytes 262176 | tf_op jit(solution)/shard_map/ppermute | solution.py:25
  317.6 5.1 collective-permute-done.97.refs_3_
  327.5 10.0 %attn_back.2 = (bf16[1024,1024]{1,0:T(8,128)(2,1)S(1)}, bf16[1024,128]{1,0:T(8,128)(2,1)S(1)}, f32[1024,256]{1,0:T(8,128)S(1)}, bf16[256,256]{1,0:T(8,128)(2,1)S(1)}, bf16[256,256]{1,0:T(8,128)(2,1)S(1)}) custom-call(s32[3]{0:T(128)S(1)} %pad_add_fusion.refs_0_, bf16[128,1024]{1,0:T(8,128)(2,1)S(1)} %get-tuple-element.238.refs_1_, ...), custom_call_target="tpu_custom_call" | custom-call | flops 805306368 | bytes 8925184 | tf_op jit(solution)/shard_map/attn_back/pallas_call | solution.py:58
  360.7 5.6 %collective-permute-done.110.refs_3_ = bf16[128,1024]{1,0:T(8,128)(2,1)S(1)} collective-permute-done((bf16[128,1024]{1,0:T(8,128)(2,1)S(1)}, bf16[128,1024]{1,0:T(8,128)(2,1)S(1)}, u32[]{:S(2)}, u32[]{:S(2)}) %collective-permute-start.110) | collective-permute-done | bytes 262176 | tf_op jit(solution)/shard_map/ppermute | solution.py:25
  373.4 4.2 collective-permute-done.114.refs_4_
  383.0 4.1 mlp_back.3
  406.5 9.8 %collective-permute-done.128.refs_3_ = bf16[256,512]{1,0:T(8,128)(2,1)S(1)} collective-permute-done((bf16[256,512]{1,0:T(8,128)(2,1)S(1)}, bf16[256,512]{1,0:T(8,128)(2,1)S(1)}, u32[]{:S(2)}, u32[]{:S(2)}) %collective-permute-start.128) | collective-permute-done | bytes 262176 | tf_op jit(solution)/shard_map/ppermute | solution.py:34
  428.3 5.1 collective-permute-done.130.refs_3_
  435.3 8.7 %attn_back.3 = (bf16[1024,1024]{1,0:T(8,128)(2,1)S(1)}, bf16[1024,128]{1,0:T(8,128)(2,1)S(1)}, f32[1024,256]{1,0:T(8,128)S(1)}, bf16[256,256]{1,0:T(8,128)(2,1)S(1)}, bf16[256,256]{1,0:T(8,128)(2,1)S(1)}) custom-call(s32[3]{0:T(128)S(1)} %pad_add_fusion.refs_0_, bf16[128,1024]{1,0:T(8,128)(2,1)S(1)} %get-tuple-element.280.refs_1_, ...), custom_call_target="tpu_custom_call" | custom-call | flops 805306368 | bytes 8138240 | tf_op jit(solution)/shard_map/attn_back/pallas_call | solution.py:58
  445.4 6.6 %collective-permute-start.137 = (bf16[256,256]{1,0:T(8,128)(2,1)S(1)}, bf16[256,256]{1,0:T(8,128)(2,1)S(1)}, u32[]{:S(2)}, u32[]{:S(2)}) collective-permute-start(bf16[256,256]{1,0:T(8,128)(2,1)S(1)} %get-tuple-element.284), channel_id=1, source_target_pairs={{0,8},{8,16},{16,24},{1,9},{9,17},{17,25},{2,10},{10,18},{18,26},{... | collective-permute-start | bytes 393224 | tf_op jit(solution)/shard_map/ppermute | solution.py:39
  466.0 4.2 collective-permute-start.150
  473.0 5.6 %collective-permute-done.148.refs_9_.refs_2_ = bf16[256,512]{1,0:T(8,128)(2,1)S(1)} collective-permute-done((bf16[256,512]{1,0:T(8,128)(2,1)S(1)}, bf16[256,512]{1,0:T(8,128)(2,1)S(1)}, u32[]{:S(2)}, u32[]{:S(2)}) %collective-permute-start.148) | collective-permute-done | bytes 262176 | tf_op jit(solution)/shard_map/ppermute | solution.py:34
  479.9 7.3 %collective-permute-done.149.refs_10_.refs_3_ = bf16[256,512]{1,0:T(8,128)(2,1)S(1)} collective-permute-done((bf16[256,512]{1,0:T(8,128)(2,1)S(1)}, bf16[256,512]{1,0:T(8,128)(2,1)S(1)}, u32[]{:S(2)}, u32[]{:S(2)}) %collective-permute-start.149) | collective-permute-done | bytes 262176 | tf_op jit(solution)/shard_map/ppermute | solution.py:34
  506.1 5.9 %collective-permute-start.157 = (f32[8,1024]{1,0:T(8,128)S(1)}, f32[8,1024]{1,0:T(8,128)S(1)}, u32[]{:S(2)}, u32[]{:S(2)}) collective-permute-start(f32[8,1024]{1,0:T(8,128)S(1)} %add_add_fusion), channel_id=1, source_target_pairs={{0,16},{8,24},{16,0},{24,8},{1,17},{9,25},{17,1},{25,9},{2,18},{10... | collective-permute-start | bytes 98312 | tf_op jit(solution)/shard_map/ppermute | solution.py:34
  (464 shorter events, 303.1 us)
Async XLA Ops:
  4.5 27.3 %collective-permute-start.24 = (bf16[64,128]{1,0:T(8,128)(2,1)S(1)}, bf16[64,128]{1,0:T(8,128)(2,1)S(1)}, u32[]{:S(2)}, u32[]{:S(2)}) collective-permute-start(bf16[64,128]{1,0:T(8,128)(2,1)S(1)} %get-tuple-element.178), channel_id=1, source_target_pairs={{0,2},{2,0},{4,6},{6,4},{1,3},{3,1},{5,7},{7,5},{8,10},{10,8},{12,... | collective-permute-start | bytes 49160 | tf_op jit(solution)/shard_map/ppermute | solution.py:25
  7.5 28.0 %collective-permute-start.25 = (bf16[64,128]{1,0:T(8,128)(2,1)S(1)}, bf16[64,128]{1,0:T(8,128)(2,1)S(1)}, u32[]{:S(2)}, u32[]{:S(2)}) collective-permute-start(bf16[64,128]{1,0:T(8,128)(2,1)S(1)} %get-tuple-element.179), channel_id=1, source_target_pairs={{0,4},{2,6},{4,0},{6,2},{1,5},{3,7},{5,1},{7,3},{8,12},{10,14},{12... | collective-permute-start | bytes 49160 | tf_op jit(solution)/shard_map/ppermute | solution.py:25
  56.3 18.0 %collective-permute-start.8 = (bf16[128,1024]{1,0:T(8,128)(2,1)S(1)}, bf16[128,1024]{1,0:T(8,128)(2,1)S(1)}, u32[]{:S(2)}, u32[]{:S(2)}) collective-permute-start(bf16[128,1024]{1,0:T(8,128)(2,1)S(1)} %collective-permute-done.4.refs_3_), channel_id=1, source_target_pairs={{0,1},{1,0},{2,3},{3,2},{4,5},{5,4},{6,7},{7,6},{8,9},{9,8},{10,11... | collective-permute-start | bytes 786440 | tf_op jit(solution)/shard_map/ppermute | solution.py:29
  89.8 29.6 %collective-permute-start.42 = (bf16[256,1152]{1,0:T(8,128)(2,1)S(1)}, bf16[256,1152]{1,0:T(8,128)(2,1)S(1)}, u32[]{:S(2)}, u32[]{:S(2)}) collective-permute-start(bf16[256,1152]{1,0:T(8,128)(2,1)S(1)} %plane_f0.1.refs_13_.refs_1_), channel_id=1, source_target_pairs={{0,16},{8,24},{16,0},{24,8},{1,17},{9,25},{17,1},{25,9},{2,18},{10... | collective-permute-start | bytes 1769480 | tf_op jit(solution)/shard_map/ppermute | solution.py:34
  92.7 31.1 %collective-permute-start.41 = (bf16[256,1152]{1,0:T(8,128)(2,1)S(1)}, bf16[256,1152]{1,0:T(8,128)(2,1)S(1)}, u32[]{:S(2)}, u32[]{:S(2)}) collective-permute-start(bf16[256,1152]{1,0:T(8,128)(2,1)S(1)} %plane_f0.1.refs_13_.refs_1_), channel_id=1, source_target_pairs={{0,8},{8,0},{16,24},{24,16},{1,9},{9,1},{17,25},{25,17},{2,10},{10... | collective-permute-start | bytes 1769480 | tf_op jit(solution)/shard_map/ppermute | solution.py:34
  93.6 25.9 %collective-permute-start.31 = (bf16[128,1024]{1,0:T(8,128)(2,1)S(1)}, bf16[128,1024]{1,0:T(8,128)(2,1)S(1)}, u32[]{:S(2)}, u32[]{:S(2)}) collective-permute-start(bf16[128,1024]{1,0:T(8,128)(2,1)S(1)} %get-tuple-element.184), channel_id=1, source_target_pairs={{0,2},{2,0},{4,6},{6,4},{1,3},{3,1},{5,7},{7,5},{8,10},{10,8},{12,... | collective-permute-start | bytes 786440 | tf_op jit(solution)/shard_map/ppermute | solution.py:25
  94.9 24.5 %collective-permute-start.32 = (bf16[128,1024]{1,0:T(8,128)(2,1)S(1)}, bf16[128,1024]{1,0:T(8,128)(2,1)S(1)}, u32[]{:S(2)}, u32[]{:S(2)}) collective-permute-start(bf16[128,1024]{1,0:T(8,128)(2,1)S(1)} %get-tuple-element.185), channel_id=1, source_target_pairs={{0,4},{2,6},{4,0},{6,2},{1,5},{3,7},{5,1},{7,3},{8,12},{10,14},{12... | collective-permute-start | bytes 786440 | tf_op jit(solution)/shard_map/ppermute | solution.py:25
  96.6 22.8 %collective-permute-start.33 = (bf16[128,1024]{1,0:T(8,128)(2,1)S(1)}, bf16[128,1024]{1,0:T(8,128)(2,1)S(1)}, u32[]{:S(2)}, u32[]{:S(2)}) collective-permute-start(bf16[128,1024]{1,0:T(8,128)(2,1)S(1)} %get-tuple-element.186), channel_id=1, source_target_pairs={{0,6},{2,4},{4,2},{6,0},{1,7},{3,5},{5,3},{7,1},{8,14},{10,12},{12... | collective-permute-start | bytes 786440 | tf_op jit(solution)/shard_map/ppermute | solution.py:25
  150.7 23.4 %collective-permute-start.52 = (bf16[256,512]{1,0:T(8,128)(2,1)S(1)}, bf16[256,512]{1,0:T(8,128)(2,1)S(1)}, u32[]{:S(2)}, u32[]{:S(2)}) collective-permute-start(bf16[256,512]{1,0:T(8,128)(2,1)S(1)} %plane_a1.1.refs_1_), channel_id=1, source_target_pairs={{0,16},{8,24},{16,0},{24,8},{1,17},{9,25},{17,1},{25,9},{2,18},{10... | collective-permute-start | bytes 786440 | tf_op jit(solution)/shard_map/ppermute | solution.py:34
  152.4 22.7 %collective-permute-start.51 = (bf16[256,512]{1,0:T(8,128)(2,1)S(1)}, bf16[256,512]{1,0:T(8,128)(2,1)S(1)}, u32[]{:S(2)}, u32[]{:S(2)}) collective-permute-start(bf16[256,512]{1,0:T(8,128)(2,1)S(1)} %plane_a1.1.refs_1_), channel_id=1, source_target_pairs={{0,8},{8,0},{16,24},{24,16},{1,9},{9,1},{17,25},{25,17},{2,10},{10... | collective-permute-start | bytes 786440 | tf_op jit(solution)/shard_map/ppermute | solution.py:34
  155.6 27.3 %collective-permute-start.45 = (bf16[128,1024]{1,0:T(8,128)(2,1)S(1)}, bf16[128,1024]{1,0:T(8,128)(2,1)S(1)}, u32[]{:S(2)}, u32[]{:S(2)}) collective-permute-start(bf16[128,1024]{1,0:T(8,128)(2,1)S(1)} %get-tuple-element.192), channel_id=1, source_target_pairs={{0,2},{2,0},{4,6},{6,4},{1,3},{3,1},{5,7},{7,5},{8,10},{10,8},{12,... | collective-permute-start | bytes 786440 | tf_op jit(solution)/shard_map/ppermute | solution.py:25
  160.3 22.6 %collective-permute-start.46 = (bf16[128,1024]{1,0:T(8,128)(2,1)S(1)}, bf16[128,1024]{1,0:T(8,128)(2,1)S(1)}, u32[]{:S(2)}, u32[]{:S(2)}) collective-permute-start(bf16[128,1024]{1,0:T(8,128)(2,1)S(1)} %get-tuple-element.193), channel_id=1, source_target_pairs={{0,4},{2,6},{4,0},{6,2},{1,5},{3,7},{5,1},{7,3},{8,12},{10,14},{12... | collective-permute-start | bytes 786440 | tf_op jit(solution)/shard_map/ppermute | solution.py:25
  161.3 21.6 %collective-permute-start.47 = (bf16[128,1024]{1,0:T(8,128)(2,1)S(1)}, bf16[128,1024]{1,0:T(8,128)(2,1)S(1)}, u32[]{:S(2)}, u32[]{:S(2)}) collective-permute-start(bf16[128,1024]{1,0:T(8,128)(2,1)S(1)} %get-tuple-element.194), channel_id=1, source_target_pairs={{0,6},{2,4},{4,2},{6,0},{1,7},{3,5},{5,3},{7,1},{8,14},{10,12},{12... | collective-permute-start | bytes 786440 | tf_op jit(solution)/shard_map/ppermute | solution.py:25
  187.4 28.3 %collective-permute-start.66 = (bf16[256,1152]{1,0:T(8,128)(2,1)S(1)}, bf16[256,1152]{1,0:T(8,128)(2,1)S(1)}, u32[]{:S(2)}, u32[]{:S(2)}) collective-permute-start(bf16[256,1152]{1,0:T(8,128)(2,1)S(1)} %plane_f1.1.refs_8_.refs_1_), channel_id=1, source_target_pairs={{0,16},{8,24},{16,0},{24,8},{1,17},{9,25},{17,1},{25,9},{2,18},{10... | collective-permute-start | bytes 1769480 | tf_op jit(solution)/shard_map/ppermute | solution.py:34
  228.6 19.7 %collective-permute-start.69 = (bf16[128,1024]{1,0:T(8,128)(2,1)S(1)}, bf16[128,1024]{1,0:T(8,128)(2,1)S(1)}, u32[]{:S(2)}, u32[]{:S(2)}) collective-permute-start(bf16[128,1024]{1,0:T(8,128)(2,1)S(1)} %get-tuple-element.212), channel_id=1, source_target_pairs={{0,4},{2,6},{4,0},{6,2},{1,5},{3,7},{5,1},{7,3},{8,12},{10,14},{12... | collective-permute-start | bytes 786440 | tf_op jit(solution)/shard_map/ppermute | solution.py:25
  229.2 19.7 %collective-permute-start.70 = (bf16[128,1024]{1,0:T(8,128)(2,1)S(1)}, bf16[128,1024]{1,0:T(8,128)(2,1)S(1)}, u32[]{:S(2)}, u32[]{:S(2)}) collective-permute-start(bf16[128,1024]{1,0:T(8,128)(2,1)S(1)} %get-tuple-element.213), channel_id=1, source_target_pairs={{0,6},{2,4},{4,2},{6,0},{1,7},{3,5},{5,3},{7,1},{8,14},{10,12},{12... | collective-permute-start | bytes 786440 | tf_op jit(solution)/shard_map/ppermute | solution.py:25
  230.8 29.1 %collective-permute-start.78 = (bf16[256,1152]{1,0:T(8,128)(2,1)S(1)}, bf16[256,1152]{1,0:T(8,128)(2,1)S(1)}, u32[]{:S(2)}, u32[]{:S(2)}) collective-permute-start(bf16[256,1152]{1,0:T(8,128)(2,1)S(1)} %plane_f1.1.refs_8_.refs_1_), channel_id=1, source_target_pairs={{0,8},{8,0},{16,24},{24,16},{1,9},{9,1},{17,25},{25,17},{2,10},{10... | collective-permute-start | bytes 1769480 | tf_op jit(solution)/shard_map/ppermute | solution.py:34
  231.4 18.9 %collective-permute-start.87 = (bf16[128,1024]{1,0:T(8,128)(2,1)S(1)}, bf16[128,1024]{1,0:T(8,128)(2,1)S(1)}, u32[]{:S(2)}, u32[]{:S(2)}) collective-permute-start(bf16[128,1024]{1,0:T(8,128)(2,1)S(1)} %get-tuple-element.222.refs_1_.refs_6_), channel_id=1, source_target_pairs={{0,6},{2,4},{4,2},{6,0},{1,7},{3,5},{5,3},{7,1},{8,14},{10,12},{12... | collective-permute-start | bytes 786440 | tf_op jit(solution)/shard_map/ppermute | solution.py:25
  236.5 22.7 %collective-permute-start.86 = (bf16[128,1024]{1,0:T(8,128)(2,1)S(1)}, bf16[128,1024]{1,0:T(8,128)(2,1)S(1)}, u32[]{:S(2)}, u32[]{:S(2)}) collective-permute-start(bf16[128,1024]{1,0:T(8,128)(2,1)S(1)} %get-tuple-element.222.refs_1_.refs_6_), channel_id=1, source_target_pairs={{0,4},{2,6},{4,0},{6,2},{1,5},{3,7},{5,1},{7,3},{8,12},{10,14},{12... | collective-permute-start | bytes 786440 | tf_op jit(solution)/shard_map/ppermute | solution.py:25
  248.9 18.7 %collective-permute-start.79 = (bf16[256,1152]{1,0:T(8,128)(2,1)S(1)}, bf16[256,1152]{1,0:T(8,128)(2,1)S(1)}, u32[]{:S(2)}, u32[]{:S(2)}) collective-permute-start(bf16[256,1152]{1,0:T(8,128)(2,1)S(1)} %collective-permute-done.66.refs_7_.refs_3_), channel_id=1, source_target_pairs={{0,8},{8,0},{16,24},{24,16},{1,9},{9,1},{17,25},{25,17},{2,10},{10... | collective-permute-start | bytes 1769480 | tf_op jit(solution)/shard_map/ppermute | solution.py:34
  283.4 27.6 %collective-permute-start.80 = (bf16[512,1024]{1,0:T(8,128)(2,1)S(1)}, bf16[512,1024]{1,0:T(8,128)(2,1)S(1)}, u32[]{:S(2)}, u32[]{:S(2)}) collective-permute-start(bf16[512,1024]{1,0:T(8,128)(2,1)S(1)} %get-tuple-element.217), channel_id=1, source_target_pairs={{0,1},{1,0},{2,3},{3,2},{4,5},{5,4},{6,7},{7,6},{8,9},{9,8},{10,11... | collective-permute-start | bytes 3145736 | tf_op jit(solution)/shard_map/ppermute | solution.py:29
  290.2 19.9 %collective-permute-start.106 = (bf16[256,1152]{1,0:T(8,128)(2,1)S(1)}, bf16[256,1152]{1,0:T(8,128)(2,1)S(1)}, u32[]{:S(2)}, u32[]{:S(2)}) collective-permute-start(bf16[256,1152]{1,0:T(8,128)(2,1)S(1)} %get-tuple-element.237.refs_11_), channel_id=1, source_target_pairs={{0,8},{8,0},{16,24},{24,16},{1,9},{9,1},{17,25},{25,17},{2,10},{10... | collective-permute-start | bytes 1769480 | tf_op jit(solution)/shard_map/ppermute | solution.py:34
  311.0 26.6 %collective-permute-start.105 = (bf16[256,1152]{1,0:T(8,128)(2,1)S(1)}, bf16[256,1152]{1,0:T(8,128)(2,1)S(1)}, u32[]{:S(2)}, u32[]{:S(2)}) collective-permute-start(bf16[256,1152]{1,0:T(8,128)(2,1)S(1)} %get-tuple-element.235.refs_9_), channel_id=1, source_target_pairs={{0,8},{8,0},{16,24},{24,16},{1,9},{9,1},{17,25},{25,17},{2,10},{10... | collective-permute-start | bytes 1769480 | tf_op jit(solution)/shard_map/ppermute | solution.py:34
  313.1 28.2 %collective-permute-start.107 = (bf16[256,1152]{1,0:T(8,128)(2,1)S(1)}, bf16[256,1152]{1,0:T(8,128)(2,1)S(1)}, u32[]{:S(2)}, u32[]{:S(2)}) collective-permute-start(bf16[256,1152]{1,0:T(8,128)(2,1)S(1)} %relay_f1.1), channel_id=1, source_target_pairs={{0,16},{8,24},{16,0},{24,8},{1,17},{9,25},{17,1},{25,9},{2,18},{10... | collective-permute-start | bytes 1769480 | tf_op jit(solution)/shard_map/ppermute | solution.py:34
  324.0 20.8 %collective-permute-start.81 = (bf16[128,1024]{1,0:T(8,128)(2,1)S(1)}, bf16[128,1024]{1,0:T(8,128)(2,1)S(1)}, u32[]{:S(2)}, u32[]{:S(2)}) collective-permute-start(bf16[128,1024]{1,0:T(8,128)(2,1)S(1)} %get-tuple-element.219), channel_id=1, source_target_pairs={{0,2},{2,0},{4,6},{6,4},{1,3},{3,1},{5,7},{7,5},{8,10},{10,8},{12,... | collective-permute-start | bytes 786440 | tf_op jit(solution)/shard_map/ppermute | solution.py:25
  325.1 19.7 %collective-permute-start.82 = (bf16[128,1024]{1,0:T(8,128)(2,1)S(1)}, bf16[128,1024]{1,0:T(8,128)(2,1)S(1)}, u32[]{:S(2)}, u32[]{:S(2)}) collective-permute-start(bf16[128,1024]{1,0:T(8,128)(2,1)S(1)} %get-tuple-element.220), channel_id=1, source_target_pairs={{0,4},{2,6},{4,0},{6,2},{1,5},{3,7},{5,1},{7,3},{8,12},{10,14},{12... | collective-permute-start | bytes 786440 | tf_op jit(solution)/shard_map/ppermute | solution.py:25
  326.4 18.4 %collective-permute-start.83 = (bf16[128,1024]{1,0:T(8,128)(2,1)S(1)}, bf16[128,1024]{1,0:T(8,128)(2,1)S(1)}, u32[]{:S(2)}, u32[]{:S(2)}) collective-permute-start(bf16[128,1024]{1,0:T(8,128)(2,1)S(1)} %get-tuple-element.221), channel_id=1, source_target_pairs={{0,6},{2,4},{4,2},{6,0},{1,7},{3,5},{5,3},{7,1},{8,14},{10,12},{12... | collective-permute-start | bytes 786440 | tf_op jit(solution)/shard_map/ppermute | solution.py:25
  397.0 24.8 %collective-permute-start.139 = (bf16[256,1152]{1,0:T(8,128)(2,1)S(1)}, bf16[256,1152]{1,0:T(8,128)(2,1)S(1)}, u32[]{:S(2)}, u32[]{:S(2)}) collective-permute-start(bf16[256,1152]{1,0:T(8,128)(2,1)S(1)} %get-tuple-element.278.refs_11_), channel_id=1, source_target_pairs={{0,8},{8,0},{16,24},{24,16},{1,9},{9,1},{17,25},{25,17},{2,10},{10... | collective-permute-start | bytes 1769480 | tf_op jit(solution)/shard_map/ppermute | solution.py:34
  421.7 31.4 %collective-permute-start.138 = (bf16[256,1152]{1,0:T(8,128)(2,1)S(1)}, bf16[256,1152]{1,0:T(8,128)(2,1)S(1)}, u32[]{:S(2)}, u32[]{:S(2)}) collective-permute-start(bf16[256,1152]{1,0:T(8,128)(2,1)S(1)} %get-tuple-element.276.refs_9_), channel_id=1, source_target_pairs={{0,8},{8,0},{16,24},{24,16},{1,9},{9,1},{17,25},{25,17},{2,10},{10... | collective-permute-start | bytes 1769480 | tf_op jit(solution)/shard_map/ppermute | solution.py:34
  426.3 29.6 %collective-permute-start.140 = (bf16[256,1152]{1,0:T(8,128)(2,1)S(1)}, bf16[256,1152]{1,0:T(8,128)(2,1)S(1)}, u32[]{:S(2)}, u32[]{:S(2)}) collective-permute-start(bf16[256,1152]{1,0:T(8,128)(2,1)S(1)} %relay_f0.1), channel_id=1, source_target_pairs={{0,16},{8,24},{16,0},{24,8},{1,17},{9,25},{17,1},{25,9},{2,18},{10... | collective-permute-start | bytes 1769480 | tf_op jit(solution)/shard_map/ppermute | solution.py:34
  465.9 21.3 %collective-permute-start.149 = (bf16[256,512]{1,0:T(8,128)(2,1)S(1)}, bf16[256,512]{1,0:T(8,128)(2,1)S(1)}, u32[]{:S(2)}, u32[]{:S(2)}) collective-permute-start(bf16[256,512]{1,0:T(8,128)(2,1)S(1)} %get-tuple-element.297.refs_5_), channel_id=1, source_target_pairs={{0,16},{8,24},{16,0},{24,8},{1,17},{9,25},{17,1},{25,9},{2,18},{10... | collective-permute-start | bytes 786440 | tf_op jit(solution)/shard_map/ppermute | solution.py:34
  466.0 21.2 %collective-permute-start.150 = (bf16[256,512]{1,0:T(8,128)(2,1)S(1)}, bf16[256,512]{1,0:T(8,128)(2,1)S(1)}, u32[]{:S(2)}, u32[]{:S(2)}) collective-permute-start(bf16[256,512]{1,0:T(8,128)(2,1)S(1)} %get-tuple-element.298.refs_6_), channel_id=1, source_target_pairs={{0,24},{8,16},{16,8},{24,0},{1,25},{9,17},{17,9},{25,1},{2,26},{10... | collective-permute-start | bytes 786440 | tf_op jit(solution)/shard_map/ppermute | solution.py:34
  (173 other events, 1515.3 us)

commit v5 on v4

--- a/solution.py
+++ b/solution.py
@@ -63,7 +63,7 @@
         out_specs=[vmem] * len(outs),
         out_shape=list(outs),
         scratch_shapes=list(scratch),
-        compiler_params=pltpu.CompilerParams(vmem_limit_bytes=24 * 1024 * 1024),
+        compiler_params=pltpu.CompilerParams(vmem_limit_bytes=12 * 1024 * 1024),
         cost_estimate=pl.CostEstimate(flops=flops, bytes_accessed=moved, transcendentals=0),
     )(ids, *ins, *after)
     return list(results)

time: 528 us -> 520 us (0.985)
  local copies, waits for them, and re-layouts: 23.9 us -> 15.9 us
    unnamed x80 -> x64, local copies, waits for them, and re-layouts: 20.4 us -> 12.4 us
where the time goes in v5:
time: 520 us; the launch traced here: 512 us
  waiting for transfers between devices  204 us (39%)
  starting transfers between devices  178 us (34%)
  Pallas kernels  103 us (20%)
  local copies, waits for them, and re-layouts  15.9 us (3%)
  other arithmetic  8.59 us (2%)
    ppermute x81, waiting for transfers between devices, hop_team(): return lax.ppermute(x, ('y', 'x'), [(i, i ^ k) for i in range(TEAM)])  110 us
    pallas_call x54, Pallas kernels, call(): pl.pallas_call(kernel, name=name, in_specs=[pl.BlockSpec(memory_space=plt...  103 us
    ppermute x81, starting transfers between devices, hop_team(): return lax.ppermute(x, ('y', 'x'), [(i, i ^ k) for i in range(TEAM)])  96.8 us
    ppermute x33, waiting for transfers between devices, hop_z(): lax.ppermute(x, 'z', [(i, i ^ s if n == 4 else (i + s) % n) for i in rang...  75.8 us
    ppermute x33, starting transfers between devices, hop_z(): lax.ppermute(x, 'z', [(i, i ^ s if n == 4 else (i + s) % n) for i in rang...  52.2 us
    ppermute x8, starting transfers between devices, step_z(): lax.ppermute(x, 'z', [(i, i + by) for i in range(n) if 0 <= i + by < n])  23.3 us
    unnamed x64, local copies, waits for them, and re-layouts  12.4 us
    ppermute x43, waiting for transfers between devices, hop_core(): return lax.ppermute(x, 'c', [(0, 1), (1, 0)])  11.9 us
  transfers between devices with their start and end apart: 165, of which 55 were waited for; matrix products, arithmetic and copies ran while one was open for 2% of the time, Pallas kernels for 14%

profile of v5, /device:TPU:0, one launch (start us, length us, event | category | flops | bytes accessed | tf_op | source)
XLA Modules:
  0.0 512.2 jit_solution(11875259176032926613)
XLA Ops:
  58.8 4.4 collective-permute-done.17.refs_3_
  82.2 4.3 collective-permute-done.23.refs_3_.refs_11_
  97.1 22.3 %collective-permute-done.42.refs_3_ = bf16[256,1152]{1,0:T(8,128)(2,1)S(1)} collective-permute-done((bf16[256,1152]{1,0:T(8,128)(2,1)S(1)}, bf16[256,1152]{1,0:T(8,128)(2,1)S(1)}, u32[]{:S(2)}, u32[]{:S(2)}) %collective-permute-start.42) | collective-permute-done | bytes 589856 | tf_op jit(solution)/shard_map/ppermute | solution.py:34
  123.9 6.7 %collective-permute-done.36.refs_4_ = bf16[128,1024]{1,0:T(8,128)(2,1)S(1)} collective-permute-done((bf16[128,1024]{1,0:T(8,128)(2,1)S(1)}, bf16[128,1024]{1,0:T(8,128)(2,1)S(1)}, u32[]{:S(2)}, u32[]{:S(2)}) %collective-permute-start.36) | collective-permute-done | bytes 262176 | tf_op jit(solution)/shard_map/ppermute | solution.py:25
  130.5 4.3 collective-permute-done.35.refs_3_
  136.7 4.1 mlp.2
  163.1 11.0 %collective-permute-done.52.refs_3_ = bf16[256,512]{1,0:T(8,128)(2,1)S(1)} collective-permute-done((bf16[256,512]{1,0:T(8,128)(2,1)S(1)}, bf16[256,512]{1,0:T(8,128)(2,1)S(1)}, u32[]{:S(2)}, u32[]{:S(2)}) %collective-permute-start.52) | collective-permute-done | bytes 262176 | tf_op jit(solution)/shard_map/ppermute | solution.py:34
  177.4 4.9 collective-permute-done.55.refs_3_
  188.8 4.0 collective-permute-done.59.refs_4_
  199.5 6.4 %collective-permute-start.64 = (bf16[256,256]{1,0:T(8,128)(2,1)S(1)}, bf16[256,256]{1,0:T(8,128)(2,1)S(1)}, u32[]{:S(2)}, u32[]{:S(2)}) collective-permute-start(bf16[256,256]{1,0:T(8,128)(2,1)S(1)} %get-tuple-element.206), channel_id=1, source_target_pairs={{0,8},{8,16},{16,24},{1,9},{9,17},{17,25},{2,10},{10,18},{18,26},{... | collective-permute-start | bytes 393224 | tf_op jit(solution)/shard_map/ppermute | solution.py:39
  207.4 8.2 %collective-permute-done.66.refs_7_.refs_3_ = bf16[256,1152]{1,0:T(8,128)(2,1)S(1)} collective-permute-done((bf16[256,1152]{1,0:T(8,128)(2,1)S(1)}, bf16[256,1152]{1,0:T(8,128)(2,1)S(1)}, u32[]{:S(2)}, u32[]{:S(2)}) %collective-permute-start.66) | collective-permute-done | bytes 589856 | tf_op jit(solution)/shard_map/ppermute | solution.py:34
  216.9 6.8 %attn.3 = (bf16[1024,128]{1,0:T(8,128)(2,1)S(1)}, bf16[512,1024]{1,0:T(8,128)(2,1)S(1)}, bf16[512,1024]{1,0:T(8,128)(2,1)S(1)}) custom-call(s32[3]{0:T(128)S(1)} %pad_add_fusion.refs_0_, bf16[1024,384]{1,0:T(8,128)(2,1)S(1)} %get-tuple-element.205.refs_1_.refs_9_, bf16[256,256]{1,0:T(8,128)(2,1)S(1)} %collective-permute-done.64.refs_2_.refs_10_, ...), custom_call_target="tpu_custom_call" | custom-call | flops 536870912 | bytes 4468736 | tf_op jit(solution)/shard_map/attn/pallas_call | solution.py:58
  237.5 10.9 %collective-permute-done.69.refs_4_ = bf16[128,1024]{1,0:T(8,128)(2,1)S(1)} collective-permute-done((bf16[128,1024]{1,0:T(8,128)(2,1)S(1)}, bf16[128,1024]{1,0:T(8,128)(2,1)S(1)}, u32[]{:S(2)}, u32[]{:S(2)}) %collective-permute-start.69) | collective-permute-done | bytes 262176 | tf_op jit(solution)/shard_map/ppermute | solution.py:25
  250.7 8.4 %collective-permute-done.86.refs_3_ = bf16[128,1024]{1,0:T(8,128)(2,1)S(1)} collective-permute-done((bf16[128,1024]{1,0:T(8,128)(2,1)S(1)}, bf16[128,1024]{1,0:T(8,128)(2,1)S(1)}, u32[]{:S(2)}, u32[]{:S(2)}) %collective-permute-start.86) | collective-permute-done | bytes 262176 | tf_op jit(solution)/shard_map/ppermute | solution.py:25
  260.4 6.6 %collective-permute-done.72.refs_3_ = bf16[128,1024]{1,0:T(8,128)(2,1)S(1)} collective-permute-done((bf16[128,1024]{1,0:T(8,128)(2,1)S(1)}, bf16[128,1024]{1,0:T(8,128)(2,1)S(1)}, u32[]{:S(2)}, u32[]{:S(2)}) %collective-permute-start.72) | collective-permute-done | bytes 262176 | tf_op jit(solution)/shard_map/ppermute | solution.py:25
  269.5 4.1 mlp.3
  273.6 4.1 mlp_back.2
  287.3 5.7 %collective-permute-done.93.refs_2_ = bf16[128,1024]{1,0:T(8,128)(2,1)S(1)} collective-permute-done((bf16[128,1024]{1,0:T(8,128)(2,1)S(1)}, bf16[128,1024]{1,0:T(8,128)(2,1)S(1)}, u32[]{:S(2)}, u32[]{:S(2)}) %collective-permute-start.93) | collective-permute-done | bytes 262176 | tf_op jit(solution)/shard_map/ppermute | solution.py:25
  292.9 5.5 %collective-permute-done.95.refs_4_ = bf16[128,1024]{1,0:T(8,128)(2,1)S(1)} collective-permute-done((bf16[128,1024]{1,0:T(8,128)(2,1)S(1)}, bf16[128,1024]{1,0:T(8,128)(2,1)S(1)}, u32[]{:S(2)}, u32[]{:S(2)}) %collective-permute-start.95) | collective-permute-done | bytes 262176 | tf_op jit(solution)/shard_map/ppermute | solution.py:25
  309.7 5.1 collective-permute-done.97.refs_3_
  319.6 10.0 %attn_back.2 = (bf16[1024,1024]{1,0:T(8,128)(2,1)S(1)}, bf16[1024,128]{1,0:T(8,128)(2,1)S(1)}, f32[1024,256]{1,0:T(8,128)S(1)}, bf16[256,256]{1,0:T(8,128)(2,1)S(1)}, bf16[256,256]{1,0:T(8,128)(2,1)S(1)}) custom-call(s32[3]{0:T(128)S(1)} %pad_add_fusion.refs_0_, bf16[128,1024]{1,0:T(8,128)(2,1)S(1)} %get-tuple-element.238.refs_1_, ...), custom_call_target="tpu_custom_call" | custom-call | flops 805306368 | bytes 8925184 | tf_op jit(solution)/shard_map/attn_back/pallas_call | solution.py:58
  352.8 5.6 %collective-permute-done.110.refs_3_ = bf16[128,1024]{1,0:T(8,128)(2,1)S(1)} collective-permute-done((bf16[128,1024]{1,0:T(8,128)(2,1)S(1)}, bf16[128,1024]{1,0:T(8,128)(2,1)S(1)}, u32[]{:S(2)}, u32[]{:S(2)}) %collective-permute-start.110) | collective-permute-done | bytes 262176 | tf_op jit(solution)/shard_map/ppermute | solution.py:25
  365.5 4.2 collective-permute-done.114.refs_4_
  375.1 4.1 mlp_back.3
  398.6 9.8 %collective-permute-done.128.refs_3_ = bf16[256,512]{1,0:T(8,128)(2,1)S(1)} collective-permute-done((bf16[256,512]{1,0:T(8,128)(2,1)S(1)}, bf16[256,512]{1,0:T(8,128)(2,1)S(1)}, u32[]{:S(2)}, u32[]{:S(2)}) %collective-permute-start.128) | collective-permute-done | bytes 262176 | tf_op jit(solution)/shard_map/ppermute | solution.py:34
  420.4 5.1 collective-permute-done.130.refs_3_
  427.4 8.7 %attn_back.3 = (bf16[1024,1024]{1,0:T(8,128)(2,1)S(1)}, bf16[1024,128]{1,0:T(8,128)(2,1)S(1)}, f32[1024,256]{1,0:T(8,128)S(1)}, bf16[256,256]{1,0:T(8,128)(2,1)S(1)}, bf16[256,256]{1,0:T(8,128)(2,1)S(1)}) custom-call(s32[3]{0:T(128)S(1)} %pad_add_fusion.refs_0_, bf16[128,1024]{1,0:T(8,128)(2,1)S(1)} %get-tuple-element.280.refs_1_, ...), custom_call_target="tpu_custom_call" | custom-call | flops 805306368 | bytes 8138240 | tf_op jit(solution)/shard_map/attn_back/pallas_call | solution.py:58
  437.5 6.6 %collective-permute-start.137 = (bf16[256,256]{1,0:T(8,128)(2,1)S(1)}, bf16[256,256]{1,0:T(8,128)(2,1)S(1)}, u32[]{:S(2)}, u32[]{:S(2)}) collective-permute-start(bf16[256,256]{1,0:T(8,128)(2,1)S(1)} %get-tuple-element.284), channel_id=1, source_target_pairs={{0,8},{8,16},{16,24},{1,9},{9,17},{17,25},{2,10},{10,18},{18,26},{... | collective-permute-start | bytes 393224 | tf_op jit(solution)/shard_map/ppermute | solution.py:39
  458.1 4.2 collective-permute-start.150
  465.1 5.6 %collective-permute-done.148.refs_9_.refs_2_ = bf16[256,512]{1,0:T(8,128)(2,1)S(1)} collective-permute-done((bf16[256,512]{1,0:T(8,128)(2,1)S(1)}, bf16[256,512]{1,0:T(8,128)(2,1)S(1)}, u32[]{:S(2)}, u32[]{:S(2)}) %collective-permute-start.148) | collective-permute-done | bytes 262176 | tf_op jit(solution)/shard_map/ppermute | solution.py:34
  472.0 7.3 %collective-permute-done.149.refs_10_.refs_3_ = bf16[256,512]{1,0:T(8,128)(2,1)S(1)} collective-permute-done((bf16[256,512]{1,0:T(8,128)(2,1)S(1)}, bf16[256,512]{1,0:T(8,128)(2,1)S(1)}, u32[]{:S(2)}, u32[]{:S(2)}) %collective-permute-start.149) | collective-permute-done | bytes 262176 | tf_op jit(solution)/shard_map/ppermute | solution.py:34
  498.2 5.9 %collective-permute-start.157 = (f32[8,1024]{1,0:T(8,128)S(1)}, f32[8,1024]{1,0:T(8,128)S(1)}, u32[]{:S(2)}, u32[]{:S(2)}) collective-permute-start(f32[8,1024]{1,0:T(8,128)S(1)} %add_add_fusion), channel_id=1, source_target_pairs={{0,16},{8,24},{16,0},{24,8},{1,17},{9,25},{17,1},{25,9},{2,18},{10... | collective-permute-start | bytes 98312 | tf_op jit(solution)/shard_map/ppermute | solution.py:34
  (448 shorter events, 295.4 us)
Async XLA Ops:
  4.5 27.3 %collective-permute-start.24 = (bf16[64,128]{1,0:T(8,128)(2,1)S(1)}, bf16[64,128]{1,0:T(8,128)(2,1)S(1)}, u32[]{:S(2)}, u32[]{:S(2)}) collective-permute-start(bf16[64,128]{1,0:T(8,128)(2,1)S(1)} %get-tuple-element.178), channel_id=1, source_target_pairs={{0,2},{2,0},{4,6},{6,4},{1,3},{3,1},{5,7},{7,5},{8,10},{10,8},{12,... | collective-permute-start | bytes 49160 | tf_op jit(solution)/shard_map/ppermute | solution.py:25
  7.5 28.0 %collective-permute-start.25 = (bf16[64,128]{1,0:T(8,128)(2,1)S(1)}, bf16[64,128]{1,0:T(8,128)(2,1)S(1)}, u32[]{:S(2)}, u32[]{:S(2)}) collective-permute-start(bf16[64,128]{1,0:T(8,128)(2,1)S(1)} %get-tuple-element.179), channel_id=1, source_target_pairs={{0,4},{2,6},{4,0},{6,2},{1,5},{3,7},{5,1},{7,3},{8,12},{10,14},{12... | collective-permute-start | bytes 49160 | tf_op jit(solution)/shard_map/ppermute | solution.py:25
  56.3 18.0 %collective-permute-start.8 = (bf16[128,1024]{1,0:T(8,128)(2,1)S(1)}, bf16[128,1024]{1,0:T(8,128)(2,1)S(1)}, u32[]{:S(2)}, u32[]{:S(2)}) collective-permute-start(bf16[128,1024]{1,0:T(8,128)(2,1)S(1)} %collective-permute-done.4.refs_3_), channel_id=1, source_target_pairs={{0,1},{1,0},{2,3},{3,2},{4,5},{5,4},{6,7},{7,6},{8,9},{9,8},{10,11... | collective-permute-start | bytes 786440 | tf_op jit(solution)/shard_map/ppermute | solution.py:29
  89.8 29.6 %collective-permute-start.42 = (bf16[256,1152]{1,0:T(8,128)(2,1)S(1)}, bf16[256,1152]{1,0:T(8,128)(2,1)S(1)}, u32[]{:S(2)}, u32[]{:S(2)}) collective-permute-start(bf16[256,1152]{1,0:T(8,128)(2,1)S(1)} %plane_f0.1.refs_13_.refs_1_), channel_id=1, source_target_pairs={{0,16},{8,24},{16,0},{24,8},{1,17},{9,25},{17,1},{25,9},{2,18},{10... | collective-permute-start | bytes 1769480 | tf_op jit(solution)/shard_map/ppermute | solution.py:34
  92.7 31.1 %collective-permute-start.41 = (bf16[256,1152]{1,0:T(8,128)(2,1)S(1)}, bf16[256,1152]{1,0:T(8,128)(2,1)S(1)}, u32[]{:S(2)}, u32[]{:S(2)}) collective-permute-start(bf16[256,1152]{1,0:T(8,128)(2,1)S(1)} %plane_f0.1.refs_13_.refs_1_), channel_id=1, source_target_pairs={{0,8},{8,0},{16,24},{24,16},{1,9},{9,1},{17,25},{25,17},{2,10},{10... | collective-permute-start | bytes 1769480 | tf_op jit(solution)/shard_map/ppermute | solution.py:34
  93.6 25.9 %collective-permute-start.31 = (bf16[128,1024]{1,0:T(8,128)(2,1)S(1)}, bf16[128,1024]{1,0:T(8,128)(2,1)S(1)}, u32[]{:S(2)}, u32[]{:S(2)}) collective-permute-start(bf16[128,1024]{1,0:T(8,128)(2,1)S(1)} %get-tuple-element.184), channel_id=1, source_target_pairs={{0,2},{2,0},{4,6},{6,4},{1,3},{3,1},{5,7},{7,5},{8,10},{10,8},{12,... | collective-permute-start | bytes 786440 | tf_op jit(solution)/shard_map/ppermute | solution.py:25
  94.9 24.5 %collective-permute-start.32 = (bf16[128,1024]{1,0:T(8,128)(2,1)S(1)}, bf16[128,1024]{1,0:T(8,128)(2,1)S(1)}, u32[]{:S(2)}, u32[]{:S(2)}) collective-permute-start(bf16[128,1024]{1,0:T(8,128)(2,1)S(1)} %get-tuple-element.185), channel_id=1, source_target_pairs={{0,4},{2,6},{4,0},{6,2},{1,5},{3,7},{5,1},{7,3},{8,12},{10,14},{12... | collective-permute-start | bytes 786440 | tf_op jit(solution)/shard_map/ppermute | solution.py:25
  96.6 22.8 %collective-permute-start.33 = (bf16[128,1024]{1,0:T(8,128)(2,1)S(1)}, bf16[128,1024]{1,0:T(8,128)(2,1)S(1)}, u32[]{:S(2)}, u32[]{:S(2)}) collective-permute-start(bf16[128,1024]{1,0:T(8,128)(2,1)S(1)} %get-tuple-element.186), channel_id=1, source_target_pairs={{0,6},{2,4},{4,2},{6,0},{1,7},{3,5},{5,3},{7,1},{8,14},{10,12},{12... | collective-permute-start | bytes 786440 | tf_op jit(solution)/shard_map/ppermute | solution.py:25
  150.7 23.4 %collective-permute-start.52 = (bf16[256,512]{1,0:T(8,128)(2,1)S(1)}, bf16[256,512]{1,0:T(8,128)(2,1)S(1)}, u32[]{:S(2)}, u32[]{:S(2)}) collective-permute-start(bf16[256,512]{1,0:T(8,128)(2,1)S(1)} %plane_a1.1.refs_1_), channel_id=1, source_target_pairs={{0,16},{8,24},{16,0},{24,8},{1,17},{9,25},{17,1},{25,9},{2,18},{10... | collective-permute-start | bytes 786440 | tf_op jit(solution)/shard_map/ppermute | solution.py:34
  152.4 22.7 %collective-permute-start.51 = (bf16[256,512]{1,0:T(8,128)(2,1)S(1)}, bf16[256,512]{1,0:T(8,128)(2,1)S(1)}, u32[]{:S(2)}, u32[]{:S(2)}) collective-permute-start(bf16[256,512]{1,0:T(8,128)(2,1)S(1)} %plane_a1.1.refs_1_), channel_id=1, source_target_pairs={{0,8},{8,0},{16,24},{24,16},{1,9},{9,1},{17,25},{25,17},{2,10},{10... | collective-permute-start | bytes 786440 | tf_op jit(solution)/shard_map/ppermute | solution.py:34
  155.6 27.3 %collective-permute-start.45 = (bf16[128,1024]{1,0:T(8,128)(2,1)S(1)}, bf16[128,1024]{1,0:T(8,128)(2,1)S(1)}, u32[]{:S(2)}, u32[]{:S(2)}) collective-permute-start(bf16[128,1024]{1,0:T(8,128)(2,1)S(1)} %get-tuple-element.192), channel_id=1, source_target_pairs={{0,2},{2,0},{4,6},{6,4},{1,3},{3,1},{5,7},{7,5},{8,10},{10,8},{12,... | collective-permute-start | bytes 786440 | tf_op jit(solution)/shard_map/ppermute | solution.py:25
  160.3 22.6 %collective-permute-start.46 = (bf16[128,1024]{1,0:T(8,128)(2,1)S(1)}, bf16[128,1024]{1,0:T(8,128)(2,1)S(1)}, u32[]{:S(2)}, u32[]{:S(2)}) collective-permute-start(bf16[128,1024]{1,0:T(8,128)(2,1)S(1)} %get-tuple-element.193), channel_id=1, source_target_pairs={{0,4},{2,6},{4,0},{6,2},{1,5},{3,7},{5,1},{7,3},{8,12},{10,14},{12... | collective-permute-start | bytes 786440 | tf_op jit(solution)/shard_map/ppermute | solution.py:25
  161.3 21.6 %collective-permute-start.47 = (bf16[128,1024]{1,0:T(8,128)(2,1)S(1)}, bf16[128,1024]{1,0:T(8,128)(2,1)S(1)}, u32[]{:S(2)}, u32[]{:S(2)}) collective-permute-start(bf16[128,1024]{1,0:T(8,128)(2,1)S(1)} %get-tuple-element.194), channel_id=1, source_target_pairs={{0,6},{2,4},{4,2},{6,0},{1,7},{3,5},{5,3},{7,1},{8,14},{10,12},{12... | collective-permute-start | bytes 786440 | tf_op jit(solution)/shard_map/ppermute | solution.py:25
  187.4 28.3 %collective-permute-start.66 = (bf16[256,1152]{1,0:T(8,128)(2,1)S(1)}, bf16[256,1152]{1,0:T(8,128)(2,1)S(1)}, u32[]{:S(2)}, u32[]{:S(2)}) collective-permute-start(bf16[256,1152]{1,0:T(8,128)(2,1)S(1)} %plane_f1.1.refs_8_.refs_1_), channel_id=1, source_target_pairs={{0,16},{8,24},{16,0},{24,8},{1,17},{9,25},{17,1},{25,9},{2,18},{10... | collective-permute-start | bytes 1769480 | tf_op jit(solution)/shard_map/ppermute | solution.py:34
  228.6 19.7 %collective-permute-start.69 = (bf16[128,1024]{1,0:T(8,128)(2,1)S(1)}, bf16[128,1024]{1,0:T(8,128)(2,1)S(1)}, u32[]{:S(2)}, u32[]{:S(2)}) collective-permute-start(bf16[128,1024]{1,0:T(8,128)(2,1)S(1)} %get-tuple-element.212), channel_id=1, source_target_pairs={{0,4},{2,6},{4,0},{6,2},{1,5},{3,7},{5,1},{7,3},{8,12},{10,14},{12... | collective-permute-start | bytes 786440 | tf_op jit(solution)/shard_map/ppermute | solution.py:25
  229.2 19.7 %collective-permute-start.70 = (bf16[128,1024]{1,0:T(8,128)(2,1)S(1)}, bf16[128,1024]{1,0:T(8,128)(2,1)S(1)}, u32[]{:S(2)}, u32[]{:S(2)}) collective-permute-start(bf16[128,1024]{1,0:T(8,128)(2,1)S(1)} %get-tuple-element.213), channel_id=1, source_target_pairs={{0,6},{2,4},{4,2},{6,0},{1,7},{3,5},{5,3},{7,1},{8,14},{10,12},{12... | collective-permute-start | bytes 786440 | tf_op jit(solution)/shard_map/ppermute | solution.py:25
  230.8 29.1 %collective-permute-start.78 = (bf16[256,1152]{1,0:T(8,128)(2,1)S(1)}, bf16[256,1152]{1,0:T(8,128)(2,1)S(1)}, u32[]{:S(2)}, u32[]{:S(2)}) collective-permute-start(bf16[256,1152]{1,0:T(8,128)(2,1)S(1)} %plane_f1.1.refs_8_.refs_1_), channel_id=1, source_target_pairs={{0,8},{8,0},{16,24},{24,16},{1,9},{9,1},{17,25},{25,17},{2,10},{10... | collective-permute-start | bytes 1769480 | tf_op jit(solution)/shard_map/ppermute | solution.py:34
  231.4 18.9 %collective-permute-start.87 = (bf16[128,1024]{1,0:T(8,128)(2,1)S(1)}, bf16[128,1024]{1,0:T(8,128)(2,1)S(1)}, u32[]{:S(2)}, u32[]{:S(2)}) collective-permute-start(bf16[128,1024]{1,0:T(8,128)(2,1)S(1)} %get-tuple-element.222.refs_1_.refs_6_), channel_id=1, source_target_pairs={{0,6},{2,4},{4,2},{6,0},{1,7},{3,5},{5,3},{7,1},{8,14},{10,12},{12... | collective-permute-start | bytes 786440 | tf_op jit(solution)/shard_map/ppermute | solution.py:25
  236.5 22.7 %collective-permute-start.86 = (bf16[128,1024]{1,0:T(8,128)(2,1)S(1)}, bf16[128,1024]{1,0:T(8,128)(2,1)S(1)}, u32[]{:S(2)}, u32[]{:S(2)}) collective-permute-start(bf16[128,1024]{1,0:T(8,128)(2,1)S(1)} %get-tuple-element.222.refs_1_.refs_6_), channel_id=1, source_target_pairs={{0,4},{2,6},{4,0},{6,2},{1,5},{3,7},{5,1},{7,3},{8,12},{10,14},{12... | collective-permute-start | bytes 786440 | tf_op jit(solution)/shard_map/ppermute | solution.py:25
  248.8 18.7 %collective-permute-start.79 = (bf16[256,1152]{1,0:T(8,128)(2,1)S(1)}, bf16[256,1152]{1,0:T(8,128)(2,1)S(1)}, u32[]{:S(2)}, u32[]{:S(2)}) collective-permute-start(bf16[256,1152]{1,0:T(8,128)(2,1)S(1)} %collective-permute-done.66.refs_7_.refs_3_), channel_id=1, source_target_pairs={{0,8},{8,0},{16,24},{24,16},{1,9},{9,1},{17,25},{25,17},{2,10},{10... | collective-permute-start | bytes 1769480 | tf_op jit(solution)/shard_map/ppermute | solution.py:34
  278.1 25.0 %collective-permute-start.80 = (bf16[512,1024]{1,0:T(8,128)(2,1)S(1)}, bf16[512,1024]{1,0:T(8,128)(2,1)S(1)}, u32[]{:S(2)}, u32[]{:S(2)}) collective-permute-start(bf16[512,1024]{1,0:T(8,128)(2,1)S(1)} %get-tuple-element.217), channel_id=1, source_target_pairs={{0,1},{1,0},{2,3},{3,2},{4,5},{5,4},{6,7},{7,6},{8,9},{9,8},{10,11... | collective-permute-start | bytes 3145736 | tf_op jit(solution)/shard_map/ppermute | solution.py:29
  282.2 19.9 %collective-permute-start.106 = (bf16[256,1152]{1,0:T(8,128)(2,1)S(1)}, bf16[256,1152]{1,0:T(8,128)(2,1)S(1)}, u32[]{:S(2)}, u32[]{:S(2)}) collective-permute-start(bf16[256,1152]{1,0:T(8,128)(2,1)S(1)} %get-tuple-element.237.refs_11_), channel_id=1, source_target_pairs={{0,8},{8,0},{16,24},{24,16},{1,9},{9,1},{17,25},{25,17},{2,10},{10... | collective-permute-start | bytes 1769480 | tf_op jit(solution)/shard_map/ppermute | solution.py:34
  303.1 26.6 %collective-permute-start.105 = (bf16[256,1152]{1,0:T(8,128)(2,1)S(1)}, bf16[256,1152]{1,0:T(8,128)(2,1)S(1)}, u32[]{:S(2)}, u32[]{:S(2)}) collective-permute-start(bf16[256,1152]{1,0:T(8,128)(2,1)S(1)} %get-tuple-element.235.refs_9_), channel_id=1, source_target_pairs={{0,8},{8,0},{16,24},{24,16},{1,9},{9,1},{17,25},{25,17},{2,10},{10... | collective-permute-start | bytes 1769480 | tf_op jit(solution)/shard_map/ppermute | solution.py:34
  305.2 28.2 %collective-permute-start.107 = (bf16[256,1152]{1,0:T(8,128)(2,1)S(1)}, bf16[256,1152]{1,0:T(8,128)(2,1)S(1)}, u32[]{:S(2)}, u32[]{:S(2)}) collective-permute-start(bf16[256,1152]{1,0:T(8,128)(2,1)S(1)} %relay_f1.1), channel_id=1, source_target_pairs={{0,16},{8,24},{16,0},{24,8},{1,17},{9,25},{17,1},{25,9},{2,18},{10... | collective-permute-start | bytes 1769480 | tf_op jit(solution)/shard_map/ppermute | solution.py:34
  316.1 20.8 %collective-permute-start.81 = (bf16[128,1024]{1,0:T(8,128)(2,1)S(1)}, bf16[128,1024]{1,0:T(8,128)(2,1)S(1)}, u32[]{:S(2)}, u32[]{:S(2)}) collective-permute-start(bf16[128,1024]{1,0:T(8,128)(2,1)S(1)} %get-tuple-element.219), channel_id=1, source_target_pairs={{0,2},{2,0},{4,6},{6,4},{1,3},{3,1},{5,7},{7,5},{8,10},{10,8},{12,... | collective-permute-start | bytes 786440 | tf_op jit(solution)/shard_map/ppermute | solution.py:25
  317.2 19.7 %collective-permute-start.82 = (bf16[128,1024]{1,0:T(8,128)(2,1)S(1)}, bf16[128,1024]{1,0:T(8,128)(2,1)S(1)}, u32[]{:S(2)}, u32[]{:S(2)}) collective-permute-start(bf16[128,1024]{1,0:T(8,128)(2,1)S(1)} %get-tuple-element.220), channel_id=1, source_target_pairs={{0,4},{2,6},{4,0},{6,2},{1,5},{3,7},{5,1},{7,3},{8,12},{10,14},{12... | collective-permute-start | bytes 786440 | tf_op jit(solution)/shard_map/ppermute | solution.py:25
  318.5 18.5 %collective-permute-start.83 = (bf16[128,1024]{1,0:T(8,128)(2,1)S(1)}, bf16[128,1024]{1,0:T(8,128)(2,1)S(1)}, u32[]{:S(2)}, u32[]{:S(2)}) collective-permute-start(bf16[128,1024]{1,0:T(8,128)(2,1)S(1)} %get-tuple-element.221), channel_id=1, source_target_pairs={{0,6},{2,4},{4,2},{6,0},{1,7},{3,5},{5,3},{7,1},{8,14},{10,12},{12... | collective-permute-start | bytes 786440 | tf_op jit(solution)/shard_map/ppermute | solution.py:25
  389.1 24.8 %collective-permute-start.139 = (bf16[256,1152]{1,0:T(8,128)(2,1)S(1)}, bf16[256,1152]{1,0:T(8,128)(2,1)S(1)}, u32[]{:S(2)}, u32[]{:S(2)}) collective-permute-start(bf16[256,1152]{1,0:T(8,128)(2,1)S(1)} %get-tuple-element.278.refs_11_), channel_id=1, source_target_pairs={{0,8},{8,0},{16,24},{24,16},{1,9},{9,1},{17,25},{25,17},{2,10},{10... | collective-permute-start | bytes 1769480 | tf_op jit(solution)/shard_map/ppermute | solution.py:34
  413.8 31.4 %collective-permute-start.138 = (bf16[256,1152]{1,0:T(8,128)(2,1)S(1)}, bf16[256,1152]{1,0:T(8,128)(2,1)S(1)}, u32[]{:S(2)}, u32[]{:S(2)}) collective-permute-start(bf16[256,1152]{1,0:T(8,128)(2,1)S(1)} %get-tuple-element.276.refs_9_), channel_id=1, source_target_pairs={{0,8},{8,0},{16,24},{24,16},{1,9},{9,1},{17,25},{25,17},{2,10},{10... | collective-permute-start | bytes 1769480 | tf_op jit(solution)/shard_map/ppermute | solution.py:34
  418.3 29.6 %collective-permute-start.140 = (bf16[256,1152]{1,0:T(8,128)(2,1)S(1)}, bf16[256,1152]{1,0:T(8,128)(2,1)S(1)}, u32[]{:S(2)}, u32[]{:S(2)}) collective-permute-start(bf16[256,1152]{1,0:T(8,128)(2,1)S(1)} %relay_f0.1), channel_id=1, source_target_pairs={{0,16},{8,24},{16,0},{24,8},{1,17},{9,25},{17,1},{25,9},{2,18},{10... | collective-permute-start | bytes 1769480 | tf_op jit(solution)/shard_map/ppermute | solution.py:34
  458.0 21.3 %collective-permute-start.149 = (bf16[256,512]{1,0:T(8,128)(2,1)S(1)}, bf16[256,512]{1,0:T(8,128)(2,1)S(1)}, u32[]{:S(2)}, u32[]{:S(2)}) collective-permute-start(bf16[256,512]{1,0:T(8,128)(2,1)S(1)} %get-tuple-element.297.refs_5_), channel_id=1, source_target_pairs={{0,16},{8,24},{16,0},{24,8},{1,17},{9,25},{17,1},{25,9},{2,18},{10... | collective-permute-start | bytes 786440 | tf_op jit(solution)/shard_map/ppermute | solution.py:34
  458.1 21.2 %collective-permute-start.150 = (bf16[256,512]{1,0:T(8,128)(2,1)S(1)}, bf16[256,512]{1,0:T(8,128)(2,1)S(1)}, u32[]{:S(2)}, u32[]{:S(2)}) collective-permute-start(bf16[256,512]{1,0:T(8,128)(2,1)S(1)} %get-tuple-element.298.refs_6_), channel_id=1, source_target_pairs={{0,24},{8,16},{16,8},{24,0},{1,25},{9,17},{17,9},{25,1},{2,26},{10... | collective-permute-start | bytes 786440 | tf_op jit(solution)/shard_map/ppermute | solution.py:34
  (165 other events, 1461.7 us)

commit v6 on v5

--- a/solution.py
+++ b/solution.py
@@ -63,7 +63,7 @@
         out_specs=[vmem] * len(outs),
         out_shape=list(outs),
         scratch_shapes=list(scratch),
-        compiler_params=pltpu.CompilerParams(vmem_limit_bytes=12 * 1024 * 1024),
+        compiler_params=pltpu.CompilerParams(vmem_limit_bytes=8 * 1024 * 1024),
         cost_estimate=pl.CostEstimate(flops=flops, bytes_accessed=moved, transcendentals=0),
     )(ids, *ins, *after)
     return list(results)

time: 520 us -> 520 us (level)
  no operation moved by 1% of the time
where the time goes in v6:
time: 520 us; the launch traced here: 512 us
  waiting for transfers between devices  204 us (39%)
  starting transfers between devices  179 us (34%)
  Pallas kernels  103 us (20%)
  local copies, waits for them, and re-layouts  15.9 us (3%)
  other arithmetic  8.59 us (2%)
    ppermute x81, waiting for transfers between devices, hop_team(): return lax.ppermute(x, ('y', 'x'), [(i, i ^ k) for i in range(TEAM)])  110 us
    pallas_call x54, Pallas kernels, call(): pl.pallas_call(kernel, name=name, in_specs=[pl.BlockSpec(memory_space=plt...  103 us
    ppermute x81, starting transfers between devices, hop_team(): return lax.ppermute(x, ('y', 'x'), [(i, i ^ k) for i in range(TEAM)])  96.7 us
    ppermute x33, waiting for transfers between devices, hop_z(): lax.ppermute(x, 'z', [(i, i ^ s if n == 4 else (i + s) % n) for i in rang...  75.8 us
    ppermute x33, starting transfers between devices, hop_z(): lax.ppermute(x, 'z', [(i, i ^ s if n == 4 else (i + s) % n) for i in rang...  52.3 us
    ppermute x8, starting transfers between devices, step_z(): lax.ppermute(x, 'z', [(i, i + by) for i in range(n) if 0 <= i + by < n])  23.3 us
    unnamed x64, local copies, waits for them, and re-layouts  12.4 us
    ppermute x43, waiting for transfers between devices, hop_core(): return lax.ppermute(x, 'c', [(0, 1), (1, 0)])  11.9 us
  transfers between devices with their start and end apart: 165, of which 55 were waited for; matrix products, arithmetic and copies ran while one was open for 2% of the time, Pallas kernels for 14%

profile of v6, /device:TPU:0, one launch (start us, length us, event | category | flops | bytes accessed | tf_op | source)
XLA Modules:
  0.0 512.2 jit_solution(15934506804095185027)
XLA Ops:
  58.8 4.4 collective-permute-done.17.refs_3_
  82.2 4.3 collective-permute-done.23.refs_3_.refs_11_
  97.1 22.3 %collective-permute-done.42.refs_3_ = bf16[256,1152]{1,0:T(8,128)(2,1)S(1)} collective-permute-done((bf16[256,1152]{1,0:T(8,128)(2,1)S(1)}, bf16[256,1152]{1,0:T(8,128)(2,1)S(1)}, u32[]{:S(2)}, u32[]{:S(2)}) %collective-permute-start.42) | collective-permute-done | bytes 589856 | tf_op jit(solution)/shard_map/ppermute | solution.py:34
  123.9 6.6 %collective-permute-done.36.refs_4_ = bf16[128,1024]{1,0:T(8,128)(2,1)S(1)} collective-permute-done((bf16[128,1024]{1,0:T(8,128)(2,1)S(1)}, bf16[128,1024]{1,0:T(8,128)(2,1)S(1)}, u32[]{:S(2)}, u32[]{:S(2)}) %collective-permute-start.36) | collective-permute-done | bytes 262176 | tf_op jit(solution)/shard_map/ppermute | solution.py:25
  130.5 4.4 collective-permute-done.35.refs_3_
  136.8 4.1 mlp.2
  163.1 11.0 %collective-permute-done.52.refs_3_ = bf16[256,512]{1,0:T(8,128)(2,1)S(1)} collective-permute-done((bf16[256,512]{1,0:T(8,128)(2,1)S(1)}, bf16[256,512]{1,0:T(8,128)(2,1)S(1)}, u32[]{:S(2)}, u32[]{:S(2)}) %collective-permute-start.52) | collective-permute-done | bytes 262176 | tf_op jit(solution)/shard_map/ppermute | solution.py:34
  177.5 4.9 collective-permute-done.55.refs_3_
  188.8 4.0 collective-permute-done.59.refs_4_
  199.5 6.4 %collective-permute-start.64 = (bf16[256,256]{1,0:T(8,128)(2,1)S(1)}, bf16[256,256]{1,0:T(8,128)(2,1)S(1)}, u32[]{:S(2)}, u32[]{:S(2)}) collective-permute-start(bf16[256,256]{1,0:T(8,128)(2,1)S(1)} %get-tuple-element.206), channel_id=1, source_target_pairs={{0,8},{8,16},{16,24},{1,9},{9,17},{17,25},{2,10},{10,18},{18,26},{... | collective-permute-start | bytes 393224 | tf_op jit(solution)/shard_map/ppermute | solution.py:39
  207.4 8.2 %collective-permute-done.66.refs_7_.refs_3_ = bf16[256,1152]{1,0:T(8,128)(2,1)S(1)} collective-permute-done((bf16[256,1152]{1,0:T(8,128)(2,1)S(1)}, bf16[256,1152]{1,0:T(8,128)(2,1)S(1)}, u32[]{:S(2)}, u32[]{:S(2)}) %collective-permute-start.66) | collective-permute-done | bytes 589856 | tf_op jit(solution)/shard_map/ppermute | solution.py:34
  216.9 6.8 %attn.3 = (bf16[1024,128]{1,0:T(8,128)(2,1)S(1)}, bf16[512,1024]{1,0:T(8,128)(2,1)S(1)}, bf16[512,1024]{1,0:T(8,128)(2,1)S(1)}) custom-call(s32[3]{0:T(128)S(1)} %pad_add_fusion.refs_0_, bf16[1024,384]{1,0:T(8,128)(2,1)S(1)} %get-tuple-element.205.refs_1_.refs_9_, bf16[256,256]{1,0:T(8,128)(2,1)S(1)} %collective-permute-done.64.refs_2_.refs_10_, ...), custom_call_target="tpu_custom_call" | custom-call | flops 536870912 | bytes 4468736 | tf_op jit(solution)/shard_map/attn/pallas_call | solution.py:58
  237.5 10.8 %collective-permute-done.69.refs_4_ = bf16[128,1024]{1,0:T(8,128)(2,1)S(1)} collective-permute-done((bf16[128,1024]{1,0:T(8,128)(2,1)S(1)}, bf16[128,1024]{1,0:T(8,128)(2,1)S(1)}, u32[]{:S(2)}, u32[]{:S(2)}) %collective-permute-start.69) | collective-permute-done | bytes 262176 | tf_op jit(solution)/shard_map/ppermute | solution.py:25
  250.7 8.5 %collective-permute-done.86.refs_3_ = bf16[128,1024]{1,0:T(8,128)(2,1)S(1)} collective-permute-done((bf16[128,1024]{1,0:T(8,128)(2,1)S(1)}, bf16[128,1024]{1,0:T(8,128)(2,1)S(1)}, u32[]{:S(2)}, u32[]{:S(2)}) %collective-permute-start.86) | collective-permute-done | bytes 262176 | tf_op jit(solution)/shard_map/ppermute | solution.py:25
  260.4 6.6 %collective-permute-done.72.refs_3_ = bf16[128,1024]{1,0:T(8,128)(2,1)S(1)} collective-permute-done((bf16[128,1024]{1,0:T(8,128)(2,1)S(1)}, bf16[128,1024]{1,0:T(8,128)(2,1)S(1)}, u32[]{:S(2)}, u32[]{:S(2)}) %collective-permute-start.72) | collective-permute-done | bytes 262176 | tf_op jit(solution)/shard_map/ppermute | solution.py:25
  269.4 4.1 mlp.3
  273.6 4.1 mlp_back.2
  287.2 5.7 %collective-permute-done.93.refs_2_ = bf16[128,1024]{1,0:T(8,128)(2,1)S(1)} collective-permute-done((bf16[128,1024]{1,0:T(8,128)(2,1)S(1)}, bf16[128,1024]{1,0:T(8,128)(2,1)S(1)}, u32[]{:S(2)}, u32[]{:S(2)}) %collective-permute-start.93) | collective-permute-done | bytes 262176 | tf_op jit(solution)/shard_map/ppermute | solution.py:25
  292.9 5.4 %collective-permute-done.95.refs_4_ = bf16[128,1024]{1,0:T(8,128)(2,1)S(1)} collective-permute-done((bf16[128,1024]{1,0:T(8,128)(2,1)S(1)}, bf16[128,1024]{1,0:T(8,128)(2,1)S(1)}, u32[]{:S(2)}, u32[]{:S(2)}) %collective-permute-start.95) | collective-permute-done | bytes 262176 | tf_op jit(solution)/shard_map/ppermute | solution.py:25
  309.6 5.1 collective-permute-done.97.refs_3_
  319.6 10.0 %attn_back.2 = (bf16[1024,1024]{1,0:T(8,128)(2,1)S(1)}, bf16[1024,128]{1,0:T(8,128)(2,1)S(1)}, f32[1024,256]{1,0:T(8,128)S(1)}, bf16[256,256]{1,0:T(8,128)(2,1)S(1)}, bf16[256,256]{1,0:T(8,128)(2,1)S(1)}) custom-call(s32[3]{0:T(128)S(1)} %pad_add_fusion.refs_0_, bf16[128,1024]{1,0:T(8,128)(2,1)S(1)} %get-tuple-element.238.refs_1_, ...), custom_call_target="tpu_custom_call" | custom-call | flops 805306368 | bytes 8925184 | tf_op jit(solution)/shard_map/attn_back/pallas_call | solution.py:58
  352.8 5.6 %collective-permute-done.110.refs_3_ = bf16[128,1024]{1,0:T(8,128)(2,1)S(1)} collective-permute-done((bf16[128,1024]{1,0:T(8,128)(2,1)S(1)}, bf16[128,1024]{1,0:T(8,128)(2,1)S(1)}, u32[]{:S(2)}, u32[]{:S(2)}) %collective-permute-start.110) | collective-permute-done | bytes 262176 | tf_op jit(solution)/shard_map/ppermute | solution.py:25
  365.5 4.2 collective-permute-done.114.refs_4_
  375.1 4.1 mlp_back.3
  398.7 9.7 %collective-permute-done.128.refs_3_ = bf16[256,512]{1,0:T(8,128)(2,1)S(1)} collective-permute-done((bf16[256,512]{1,0:T(8,128)(2,1)S(1)}, bf16[256,512]{1,0:T(8,128)(2,1)S(1)}, u32[]{:S(2)}, u32[]{:S(2)}) %collective-permute-start.128) | collective-permute-done | bytes 262176 | tf_op jit(solution)/shard_map/ppermute | solution.py:34
  420.4 5.1 collective-permute-done.130.refs_3_
  427.4 8.7 %attn_back.3 = (bf16[1024,1024]{1,0:T(8,128)(2,1)S(1)}, bf16[1024,128]{1,0:T(8,128)(2,1)S(1)}, f32[1024,256]{1,0:T(8,128)S(1)}, bf16[256,256]{1,0:T(8,128)(2,1)S(1)}, bf16[256,256]{1,0:T(8,128)(2,1)S(1)}) custom-call(s32[3]{0:T(128)S(1)} %pad_add_fusion.refs_0_, bf16[128,1024]{1,0:T(8,128)(2,1)S(1)} %get-tuple-element.280.refs_1_, ...), custom_call_target="tpu_custom_call" | custom-call | flops 805306368 | bytes 8138240 | tf_op jit(solution)/shard_map/attn_back/pallas_call | solution.py:58
  437.5 6.7 %collective-permute-start.137 = (bf16[256,256]{1,0:T(8,128)(2,1)S(1)}, bf16[256,256]{1,0:T(8,128)(2,1)S(1)}, u32[]{:S(2)}, u32[]{:S(2)}) collective-permute-start(bf16[256,256]{1,0:T(8,128)(2,1)S(1)} %get-tuple-element.284), channel_id=1, source_target_pairs={{0,8},{8,16},{16,24},{1,9},{9,17},{17,25},{2,10},{10,18},{18,26},{... | collective-permute-start | bytes 393224 | tf_op jit(solution)/shard_map/ppermute | solution.py:39
  458.1 4.3 collective-permute-start.150
  465.2 5.5 %collective-permute-done.148.refs_9_.refs_2_ = bf16[256,512]{1,0:T(8,128)(2,1)S(1)} collective-permute-done((bf16[256,512]{1,0:T(8,128)(2,1)S(1)}, bf16[256,512]{1,0:T(8,128)(2,1)S(1)}, u32[]{:S(2)}, u32[]{:S(2)}) %collective-permute-start.148) | collective-permute-done | bytes 262176 | tf_op jit(solution)/shard_map/ppermute | solution.py:34
  472.0 7.4 %collective-permute-done.149.refs_10_.refs_3_ = bf16[256,512]{1,0:T(8,128)(2,1)S(1)} collective-permute-done((bf16[256,512]{1,0:T(8,128)(2,1)S(1)}, bf16[256,512]{1,0:T(8,128)(2,1)S(1)}, u32[]{:S(2)}, u32[]{:S(2)}) %collective-permute-start.149) | collective-permute-done | bytes 262176 | tf_op jit(solution)/shard_map/ppermute | solution.py:34
  498.3 5.9 %collective-permute-start.157 = (f32[8,1024]{1,0:T(8,128)S(1)}, f32[8,1024]{1,0:T(8,128)S(1)}, u32[]{:S(2)}, u32[]{:S(2)}) collective-permute-start(f32[8,1024]{1,0:T(8,128)S(1)} %add_add_fusion), channel_id=1, source_target_pairs={{0,16},{8,24},{16,0},{24,8},{1,17},{9,25},{17,1},{25,9},{2,18},{10... | collective-permute-start | bytes 98312 | tf_op jit(solution)/shard_map/ppermute | solution.py:34
  (448 shorter events, 295.3 us)
Async XLA Ops:
  4.5 27.3 %collective-permute-start.24 = (bf16[64,128]{1,0:T(8,128)(2,1)S(1)}, bf16[64,128]{1,0:T(8,128)(2,1)S(1)}, u32[]{:S(2)}, u32[]{:S(2)}) collective-permute-start(bf16[64,128]{1,0:T(8,128)(2,1)S(1)} %get-tuple-element.178), channel_id=1, source_target_pairs={{0,2},{2,0},{4,6},{6,4},{1,3},{3,1},{5,7},{7,5},{8,10},{10,8},{12,... | collective-permute-start | bytes 49160 | tf_op jit(solution)/shard_map/ppermute | solution.py:25
  7.5 28.0 %collective-permute-start.25 = (bf16[64,128]{1,0:T(8,128)(2,1)S(1)}, bf16[64,128]{1,0:T(8,128)(2,1)S(1)}, u32[]{:S(2)}, u32[]{:S(2)}) collective-permute-start(bf16[64,128]{1,0:T(8,128)(2,1)S(1)} %get-tuple-element.179), channel_id=1, source_target_pairs={{0,4},{2,6},{4,0},{6,2},{1,5},{3,7},{5,1},{7,3},{8,12},{10,14},{12... | collective-permute-start | bytes 49160 | tf_op jit(solution)/shard_map/ppermute | solution.py:25
  56.3 18.0 %collective-permute-start.8 = (bf16[128,1024]{1,0:T(8,128)(2,1)S(1)}, bf16[128,1024]{1,0:T(8,128)(2,1)S(1)}, u32[]{:S(2)}, u32[]{:S(2)}) collective-permute-start(bf16[128,1024]{1,0:T(8,128)(2,1)S(1)} %collective-permute-done.4.refs_3_), channel_id=1, source_target_pairs={{0,1},{1,0},{2,3},{3,2},{4,5},{5,4},{6,7},{7,6},{8,9},{9,8},{10,11... | collective-permute-start | bytes 786440 | tf_op jit(solution)/shard_map/ppermute | solution.py:29
  89.8 29.6 %collective-permute-start.42 = (bf16[256,1152]{1,0:T(8,128)(2,1)S(1)}, bf16[256,1152]{1,0:T(8,128)(2,1)S(1)}, u32[]{:S(2)}, u32[]{:S(2)}) collective-permute-start(bf16[256,1152]{1,0:T(8,128)(2,1)S(1)} %plane_f0.1.refs_13_.refs_1_), channel_id=1, source_target_pairs={{0,16},{8,24},{16,0},{24,8},{1,17},{9,25},{17,1},{25,9},{2,18},{10... | collective-permute-start | bytes 1769480 | tf_op jit(solution)/shard_map/ppermute | solution.py:34
  92.7 31.1 %collective-permute-start.41 = (bf16[256,1152]{1,0:T(8,128)(2,1)S(1)}, bf16[256,1152]{1,0:T(8,128)(2,1)S(1)}, u32[]{:S(2)}, u32[]{:S(2)}) collective-permute-start(bf16[256,1152]{1,0:T(8,128)(2,1)S(1)} %plane_f0.1.refs_13_.refs_1_), channel_id=1, source_target_pairs={{0,8},{8,0},{16,24},{24,16},{1,9},{9,1},{17,25},{25,17},{2,10},{10... | collective-permute-start | bytes 1769480 | tf_op jit(solution)/shard_map/ppermute | solution.py:34
  93.6 25.9 %collective-permute-start.31 = (bf16[128,1024]{1,0:T(8,128)(2,1)S(1)}, bf16[128,1024]{1,0:T(8,128)(2,1)S(1)}, u32[]{:S(2)}, u32[]{:S(2)}) collective-permute-start(bf16[128,1024]{1,0:T(8,128)(2,1)S(1)} %get-tuple-element.184), channel_id=1, source_target_pairs={{0,2},{2,0},{4,6},{6,4},{1,3},{3,1},{5,7},{7,5},{8,10},{10,8},{12,... | collective-permute-start | bytes 786440 | tf_op jit(solution)/shard_map/ppermute | solution.py:25
  94.9 24.5 %collective-permute-start.32 = (bf16[128,1024]{1,0:T(8,128)(2,1)S(1)}, bf16[128,1024]{1,0:T(8,128)(2,1)S(1)}, u32[]{:S(2)}, u32[]{:S(2)}) collective-permute-start(bf16[128,1024]{1,0:T(8,128)(2,1)S(1)} %get-tuple-element.185), channel_id=1, source_target_pairs={{0,4},{2,6},{4,0},{6,2},{1,5},{3,7},{5,1},{7,3},{8,12},{10,14},{12... | collective-permute-start | bytes 786440 | tf_op jit(solution)/shard_map/ppermute | solution.py:25
  96.6 22.8 %collective-permute-start.33 = (bf16[128,1024]{1,0:T(8,128)(2,1)S(1)}, bf16[128,1024]{1,0:T(8,128)(2,1)S(1)}, u32[]{:S(2)}, u32[]{:S(2)}) collective-permute-start(bf16[128,1024]{1,0:T(8,128)(2,1)S(1)} %get-tuple-element.186), channel_id=1, source_target_pairs={{0,6},{2,4},{4,2},{6,0},{1,7},{3,5},{5,3},{7,1},{8,14},{10,12},{12... | collective-permute-start | bytes 786440 | tf_op jit(solution)/shard_map/ppermute | solution.py:25
  150.7 23.5 %collective-permute-start.52 = (bf16[256,512]{1,0:T(8,128)(2,1)S(1)}, bf16[256,512]{1,0:T(8,128)(2,1)S(1)}, u32[]{:S(2)}, u32[]{:S(2)}) collective-permute-start(bf16[256,512]{1,0:T(8,128)(2,1)S(1)} %plane_a1.1.refs_1_), channel_id=1, source_target_pairs={{0,16},{8,24},{16,0},{24,8},{1,17},{9,25},{17,1},{25,9},{2,18},{10... | collective-permute-start | bytes 786440 | tf_op jit(solution)/shard_map/ppermute | solution.py:34
  152.4 22.7 %collective-permute-start.51 = (bf16[256,512]{1,0:T(8,128)(2,1)S(1)}, bf16[256,512]{1,0:T(8,128)(2,1)S(1)}, u32[]{:S(2)}, u32[]{:S(2)}) collective-permute-start(bf16[256,512]{1,0:T(8,128)(2,1)S(1)} %plane_a1.1.refs_1_), channel_id=1, source_target_pairs={{0,8},{8,0},{16,24},{24,16},{1,9},{9,1},{17,25},{25,17},{2,10},{10... | collective-permute-start | bytes 786440 | tf_op jit(solution)/shard_map/ppermute | solution.py:34
  155.7 27.3 %collective-permute-start.45 = (bf16[128,1024]{1,0:T(8,128)(2,1)S(1)}, bf16[128,1024]{1,0:T(8,128)(2,1)S(1)}, u32[]{:S(2)}, u32[]{:S(2)}) collective-permute-start(bf16[128,1024]{1,0:T(8,128)(2,1)S(1)} %get-tuple-element.192), channel_id=1, source_target_pairs={{0,2},{2,0},{4,6},{6,4},{1,3},{3,1},{5,7},{7,5},{8,10},{10,8},{12,... | collective-permute-start | bytes 786440 | tf_op jit(solution)/shard_map/ppermute | solution.py:25
  160.4 22.6 %collective-permute-start.46 = (bf16[128,1024]{1,0:T(8,128)(2,1)S(1)}, bf16[128,1024]{1,0:T(8,128)(2,1)S(1)}, u32[]{:S(2)}, u32[]{:S(2)}) collective-permute-start(bf16[128,1024]{1,0:T(8,128)(2,1)S(1)} %get-tuple-element.193), channel_id=1, source_target_pairs={{0,4},{2,6},{4,0},{6,2},{1,5},{3,7},{5,1},{7,3},{8,12},{10,14},{12... | collective-permute-start | bytes 786440 | tf_op jit(solution)/shard_map/ppermute | solution.py:25
  161.4 21.6 %collective-permute-start.47 = (bf16[128,1024]{1,0:T(8,128)(2,1)S(1)}, bf16[128,1024]{1,0:T(8,128)(2,1)S(1)}, u32[]{:S(2)}, u32[]{:S(2)}) collective-permute-start(bf16[128,1024]{1,0:T(8,128)(2,1)S(1)} %get-tuple-element.194), channel_id=1, source_target_pairs={{0,6},{2,4},{4,2},{6,0},{1,7},{3,5},{5,3},{7,1},{8,14},{10,12},{12... | collective-permute-start | bytes 786440 | tf_op jit(solution)/shard_map/ppermute | solution.py:25
  187.4 28.2 %collective-permute-start.66 = (bf16[256,1152]{1,0:T(8,128)(2,1)S(1)}, bf16[256,1152]{1,0:T(8,128)(2,1)S(1)}, u32[]{:S(2)}, u32[]{:S(2)}) collective-permute-start(bf16[256,1152]{1,0:T(8,128)(2,1)S(1)} %plane_f1.1.refs_8_.refs_1_), channel_id=1, source_target_pairs={{0,16},{8,24},{16,0},{24,8},{1,17},{9,25},{17,1},{25,9},{2,18},{10... | collective-permute-start | bytes 1769480 | tf_op jit(solution)/shard_map/ppermute | solution.py:34
  228.6 19.7 %collective-permute-start.69 = (bf16[128,1024]{1,0:T(8,128)(2,1)S(1)}, bf16[128,1024]{1,0:T(8,128)(2,1)S(1)}, u32[]{:S(2)}, u32[]{:S(2)}) collective-permute-start(bf16[128,1024]{1,0:T(8,128)(2,1)S(1)} %get-tuple-element.212), channel_id=1, source_target_pairs={{0,4},{2,6},{4,0},{6,2},{1,5},{3,7},{5,1},{7,3},{8,12},{10,14},{12... | collective-permute-start | bytes 786440 | tf_op jit(solution)/shard_map/ppermute | solution.py:25
  229.2 19.7 %collective-permute-start.70 = (bf16[128,1024]{1,0:T(8,128)(2,1)S(1)}, bf16[128,1024]{1,0:T(8,128)(2,1)S(1)}, u32[]{:S(2)}, u32[]{:S(2)}) collective-permute-start(bf16[128,1024]{1,0:T(8,128)(2,1)S(1)} %get-tuple-element.213), channel_id=1, source_target_pairs={{0,6},{2,4},{4,2},{6,0},{1,7},{3,5},{5,3},{7,1},{8,14},{10,12},{12... | collective-permute-start | bytes 786440 | tf_op jit(solution)/shard_map/ppermute | solution.py:25
  230.8 29.1 %collective-permute-start.78 = (bf16[256,1152]{1,0:T(8,128)(2,1)S(1)}, bf16[256,1152]{1,0:T(8,128)(2,1)S(1)}, u32[]{:S(2)}, u32[]{:S(2)}) collective-permute-start(bf16[256,1152]{1,0:T(8,128)(2,1)S(1)} %plane_f1.1.refs_8_.refs_1_), channel_id=1, source_target_pairs={{0,8},{8,0},{16,24},{24,16},{1,9},{9,1},{17,25},{25,17},{2,10},{10... | collective-permute-start | bytes 1769480 | tf_op jit(solution)/shard_map/ppermute | solution.py:34
  231.4 18.9 %collective-permute-start.87 = (bf16[128,1024]{1,0:T(8,128)(2,1)S(1)}, bf16[128,1024]{1,0:T(8,128)(2,1)S(1)}, u32[]{:S(2)}, u32[]{:S(2)}) collective-permute-start(bf16[128,1024]{1,0:T(8,128)(2,1)S(1)} %get-tuple-element.222.refs_1_.refs_6_), channel_id=1, source_target_pairs={{0,6},{2,4},{4,2},{6,0},{1,7},{3,5},{5,3},{7,1},{8,14},{10,12},{12... | collective-permute-start | bytes 786440 | tf_op jit(solution)/shard_map/ppermute | solution.py:25
  236.5 22.7 %collective-permute-start.86 = (bf16[128,1024]{1,0:T(8,128)(2,1)S(1)}, bf16[128,1024]{1,0:T(8,128)(2,1)S(1)}, u32[]{:S(2)}, u32[]{:S(2)}) collective-permute-start(bf16[128,1024]{1,0:T(8,128)(2,1)S(1)} %get-tuple-element.222.refs_1_.refs_6_), channel_id=1, source_target_pairs={{0,4},{2,6},{4,0},{6,2},{1,5},{3,7},{5,1},{7,3},{8,12},{10,14},{12... | collective-permute-start | bytes 786440 | tf_op jit(solution)/shard_map/ppermute | solution.py:25
  248.8 18.7 %collective-permute-start.79 = (bf16[256,1152]{1,0:T(8,128)(2,1)S(1)}, bf16[256,1152]{1,0:T(8,128)(2,1)S(1)}, u32[]{:S(2)}, u32[]{:S(2)}) collective-permute-start(bf16[256,1152]{1,0:T(8,128)(2,1)S(1)} %collective-permute-done.66.refs_7_.refs_3_), channel_id=1, source_target_pairs={{0,8},{8,0},{16,24},{24,16},{1,9},{9,1},{17,25},{25,17},{2,10},{10... | collective-permute-start | bytes 1769480 | tf_op jit(solution)/shard_map/ppermute | solution.py:34
  278.2 24.9 %collective-permute-start.80 = (bf16[512,1024]{1,0:T(8,128)(2,1)S(1)}, bf16[512,1024]{1,0:T(8,128)(2,1)S(1)}, u32[]{:S(2)}, u32[]{:S(2)}) collective-permute-start(bf16[512,1024]{1,0:T(8,128)(2,1)S(1)} %get-tuple-element.217), channel_id=1, source_target_pairs={{0,1},{1,0},{2,3},{3,2},{4,5},{5,4},{6,7},{7,6},{8,9},{9,8},{10,11... | collective-permute-start | bytes 3145736 | tf_op jit(solution)/shard_map/ppermute | solution.py:29
  282.3 19.8 %collective-permute-start.106 = (bf16[256,1152]{1,0:T(8,128)(2,1)S(1)}, bf16[256,1152]{1,0:T(8,128)(2,1)S(1)}, u32[]{:S(2)}, u32[]{:S(2)}) collective-permute-start(bf16[256,1152]{1,0:T(8,128)(2,1)S(1)} %get-tuple-element.237.refs_11_), channel_id=1, source_target_pairs={{0,8},{8,0},{16,24},{24,16},{1,9},{9,1},{17,25},{25,17},{2,10},{10... | collective-permute-start | bytes 1769480 | tf_op jit(solution)/shard_map/ppermute | solution.py:34
  303.1 26.6 %collective-permute-start.105 = (bf16[256,1152]{1,0:T(8,128)(2,1)S(1)}, bf16[256,1152]{1,0:T(8,128)(2,1)S(1)}, u32[]{:S(2)}, u32[]{:S(2)}) collective-permute-start(bf16[256,1152]{1,0:T(8,128)(2,1)S(1)} %get-tuple-element.235.refs_9_), channel_id=1, source_target_pairs={{0,8},{8,0},{16,24},{24,16},{1,9},{9,1},{17,25},{25,17},{2,10},{10... | collective-permute-start | bytes 1769480 | tf_op jit(solution)/shard_map/ppermute | solution.py:34
  305.2 28.2 %collective-permute-start.107 = (bf16[256,1152]{1,0:T(8,128)(2,1)S(1)}, bf16[256,1152]{1,0:T(8,128)(2,1)S(1)}, u32[]{:S(2)}, u32[]{:S(2)}) collective-permute-start(bf16[256,1152]{1,0:T(8,128)(2,1)S(1)} %relay_f1.1), channel_id=1, source_target_pairs={{0,16},{8,24},{16,0},{24,8},{1,17},{9,25},{17,1},{25,9},{2,18},{10... | collective-permute-start | bytes 1769480 | tf_op jit(solution)/shard_map/ppermute | solution.py:34
  316.1 20.8 %collective-permute-start.81 = (bf16[128,1024]{1,0:T(8,128)(2,1)S(1)}, bf16[128,1024]{1,0:T(8,128)(2,1)S(1)}, u32[]{:S(2)}, u32[]{:S(2)}) collective-permute-start(bf16[128,1024]{1,0:T(8,128)(2,1)S(1)} %get-tuple-element.219), channel_id=1, source_target_pairs={{0,2},{2,0},{4,6},{6,4},{1,3},{3,1},{5,7},{7,5},{8,10},{10,8},{12,... | collective-permute-start | bytes 786440 | tf_op jit(solution)/shard_map/ppermute | solution.py:25
  317.2 19.7 %collective-permute-start.82 = (bf16[128,1024]{1,0:T(8,128)(2,1)S(1)}, bf16[128,1024]{1,0:T(8,128)(2,1)S(1)}, u32[]{:S(2)}, u32[]{:S(2)}) collective-permute-start(bf16[128,1024]{1,0:T(8,128)(2,1)S(1)} %get-tuple-element.220), channel_id=1, source_target_pairs={{0,4},{2,6},{4,0},{6,2},{1,5},{3,7},{5,1},{7,3},{8,12},{10,14},{12... | collective-permute-start | bytes 786440 | tf_op jit(solution)/shard_map/ppermute | solution.py:25
  318.4 18.5 %collective-permute-start.83 = (bf16[128,1024]{1,0:T(8,128)(2,1)S(1)}, bf16[128,1024]{1,0:T(8,128)(2,1)S(1)}, u32[]{:S(2)}, u32[]{:S(2)}) collective-permute-start(bf16[128,1024]{1,0:T(8,128)(2,1)S(1)} %get-tuple-element.221), channel_id=1, source_target_pairs={{0,6},{2,4},{4,2},{6,0},{1,7},{3,5},{5,3},{7,1},{8,14},{10,12},{12... | collective-permute-start | bytes 786440 | tf_op jit(solution)/shard_map/ppermute | solution.py:25
  389.1 24.8 %collective-permute-start.139 = (bf16[256,1152]{1,0:T(8,128)(2,1)S(1)}, bf16[256,1152]{1,0:T(8,128)(2,1)S(1)}, u32[]{:S(2)}, u32[]{:S(2)}) collective-permute-start(bf16[256,1152]{1,0:T(8,128)(2,1)S(1)} %get-tuple-element.278.refs_11_), channel_id=1, source_target_pairs={{0,8},{8,0},{16,24},{24,16},{1,9},{9,1},{17,25},{25,17},{2,10},{10... | collective-permute-start | bytes 1769480 | tf_op jit(solution)/shard_map/ppermute | solution.py:34
  413.8 31.5 %collective-permute-start.138 = (bf16[256,1152]{1,0:T(8,128)(2,1)S(1)}, bf16[256,1152]{1,0:T(8,128)(2,1)S(1)}, u32[]{:S(2)}, u32[]{:S(2)}) collective-permute-start(bf16[256,1152]{1,0:T(8,128)(2,1)S(1)} %get-tuple-element.276.refs_9_), channel_id=1, source_target_pairs={{0,8},{8,0},{16,24},{24,16},{1,9},{9,1},{17,25},{25,17},{2,10},{10... | collective-permute-start | bytes 1769480 | tf_op jit(solution)/shard_map/ppermute | solution.py:34
  418.4 29.6 %collective-permute-start.140 = (bf16[256,1152]{1,0:T(8,128)(2,1)S(1)}, bf16[256,1152]{1,0:T(8,128)(2,1)S(1)}, u32[]{:S(2)}, u32[]{:S(2)}) collective-permute-start(bf16[256,1152]{1,0:T(8,128)(2,1)S(1)} %relay_f0.1), channel_id=1, source_target_pairs={{0,16},{8,24},{16,0},{24,8},{1,17},{9,25},{17,1},{25,9},{2,18},{10... | collective-permute-start | bytes 1769480 | tf_op jit(solution)/shard_map/ppermute | solution.py:34
  458.1 21.3 %collective-permute-start.149 = (bf16[256,512]{1,0:T(8,128)(2,1)S(1)}, bf16[256,512]{1,0:T(8,128)(2,1)S(1)}, u32[]{:S(2)}, u32[]{:S(2)}) collective-permute-start(bf16[256,512]{1,0:T(8,128)(2,1)S(1)} %get-tuple-element.297.refs_5_), channel_id=1, source_target_pairs={{0,16},{8,24},{16,0},{24,8},{1,17},{9,25},{17,1},{25,9},{2,18},{10... | collective-permute-start | bytes 786440 | tf_op jit(solution)/shard_map/ppermute | solution.py:34
  458.1 21.3 %collective-permute-start.150 = (bf16[256,512]{1,0:T(8,128)(2,1)S(1)}, bf16[256,512]{1,0:T(8,128)(2,1)S(1)}, u32[]{:S(2)}, u32[]{:S(2)}) collective-permute-start(bf16[256,512]{1,0:T(8,128)(2,1)S(1)} %get-tuple-element.298.refs_6_), channel_id=1, source_target_pairs={{0,24},{8,16},{16,8},{24,0},{1,25},{9,17},{17,9},{25,1},{2,26},{10... | collective-permute-start | bytes 786440 | tf_op jit(solution)/shard_map/ppermute | solution.py:34
  (165 other events, 1462.3 us)
